TPU v7x, 32 devices: a whole 2x2x4 slice. The times are simulated.
32 devices in a mesh: dp: 2 (over x), seq: 4 (over z), mp: 4 (over y, core).
Axes of the slice: x: 2, y: 2, z: 4, core: 2. Of those that a mesh axis runs over, the one named last changes fastest.
Arguments:
- inputs: bfloat16 [2, 8192, 768], P('dp', 'seq'), may hold values from -6 to 6
- selection: int32 [2, 64, 4], P('dp', 'seq'), may hold values from 0 to 63, as said below
- gain1: float32 [768], replicated, may hold values from 0.5 to 1.5
- shift1: float32 [768], replicated, may hold values from -3 to 3
- w_qkv: bfloat16 [768, 3, 768], P(None, None, 'mp'), may hold values from -0.21875 to 0.21875
- b_qv: float32 [2, 768], P(None, 'mp'), may hold values from -3 to 3
- w_score: bfloat16 [768, 12], P(None, 'mp'), may hold values from -0.3125 to 0.3125
- b_score: float32 [12], P('mp'), may hold values from -3 to 3
- w_out: bfloat16 [768, 768], P('mp'), may hold values from -2 to 2
- b_out: float32 [768], replicated, may hold values from -3 to 3
- gain2: float32 [768], replicated, may hold values from 0.5 to 1.5
- shift2: float32 [768], replicated, may hold values from -3 to 3
- w_up: bfloat16 [768, 3072], P(None, 'mp'), may hold values from -0.21875 to 0.21875
- b_up: float32 [3072], P('mp'), may hold values from -3 to 3
- w_down: bfloat16 [3072, 768], P('mp'), may hold values from -0.109375 to 0.109375
- b_down: float32 [768], replicated, may hold values from -3 to 3
- cotangent: bfloat16 [2, 8192, 768], P('dp', 'seq'), may hold values from -6 to 6
Outputs:
- output: bfloat16 [2, 8192, 768], P('dp', 'seq')
- input_grad: bfloat16 [2, 8192, 768], P('dp', 'seq')
- gain1_grad: float32 [768], replicated
- shift1_grad: float32 [768], replicated
- qkv_grad: float32 [768, 3, 768], P(None, None, 'mp')
- qv_bias_grad: float32 [2, 768], P(None, 'mp')
- score_grad: float32 [768, 12], P(None, 'mp')
- score_bias_grad: float32 [12], P('mp')
- out_grad: float32 [768, 768], P('mp')
- out_bias_grad: float32 [768], replicated
- gain2_grad: float32 [768], replicated
- shift2_grad: float32 [768], replicated
- up_grad: float32 [768, 3072], P(None, 'mp')
- up_bias_grad: float32 [3072], P('mp')
- down_grad: float32 [3072, 768], P('mp')
- down_bias_grad: float32 [768], replicated
Inputs may be any that keep to these rules, and one draw needn't show every extreme that they name: selection[s, b, t] names a block of 128 keys of sequence s at or before query block b; selection[s, b, 0] = b.
All inputs are finite; a program needn't handle non-finite values.
Results may differ from a plain program's by a relative error of at most 0.017.
Values may be sent and summed in bfloat16 or wider, within the bound.
No kernel may reach another device: no remote copies, remote signals or barrier semaphores. Data moves between devices by JAX's collectives and lax.ppermute only.
A program may use at most 384 MiB of HBM per device.

v0:
```python
import jax
import jax.numpy as jnp
from jax import lax
from jax.sharding import PartitionSpec as P

HD = 64
KB = 128
WINDOW = 64


EPSILON = 1e-05
NEGATIVE = -1e30
HIGHEST = lax.Precision.HIGHEST


def layer_norm(value, gain, shift):
    center = jnp.mean(value, axis=-1, keepdims=True)
    centered = value - center
    spread = jnp.mean(centered * centered, axis=-1, keepdims=True)
    return centered * lax.rsqrt(spread + EPSILON) * gain + shift


def gelu_tanh(value):
    return jax.nn.gelu(value, approximate=True)


def rows_inner(left, right):
    return lax.dot_general(
        left, right, (((0,), (0,)), ((), ())), preferred_element_type=jnp.float32
    )


def cols_inner(left, right):
    return lax.dot_general(
        left, right, (((1,), (1,)), ((), ())), preferred_element_type=jnp.float32
    )


def block_masks(block_ids, picked_raw):
    offsets = jnp.arange(KB, dtype=jnp.int32)
    query_pos = block_ids[:, None] * KB + offsets
    key_pos = jnp.maximum(picked_raw, 0)[:, :, None] * KB + offsets
    slot_ids = jnp.arange(picked_raw.shape[1], dtype=jnp.int32)[None, None, :, None]
    query_at = query_pos[:, :, None, None]
    key_at = key_pos[:, None]
    window_mask = (
        (key_at <= query_at)
        & (key_at > query_at - WINDOW)
        & (slot_ids < 2)
        & (picked_raw >= 0)[:, None, :, None]
    )
    chosen_mask = (key_at <= query_at - WINDOW) & (slot_ids >= 2)
    return (window_mask, chosen_mask)


def block_scores(query_blocks, key_cand, mark_cand, window_mask, chosen_mask):
    logits = jnp.einsum(
        "gihd,gcjhd->ghicj", query_blocks, key_cand, preferred_element_type=jnp.float32
    ) * HD ** (-0.5)
    mark_term = mark_cand.astype(jnp.float32).transpose(0, 3, 1, 2)[:, :, None]
    return jnp.where(
        window_mask[:, None], logits, jnp.where(chosen_mask[:, None], logits + mark_term, NEGATIVE)
    )


def body(
    inputs,
    selection,
    gain1,
    shift1,
    w_qkv,
    b_qv,
    w_score,
    b_score,
    w_out,
    b_out,
    gain2,
    shift2,
    w_up,
    b_up,
    w_down,
    b_down,
    cotangent,
):
    seq_rank = lax.axis_index("seq")
    tokens = inputs[0].astype(jnp.float32)
    row_count = tokens.shape[0]
    local_blocks = row_count // KB
    local_width = w_qkv.shape[2]
    local_heads = local_width // HD
    scale = HD ** (-0.5)
    normed1, pull_norm1 = jax.vjp(layer_norm, tokens, gain1, shift1)
    first_in = normed1.astype(jnp.bfloat16)
    projected = jnp.einsum("td,dsk->tsk", first_in, w_qkv, preferred_element_type=jnp.float32)
    query_rows = (projected[:, 0] + b_qv[0]).astype(jnp.bfloat16)
    key_rows = projected[:, 1].astype(jnp.bfloat16)
    value_rows = (projected[:, 2] + b_qv[1]).astype(jnp.bfloat16)
    rating = jnp.dot(first_in, w_score, preferred_element_type=jnp.float32) + b_score
    marks = jax.nn.log_sigmoid(rating).astype(jnp.bfloat16)
    all_keys, all_values, all_marks = (
        lax.all_gather(key_rows, "seq", axis=0, tiled=True),
        lax.all_gather(value_rows, "seq", axis=0, tiled=True),
        lax.all_gather(marks, "seq", axis=0, tiled=True),
    )
    total_blocks = all_keys.shape[0] // KB
    key_blocks = all_keys.reshape(total_blocks, KB, local_heads, HD)
    value_blocks = all_values.reshape(total_blocks, KB, local_heads, HD)
    mark_blocks = all_marks.reshape(total_blocks, KB, local_heads)
    block_ids = seq_rank * local_blocks + jnp.arange(local_blocks, dtype=jnp.int32)
    picked_raw = jnp.concatenate([block_ids[:, None] - 1, block_ids[:, None], selection[0]], axis=1)
    picked = jnp.maximum(picked_raw, 0)
    key_cand = jnp.take(key_blocks, picked, axis=0)
    value_cand = jnp.take(value_blocks, picked, axis=0)
    mark_cand = jnp.take(mark_blocks, picked, axis=0)
    window_mask, chosen_mask = block_masks(block_ids, picked_raw)
    query_blocks = query_rows.reshape(local_blocks, KB, local_heads, HD)
    scores = block_scores(query_blocks, key_cand, mark_cand, window_mask, chosen_mask)
    highest = jnp.max(scores, axis=(3, 4), keepdims=True)
    exponent = jnp.exp(scores - highest)
    summed = jnp.sum(exponent, axis=(3, 4), keepdims=True)
    weights = exponent / summed
    log_norm = highest + jnp.log(summed)
    attended = jnp.einsum(
        "ghicj,gcjhd->gihd",
        weights.astype(jnp.bfloat16),
        value_cand,
        preferred_element_type=jnp.float32,
    )
    mixed = attended.reshape(row_count, local_width).astype(jnp.bfloat16)
    branch = lax.psum(jnp.dot(mixed, w_out, preferred_element_type=jnp.float32), "mp")
    hidden = tokens + branch + b_out
    normed2, pull_norm2 = jax.vjp(layer_norm, hidden, gain2, shift2)
    second_in = normed2.astype(jnp.bfloat16)
    pre = jnp.dot(second_in, w_up, preferred_element_type=jnp.float32) + b_up
    activated, pull_gelu = jax.vjp(gelu_tanh, pre)
    act_low = activated.astype(jnp.bfloat16)
    feed = lax.psum(
        jnp.dot(act_low, w_down, preferred_element_type=jnp.float32).astype(jnp.bfloat16), "mp"
    ).astype(jnp.float32)
    output = (hidden + feed + b_down).astype(jnp.bfloat16)
    upstream = cotangent[0]
    upstream_f = upstream.astype(jnp.float32)
    down_grad = rows_inner(act_low, upstream)
    down_bias_grad = jnp.sum(upstream_f, axis=0)
    act_grad = cols_inner(upstream, w_down)
    pre_grad = pull_gelu(act_grad)[0].astype(jnp.bfloat16)
    up_grad = rows_inner(second_in, pre_grad)
    up_bias_grad = jnp.sum(pre_grad.astype(jnp.float32), axis=0)
    second_grad = lax.psum(cols_inner(pre_grad, w_up), "mp")
    hidden_back, gain2_grad, shift2_grad = pull_norm2(second_grad)
    hidden_grad = upstream_f + hidden_back
    out_bias_grad = jnp.sum(hidden_grad, axis=0)
    branch_grad = hidden_grad.astype(jnp.bfloat16)
    out_grad = rows_inner(mixed, branch_grad)
    mixed_grad = cols_inner(branch_grad, w_out).astype(jnp.bfloat16)
    grad_blocks = mixed_grad.reshape(local_blocks, KB, local_heads, HD)
    again = block_scores(query_blocks, key_cand, mark_cand, window_mask, chosen_mask)
    prob_again = jnp.exp(again - log_norm)
    grad_prob = jnp.einsum(
        "gihd,gcjhd->ghicj", grad_blocks, value_cand, preferred_element_type=jnp.float32
    )
    delta = jnp.sum(prob_again * grad_prob, axis=(3, 4), keepdims=True)
    score_full = prob_again * (grad_prob - delta)
    score_low = score_full.astype(jnp.bfloat16)
    query_grad = (
        (
            jnp.einsum("ghicj,gcjhd->gihd", score_low, key_cand, preferred_element_type=jnp.float32)
            * scale
        )
        .reshape(row_count, local_width)
        .astype(jnp.bfloat16)
    )
    prob_low = prob_again.astype(jnp.bfloat16)
    key_part = (
        jnp.einsum("ghicj,gihd->gcjhd", score_low, query_blocks, preferred_element_type=jnp.float32)
        * scale
    )
    value_part = jnp.einsum(
        "ghicj,gihd->gcjhd", prob_low, grad_blocks, preferred_element_type=jnp.float32
    )
    mark_part = jnp.sum(jnp.where(chosen_mask[:, None], score_full, 0.0), axis=2).transpose(
        0, 2, 3, 1
    )
    key_spread = (
        jnp.zeros((total_blocks, KB, local_heads, HD), jnp.float32).at[picked].add(key_part)
    )
    value_spread = (
        jnp.zeros((total_blocks, KB, local_heads, HD), jnp.float32).at[picked].add(value_part)
    )
    mark_spread = jnp.zeros((total_blocks, KB, local_heads), jnp.float32).at[picked].add(mark_part)
    key_total, value_total, mark_total = (
        lax.psum_scatter(
            key_spread.reshape(total_blocks * KB, local_width),
            "seq",
            scatter_dimension=0,
            tiled=True,
        ),
        lax.psum_scatter(
            value_spread.reshape(total_blocks * KB, local_width),
            "seq",
            scatter_dimension=0,
            tiled=True,
        ),
        lax.psum_scatter(
            mark_spread.reshape(total_blocks * KB, local_heads),
            "seq",
            scatter_dimension=0,
            tiled=True,
        ),
    )
    key_grad = key_total.astype(jnp.bfloat16)
    value_grad = value_total.astype(jnp.bfloat16)
    rating_grad = mark_total * jax.nn.sigmoid(-rating)
    score_grad = lax.dot_general(
        first_in.astype(jnp.float32),
        rating_grad,
        (((0,), (0,)), ((), ())),
        precision=HIGHEST,
        preferred_element_type=jnp.float32,
    )
    score_bias_grad = jnp.sum(rating_grad, axis=0)
    stacked = jnp.stack([query_grad, key_grad, value_grad], axis=1)
    qkv_grad = jnp.einsum("td,tsk->dsk", first_in, stacked, preferred_element_type=jnp.float32)
    qv_bias_grad = jnp.stack(
        [
            jnp.sum(query_grad.astype(jnp.float32), axis=0),
            jnp.sum(value_grad.astype(jnp.float32), axis=0),
        ],
        axis=0,
    )
    first_part = jnp.einsum("tsk,dsk->td", stacked, w_qkv, preferred_element_type=jnp.float32)
    first_part = first_part + jnp.dot(rating_grad, w_score.astype(jnp.float32).T, precision=HIGHEST)
    first_grad = lax.psum(first_part.astype(jnp.bfloat16), "mp").astype(jnp.float32)
    token_back, gain1_grad, shift1_grad = pull_norm1(first_grad)
    input_grad = (hidden_grad + token_back).astype(jnp.bfloat16)
    summed_grads = lax.psum(
        (
            gain1_grad,
            shift1_grad,
            qkv_grad,
            qv_bias_grad,
            score_grad,
            score_bias_grad,
            out_grad,
            out_bias_grad,
            gain2_grad,
            shift2_grad,
            up_grad,
            up_bias_grad,
            down_grad,
            down_bias_grad,
        ),
        ("dp", "seq"),
    )
    return (
        output[None],
        input_grad[None],
        summed_grads[0],
        summed_grads[1],
        summed_grads[2],
        summed_grads[3],
        summed_grads[4],
        summed_grads[5],
        summed_grads[6],
        summed_grads[7],
        summed_grads[8],
        summed_grads[9],
        summed_grads[10],
        summed_grads[11],
        summed_grads[12],
        summed_grads[13],
    )


def solution(mesh):
    return jax.shard_map(
        body,
        mesh=mesh,
        in_specs=(
            P("dp", "seq", None),
            P("dp", "seq", None),
            P(),
            P(),
            P(None, None, "mp"),
            P(None, "mp"),
            P(None, "mp"),
            P("mp"),
            P("mp", None),
            P(),
            P(),
            P(),
            P(None, "mp"),
            P("mp"),
            P("mp", None),
            P(),
            P("dp", "seq", None),
        ),
        out_specs=(
            P("dp", "seq", None),
            P("dp", "seq", None),
            P(),
            P(),
            P(None, None, "mp"),
            P(None, "mp"),
            P(None, "mp"),
            P("mp"),
            P("mp", None),
            P(),
            P(),
            P(),
            P(None, "mp"),
            P("mp"),
            P("mp", None),
            P(),
        ),
        check_vma=False,
    )
```

profile of v0, /device:TPU:0, one launch (start us, length us, event | category | flops | bytes accessed | tf_op | source)
XLA Modules:
  0.0 1239.9 jit_solution(6036443825273681579)
XLA Ops:
  30.9 15.6 %all_gather.11 = bf16[8192,3]{0,1:T(4,128)(2,1)S(1)} all-gather(bf16[2048,3]{0,1:T(4,128)(2,1)S(1)} %get-tuple-element.65), channel_id=1, replica_groups=mesh['dp'=2,'seq'=4,'mp'=4] {'seq'}, dimensions={0}, use_global_device_ids=true | all-gather | bytes 61440 | tf_op jit(solution)/shard_map/all_gather | solution.py:103
  53.5 35.0 %all-gather.4.cloned.1.call-done = bf16[8192,192]{0,1:T(8,128)(2,1)} async-done(((bf16[2048,192]{0,1:T(8,128)(2,1)}), bf16[8192,192]{0,1:T(8,128)(2,1)}) %all-gather.4.cloned.1.call-update) | async-done | bytes 3145744 | tf_op jit(solution)/shard_map/all_gather | solution.py:102
  95.0 57.8 %all-gather.6.cloned.1.call-done = bf16[8192,1,192]{0,2,1:T(8,128)(2,1)} async-done(((bf16[2048,1,192]{0,2,1:T(8,128)(2,1)}), bf16[8192,1,192]{0,2,1:T(8,128)(2,1)}) %all-gather.6.cloned.1.call-update) | async-done | bytes 3145744 | tf_op jit(solution)/shard_map/all_gather | solution.py:101
  169.9 8.2 broadcast_select_fusion.1
  178.1 17.1 %fusion.88 = (f32[16,3,128]{2,1,0:T(4,128)S(1)}, f32[16,3,128,6,128]{2,4,3,1,0:T(8,128)}) fusion(pred[16,128,6,128]{1,3,2,0:T(8,128)(4,1)S(1)} %get-tuple-element.54, bf16[16,6,128,3,64]{2,4,3,1,0:T(8,128)(2,1)} %get-tuple-element.60, f32[16,128,3,64]{1,0,3,2:T(8,128)} %bitcast.233, f32[3,64]{1,0:T(4,128)S(1)} %add.316, ...), kind=kOutput, calls=%fused_computation.155 | convolution fusion | flops 628426752 | bytes 28410720 | tf_op jit(solution)/shard_map/gihd,gcjhd->ghicj/dot_general | solution.py:57
  195.2 10.6 fusion
  205.8 11.9 fusion.61
  222.9 118.4 %all-reduce.8.cloned.1.call-done = f32[2048,768]{1,0:T(8,128)} async-done(((f32[2048,768]{1,0:T(8,128)}), f32[2048,768]{1,0:T(8,128)}) %all-reduce.8.cloned.1.call-update) | async-done | bytes 6291472 | tf_op jit(solution)/shard_map/psum | solution.py:130
  353.1 7.0 convert_reduce_fusion.3
  366.9 119.2 %all-reduce.10.cloned.1.call-done = f32[2048,768]{1,0:T(8,128)} async-done(((f32[2048,768]{1,0:T(8,128)}), f32[2048,768]{1,0:T(8,128)}) %all-reduce.10.cloned.1.call-update) | async-done | bytes 6291472 | tf_op jit(solution)/shard_map/psum | solution.py:149
  486.2 6.4 multiply_reduce_fusion.1
  501.3 13.8 %multiply_reduce_fusion = (f32[16,3,128]{2,1,0:T(4,128)S(1)}, f32[16,3,128,6,128]{2,4,3,1,0:T(8,128)}) fusion(f32[16,3,128,6,128]{2,4,3,1,0:T(8,128)} %get-tuple-element.68, f32[16,3,128]{2,1,0:T(4,128)S(1)} %copy-done.22, bf16[16,6,128,3,64]{2,4,3,1,0:T(8,128)(2,1)} %get-tuple-element.59, bf16[16,128,3,64,1]{1,0,3,2,4:T(8,128)(2,1)S(1)} %bitcast.231), kind=kOutput, calls=%fused_computation.8 | convolution fusion | flops 618129408 | bytes 43302912 | tf_op jit(solution)/shard_map/gihd,gcjhd->ghicj/dot_general | solution.py:159
  515.2 17.3 %fusion.28 = (bf16[16,3,128,6,128]{2,4,3,1,0:T(8,128)(2,1)}, f32[16,3,6,128]{3,2,1,0:T(8,128)S(1)}) fusion(f32[16,3,128,6,128]{2,4,3,1,0:T(8,128)} %get-tuple-element.70, f32[16,3,128]{2,1,0:T(4,128)S(1)} %get-tuple-element.69, f32[16,3,128,6,128]{2,4,3,1,0:T(8,128)} %get-tuple-element.68, f32[16,3,128]{2,1,0:T(4,128)S(1)} %copy-done.22, ...), kind=kLoop, calls=%fused_computation.65 | loop fusion | flops 28274688 | bytes 48955392 | tf_op jit(solution)/shard_map/convert_element_type | solution.py:164
  533.9 11.0 scatter_fusion.2
  562.8 24.0 %scatter_fusion = f32[64,128,3,64]{1,3,2,0:T(8,128)} fusion(f32[64,128,3,64]{1,3,2,0:T(8,128)} %broadcast.318.clone.1, s32[96]{0:T(128)S(1)} %copy-done.20, f32[96,128,3,64]{1,3,2,0:T(8,128)} %bitcast.222), kind=kCustom, calls=%fused_computation.3 | custom fusion | flops 2359296 | bytes 28311936 | tf_op jit(solution)/shard_map/scatter-add | solution.py:185
  586.8 6.4 copy.151
  593.3 8.2 copy.237
  602.2 13.4 %fusion.36 = f32[16,6,128,3,64]{2,4,1,3,0:T(8,128)} fusion(f32[16,3,128,6,128]{2,4,3,1,0:T(8,128)} %get-tuple-element.68, f32[16,3,128]{2,1,0:T(4,128)S(1)} %copy-done.23, bf16[16,128,3,64,1]{1,0,3,2,4:T(8,128)(2,1)S(1)} %bitcast.232), kind=kOutput, calls=%fused_computation.75 | convolution fusion | flops 613416960 | bytes 29122560 | tf_op jit(solution)/shard_map/ghicj,gihd->gcjhd/dot_general | solution.py:178
  615.5 9.2 copy.154
  628.2 24.3 %scatter_fusion.1 = f32[64,128,3,64]{1,3,2,0:T(8,128)} fusion(f32[64,128,3,64]{1,3,2,0:T(8,128)} %broadcast.318.clone, s32[96]{0:T(128)S(1)} %copy-done.20, f32[96,128,3,64]{1,3,2,0:T(8,128)} %bitcast.221), kind=kCustom, calls=%fused_computation.4 | custom fusion | flops 2359296 | bytes 28311936 | tf_op jit(solution)/shard_map/scatter-add | solution.py:188
  652.5 6.5 copy.155
  659.0 8.1 copy.236
  667.8 8.5 convolution_convert_fusion
  676.3 7.8 convert_reduce_fusion.5
  692.1 47.0 %reduce-scatter.6.cloned.1.call-done = f32[2048,192]{0,1:T(8,128)} async-done(((f32[8192,192]{0,1:T(8,128)}), f32[2048,192]{0,1:T(8,128)}) %reduce-scatter.6.cloned.1.call-update) | async-done | bytes 1572880 | tf_op jit(solution)/shard_map/reduce_scatter | solution.py:192
  740.6 112.2 %reduce-scatter.8.cloned.1.call-done = f32[2048,192]{0,1:T(8,128)} async-done(((f32[8192,192]{0,1:T(8,128)}), f32[2048,192]{0,1:T(8,128)}) %reduce-scatter.8.cloned.1.call-update) | async-done | bytes 1572880 | tf_op jit(solution)/shard_map/reduce_scatter | solution.py:198
  861.0 7.1 fusion.94
  868.1 7.9 fusion.41
  885.7 95.3 %all-reduce.14.cloned.1.call-done = (bf16[2048,768]{1,0:T(8,128)(2,1)}, bf16[2048,768]{1,0:T(8,128)(2,1)}) async-done(((bf16[2048,768]{1,0:T(8,128)(2,1)}, bf16[2048,768]{1,0:T(8,128)(2,1)}), (bf16[2048,768]{1,0:T(8,128)(2,1)}, bf16[2048,768]{1,0:T(8,128)(2,1)})) %all-reduce.14.cloned.1.call-update) | async-done | bytes 6291472 | tf_op jit(solution)/shard_map/psum | solution.py:137
  989.6 6.3 convert_reduce_fusion.1
  995.9 42.3 %all-reduce = (f32[768]{0:T(1024)}, f32[768]{0:T(1024)}, f32[2,192]{1,0:T(2,128)}, f32[768,3]{0,1:T(4,128)}, f32[3]{0:T(128)}, /*index=5*/f32[768]{0:T(1024)}, f...) all-reduce(f32[768]{0:T(1024)S(1)} %get-tuple-element.19, ...), channel_id=1, replica_groups=mesh['dp'=2,'seq'=4,'mp'=4] {'dp','seq'}, use_global_device_ids=true, to_apply=%region_23.25 | all-reduce | flops 8067 | bytes 64536 | tf_op jit(solution)/shard_map/psum | solution.py:236
  1044.4 181.0 %all-reduce.12.cloned.1.call-done = (f32[768,3,192]{0,2,1:T(8,128)}, f32[192,768]{1,0:T(8,128)}, f32[768,768]{1,0:T(8,128)}, f32[768,768]{1,0:T(8,128)}) async-done(((f32[768,3,192]{0,2,1:T(8,128)}, f32[192,768]{1,0:T(8,128)}, f32[768,768]{1,0:T(8,128)}, f32[768,768]{1,0:T(8,128)}), (f32[768,3,192]{0,2,1:T(8,128)}, f32[192,768]{1,0:T(8,128)}, f32[768,768]{1,0:T(8,128)}, ...) | async-done | bytes 7077904 | tf_op jit(solution)/shard_map/psum | solution.py:236
  (225 shorter events, 160.2 us)
Async XLA Ops:
  7.2 345.8 %copy-start = (bf16[768,768]{1,0:T(8,128)(2,1)S(1)}, bf16[768,768]{1,0:T(8,128)(2,1)}, u32[]{:S(2)}) copy-start(bf16[768,768]{1,0:T(8,128)(2,1)} %param.33) | copy-start | bytes 3538948
  7.2 8.6 copy-start.50
  7.2 81.3 %all-gather.4.cloned.1.call-start = ((), (), s32[]{:S(2)}) async-start(), calls=%async_computation.3 | async-start | bytes 3932160 | tf_op jit(solution)/shard_map/all_gather | solution.py:102
  9.8 8.1 copy-start.24
  15.9 7.9 copy-start.38
  17.9 9.6 copy-start.36
  17.9 9.6 copy-start.48
  21.2 131.6 %all-gather.6.cloned.1.call-start = ((), (), s32[]{:S(2)}) async-start(), calls=%async_computation.8 | async-start | bytes 3932160 | tf_op jit(solution)/shard_map/all_gather | solution.py:101
  23.7 317.6 %all-reduce.8.cloned.1.call-start = ((), (), s32[]{:S(2)}) async-start(), calls=%async_computation.4 | async-start | bytes 12582912 | tf_op jit(solution)/shard_map/psum | solution.py:130
  24.5 22.1 %copy-start.19 = (s32[96]{0:T(128)}, s32[96]{0:T(128)S(1)}, u32[]{:S(2)}) copy-start(s32[96]{0:T(128)S(1)} %reshape.352) | copy-start | bytes 1156
  205.8 13.3 %copy-start.21 = (bf16[192,768]{1,0:T(8,128)(2,1)S(1)}, bf16[192,768]{1,0:T(8,128)(2,1)}, u32[]{:S(2)}) copy-start(bf16[192,768]{1,0:T(8,128)(2,1)} %param.27) | copy-start | bytes 884740
  219.1 122.2 %copy-start.45 = (f32[768]{0:T(1024)S(1)}, f32[768]{0:T(1024)}, u32[]{:S(2)}) copy-start(f32[768]{0:T(1024)} %param.28) | copy-start | bytes 9220
  222.8 263.3 %all-reduce.10.cloned.1.call-start = ((), (), s32[]{:S(2)}) async-start(), calls=%async_computation.5 | async-start | bytes 12582912 | tf_op jit(solution)/shard_map/psum | solution.py:149
  366.2 318.8 %reduce-scatter.10.cloned.1.call-start = ((), (), s32[]{:S(2)}) async-start(), calls=%async_computation.9 | async-start | bytes 5242880
  515.2 18.7 %copy-start.20 = (s32[96]{0:T(128)S(1)}, s32[96]{0:T(128)}, u32[]{:S(2)}) copy-start(s32[96]{0:T(128)} %copy-done.19) | copy-start | bytes 1156
  532.5 16.0 %copy-start.14 = (f32[24,8,16,128]{3,2,1,0:T(8,128)S(1)}, f32[24,8,16,128]{3,2,1,0:T(8,128)}, u32[]{:S(2)}) copy-start(f32[24,8,16,128]{3,2,1,0:T(8,128)} %copy.178) | copy-start | bytes 4718596
  548.4 190.6 %reduce-scatter.6.cloned.1.call-start = ((), (), s32[]{:S(2)}) async-start(), calls=%async_computation.6 | async-start | bytes 7864320 | tf_op jit(solution)/shard_map/reduce_scatter | solution.py:192
  601.4 251.3 %reduce-scatter.8.cloned.1.call-start = ((), (), s32[]{:S(2)}) async-start(), calls=%async_computation.7 | async-start | bytes 7864320 | tf_op jit(solution)/shard_map/reduce_scatter | solution.py:198
  667.1 313.8 %all-reduce.14.cloned.1.call-start = ((), (), s32[]{:S(2)}) async-start(), calls=%async_computation.11 | async-start | bytes 12582912 | tf_op jit(solution)/shard_map/psum | solution.py:137
  676.3 10.3 copy-start.28
  676.3 11.1 copy-start.37
  860.5 364.9 %all-reduce.12.cloned.1.call-start = ((), (), s32[]{:S(2)}) async-start(), calls=%async_computation.10 | async-start | bytes 14155776 | tf_op jit(solution)/shard_map/psum | solution.py:236
  861.0 15.0 %slice-start = ((s8[6291456]{0:T(1024)(128)(4,1)}), s8[4194304]{0:T(1024)(128)(4,1)S(1)}, s32[]{:S(2)}) async-start(s8[6291456]{0:T(1024)(128)(4,1)} %bitcast.215), calls=%async_computation.12 | async-start | bytes 8388608
  868.1 7.9 slice-start.1
  868.1 7.9 copy-start.13
  881.6 99.4 %copy-start.25 = (f32[2048]{0:T(1024)S(1)}, f32[2048]{0:T(1024)}, u32[]{:S(2)}) copy-start(f32[2048]{0:T(1024)} %copy-done.24) | copy-start | bytes 24580
  881.6 99.4 %copy-start.34 = (f32[768]{0:T(1024)S(1)}, f32[768]{0:T(1024)}, u32[]{:S(2)}) copy-start(f32[768]{0:T(1024)} %param.21) | copy-start | bytes 9220
  881.6 108.0 %slice-start.2 = ((s8[6291456]{0:T(1024)(128)(4,1)}), s8[2097152]{0:T(1024)(128)(4,1)S(1)}, s32[]{:S(2)}) async-start(s8[6291456]{0:T(1024)(128)(4,1)} %bitcast.217), calls=%async_computation.14 | async-start | bytes 4194304
  881.6 104.2 %copy-start.32 = (f32[2048]{0:T(1024)S(1)}, f32[2048]{0:T(1024)}, u32[]{:S(2)}) copy-start(f32[2048]{0:T(1024)} %copy-done.31) | copy-start | bytes 24580
  881.6 104.3 %copy-start.30 = (f32[2048]{0:T(1024)S(1)}, f32[2048]{0:T(1024)}, u32[]{:S(2)}) copy-start(f32[2048]{0:T(1024)} %copy-done.29) | copy-start | bytes 24580
  981.0 8.6 slice-start.3
  989.6 48.6 %copy-start.43 = (f32[768]{0:T(1024)S(1)}, f32[768]{0:T(1024)}, u32[]{:S(2)}) copy-start(f32[768]{0:T(1024)} %param.34) | copy-start | bytes 9220
  (37 other events, 138.3 us)
Sparse Core Ops, SparseCore 0:
  21.3 67.1 all-gather.3
  90.6 62.0 all-gather.5
  223.0 118.2 all-reduce.7
  366.4 119.7 all-reduce.9
  548.6 76.8 reduce-scatter.9
  627.8 111.2 reduce-scatter.5
  741.4 111.2 reduce-scatter.7
  860.6 120.2 all-reduce.13
  987.2 238.2 all-reduce.11
where the time goes:
time: 1250 us; the launch traced here: 1240 us
  waiting for transfers between devices  766 us (61%)
  other arithmetic  152 us (12%)
  matrix products  138 us (11%)
  local copies, waits for them, and re-layouts  110 us (9%)
  blocking collectives  57.9 us (5%)
  between operations  14.9 us (1%)
    psum x1, waiting for transfers between devices, body(): lax.psum((gain1_grad, shift1_grad, qkv_grad, qv_bias_grad, score_grad, sc...  181 us
    psum x1, waiting for transfers between devices, body(): second_grad = lax.psum(cols_inner(pre_grad, w_up), 'mp')  119 us
    psum x1, waiting for transfers between devices, body(): lax.psum(jnp.dot(mixed, w_out, preferred_element_type=jnp.float32), 'mp')  118 us
    reduce_scatter x1, waiting for transfers between devices, body(): lax.psum_scatter(value_spread.reshape(total_blocks * KB, local_width), 's...  112 us
    psum x1, waiting for transfers between devices, body(): lax.psum(jnp.dot(act_low, w_down, preferred_element_type=jnp.float32).ast...  95.3 us
    all_gather x1, waiting for transfers between devices, body(): lax.all_gather(key_rows, 'seq', axis=0, tiled=True)  57.8 us
    unnamed x133, local copies, waits for them, and re-layouts  51.5 us
    scatter-add x2, other arithmetic, body(): jnp.zeros((total_blocks, KB, local_heads, HD), jnp.float32).at[picked]  48.3 us
  transfers between devices with their start and end apart: 9, of which 8 were waited for; matrix products, arithmetic and copies ran while one was open for 17% of the time, Pallas kernels for 0%

commit v1 on v0

--- a/solution.py
+++ b/solution.py
@@ -1,6 +1,10 @@
+import functools
+
 import jax
 import jax.numpy as jnp
 from jax import lax
+from jax.experimental import pallas as pl
+from jax.experimental.pallas import tpu as pltpu
 from jax.sharding import PartitionSpec as P
 
 HD = 64
@@ -63,7 +67,7 @@
     )
 
 
-def body(
+def body_general(
     inputs,
     selection,
     gain1,
@@ -272,7 +276,612 @@
     )
 
 
+WIDE = 256
+BF = jnp.bfloat16
+F32 = jnp.float32
+
+
+def matmul(left, right):
+    return jnp.dot(left, right, preferred_element_type=F32)
+
+
+def near_far(left, right):
+    return lax.dot_general(left, right, (((1,), (1,)), ((), ())), preferred_element_type=F32)
+
+
+def project_kernel(first, *refs):
+    if first:
+        (x, gain, shift, wk, wkt, wv, wvt, wqt, bk, bv, bvt, bqt, fi, ka, va, kt, vt, qt) = refs
+    else:
+        (x, gain, shift, wk, wkt, wv, wvt, bk, bv, bvt) = refs[:10]
+        (fi, ka, va, kt, vt) = refs[15:]
+    value = x[...].astype(F32)
+    center = jnp.mean(value, axis=-1, keepdims=True)
+    centered = value - center
+    spread = jnp.mean(centered * centered, axis=-1, keepdims=True)
+    normed = (centered * lax.rsqrt(spread + EPSILON) * gain[...] + shift[...]).astype(BF)
+    fi[...] = normed
+    width = kt.shape[0]
+    half = WIDE // 2
+    heads = width // HD
+    base = width - half
+    keys = matmul(normed, wk[...]) + bk[...]
+    values = matmul(normed, wv[...]) + bv[...]
+    low, high = keys[:, :half], keys[:, half:]
+    lane = lax.broadcasted_iota(jnp.int32, high.shape, 1) - base
+    small = jnp.exp(-jnp.abs(high))
+    mark = jnp.minimum(high, 0.0) - jnp.log1p(small)
+    slope = jnp.where(high >= 0, small, 1.0) / (1.0 + small)
+    ones = jnp.where((lane >= heads) & (lane < heads + 3), 1.0, 0.0)
+    marked = (lane >= 0) & (lane < heads)
+    ka[:, :half] = low.astype(BF)
+    ka[:, half:] = jnp.where(lane < 0, high, jnp.where(marked, mark, ones)).astype(BF)
+    va[:, :half] = values[:, :half].astype(BF)
+    va[:, half:] = jnp.where(
+        lane < 0, values[:, half:], jnp.where(marked, slope, ones)
+    ).astype(BF)
+    kt[...] = near_far(wkt[...], normed).astype(BF)
+    vt[...] = (near_far(wvt[...], normed) + bvt[...]).astype(BF)
+    if first:
+        query = (near_far(wqt[...], normed) + bqt[...]).astype(BF)
+        qt[...] = (query.astype(F32) * HD ** (-0.5)).astype(BF)
+
+
+def whole(array):
+    shape = array.shape
+    return pl.BlockSpec(shape, lambda *_: (0,) * len(shape), pipeline_mode=pl.Buffered(1))
+
+
+def project(x, weights, buffers, place, total, block, queries=None):
+    (gain, shift, wk, wkt, wv, wvt, bk, bv, bvt) = weights
+    width = wkt.shape[0]
+    steps = x.shape[0] // block
+    rows = lambda cols: pl.BlockSpec((block, cols), lambda j: (place(j), 0))
+    flat = pl.BlockSpec((width, block), lambda j: (0, place(j)))
+    out_shape = [
+        jax.ShapeDtypeStruct((total, x.shape[1]), BF),
+        jax.ShapeDtypeStruct((total, WIDE), BF),
+        jax.ShapeDtypeStruct((total, WIDE), BF),
+        jax.ShapeDtypeStruct((width, total), BF),
+        jax.ShapeDtypeStruct((width, total), BF),
+    ]
+    out_specs = [rows(x.shape[1]), rows(WIDE), rows(WIDE), flat, flat]
+    if buffers is None:
+        wqt, bqt = queries
+        operands = [x, gain, shift, wk, wkt, wv, wvt, wqt, bk, bv, bvt, bqt]
+        extra, aliases = [], {}
+        out_shape.append(jax.ShapeDtypeStruct((width, x.shape[0]), BF))
+        out_specs.append(pl.BlockSpec((width, block), lambda j: (0, j)))
+    else:
+        operands = [x, gain, shift, wk, wkt, wv, wvt, bk, bv, bvt]
+        extra = list(buffers)
+        aliases = {len(operands) + i: i for i in range(len(extra))}
+    return pl.pallas_call(
+        functools.partial(project_kernel, buffers is None),
+        grid=(steps,),
+        in_specs=[pl.BlockSpec((block, x.shape[1]), lambda j: (j, 0))]
+        + [whole(a) for a in operands[1:]]
+        + [pl.BlockSpec(memory_space=pl.ANY) for _ in extra],
+        out_specs=out_specs,
+        out_shape=out_shape,
+        input_output_aliases=aliases,
+        compiler_params=pltpu.CompilerParams(vmem_limit_bytes=32 * 1024 * 1024),
+        cost_estimate=pl.CostEstimate(
+            flops=8 * x.shape[0] * x.shape[1] * WIDE,
+            bytes_accessed=x.shape[0] * 2 * (2 * x.shape[1] + 4 * WIDE),
+            transcendentals=0,
+        ),
+        name="project",
+    )(*operands, *extra)
+
+
+def head_diagonal(rows, tail):
+    width = rows.shape[0]
+    heads = width // HD
+    columns = []
+    for h in range(heads):
+        parts = []
+        if h > 0:
+            parts.append(jnp.zeros((h * HD, KB), BF))
+        parts.append(rows[h * HD : (h + 1) * HD])
+        if h < heads - 1:
+            parts.append(jnp.zeros(((heads - 1 - h) * HD, KB), BF))
+        columns.append(jnp.concatenate(parts, axis=0))
+    top = jnp.concatenate(columns, axis=1)
+    rest = jnp.zeros((WIDE - width - 16, heads * KB), BF)
+    return jnp.concatenate([top, tail.astype(BF), rest], axis=0)
+
+
+def tail_rows(heads, marked, term):
+    shape = (16, heads * KB)
+    row = lax.broadcasted_iota(jnp.int32, shape, 0)
+    column = lax.broadcasted_iota(jnp.int32, shape, 1) // KB
+    tail = jnp.where(row == column, 1.0, 0.0) if marked else jnp.zeros(shape, F32)
+    if term is not None:
+        for piece in range(3):
+            part = term.astype(BF).astype(F32)
+            tail = jnp.where(row == heads + piece, part, tail)
+            term = term - part
+    return tail
+
+
+def offsets_tile(heads):
+    shape = (KB, heads * KB)
+    key = lax.broadcasted_iota(jnp.int32, shape, 0)
+    query = lax.rem(lax.broadcasted_iota(jnp.int32, shape, 1), KB)
+    return key - query
+
+
+def masks_of(gap, bounds, step):
+    previous = gap > bounds[4 * step]
+    own = gap <= 0
+    return [previous, own] + [gap <= bounds[4 * step + 1 + t] for t in range(3)]
+
+
+def diagonal_of(full, heads):
+    return jnp.concatenate(
+        [full[h * HD : (h + 1) * HD, h * KB : (h + 1) * KB] for h in range(heads)], axis=0
+    )
+
+
+def attend_kernel(places, bounds, ka, vt, qt, mixed, norm):
+    step = pl.program_id(0)
+    width = qt.shape[0]
+    heads = width // HD
+    query = qt[...]
+    plain = head_diagonal(query, tail_rows(heads, False, None))
+    marked = head_diagonal(query, tail_rows(heads, True, None))
+    starts = [pl.multiple_of(places[5 * step + c] * KB, KB) for c in range(5)]
+    tiles = [ka[pl.ds(s, KB), :] for s in starts]
+    near = matmul(jnp.concatenate(tiles[:2], axis=0), plain)
+    far = matmul(jnp.concatenate(tiles[1:], axis=0), marked)
+    gap = offsets_tile(heads)
+    masks = masks_of(gap, bounds, step)
+    scores = [near[:KB], jnp.where(gap > -WINDOW, near[KB:], far[:KB])]
+    scores += [far[KB * (1 + t) : KB * (2 + t)] for t in range(3)]
+    scores = [jnp.where(m, s, NEGATIVE) for m, s in zip(masks, scores)]
+    top = functools.reduce(jnp.maximum, scores)
+    top = jnp.max(top, axis=0, keepdims=True)
+    weights = [jnp.exp(s - top) for s in scores]
+    total = jnp.sum(functools.reduce(jnp.add, weights), axis=0, keepdims=True)
+    stacked = jnp.concatenate([w.astype(BF) for w in weights], axis=0)
+    values = jnp.concatenate([vt[:, pl.ds(s, KB)] for s in starts], axis=1)
+    full = matmul(values, stacked) / total
+    mixed[...] = diagonal_of(full, heads).astype(BF)
+    norm[0] = top + jnp.log(total)
+
+
+def attend(places, bounds, ka, vt, qt, blocks):
+    width = qt.shape[0]
+    heads = width // HD
+    return pl.pallas_call(
+        attend_kernel,
+        grid_spec=pltpu.PrefetchScalarGridSpec(
+            num_scalar_prefetch=2,
+            grid=(blocks,),
+            in_specs=[whole(ka), whole(vt), pl.BlockSpec((width, KB), lambda i, *_: (0, i))],
+            out_specs=[
+                pl.BlockSpec((width, KB), lambda i, *_: (0, i)),
+                pl.BlockSpec((1, 1, heads * KB), lambda i, *_: (i, 0, 0)),
+            ],
+        ),
+        out_shape=[
+            jax.ShapeDtypeStruct((width, blocks * KB), BF),
+            jax.ShapeDtypeStruct((blocks, 1, heads * KB), F32),
+        ],
+        compiler_params=pltpu.CompilerParams(vmem_limit_bytes=40 * 1024 * 1024),
+        cost_estimate=pl.CostEstimate(
+            flops=4 * blocks * 5 * KB * heads * KB * WIDE,
+            bytes_accessed=ka.shape[0] * 4 * WIDE,
+            transcendentals=blocks * 5 * KB * heads * KB,
+        ),
+        name="attend",
+    )(places, bounds, ka, vt, qt)
+
+
+def attend_back_kernel(
+    blocks, places, bounds, ka, va, kt, qt, mixed, grad, norm, spread, query_grad, key_sum, value_sum
+):
+    step = pl.program_id(0)
+    width = qt.shape[0]
+    heads = width // HD
+
+    @pl.when(step == 0)
+    def _():
+        key_sum[...] = jnp.zeros_like(key_sum)
+        value_sum[...] = jnp.zeros_like(value_sum)
+
+    @pl.when(step < blocks)
+    def _():
+        query = qt[...]
+        upstream = grad[...]
+        product = upstream.astype(F32) * mixed[...].astype(F32)
+        delta = jnp.concatenate(
+            [
+                jnp.sum(product[h * HD : (h + 1) * HD], axis=0, keepdims=True)
+                for h in range(heads)
+            ],
+            axis=1,
+        )
+        plain = head_diagonal(query, tail_rows(heads, False, -norm[0]))
+        marked = head_diagonal(query, tail_rows(heads, True, -norm[0]))
+        back = head_diagonal(upstream, tail_rows(heads, False, -delta))
+        starts = [pl.multiple_of(places[5 * step + c] * KB, KB) for c in range(5)]
+        tiles = [ka[pl.ds(s, KB), :] for s in starts]
+        near = matmul(jnp.concatenate(tiles[:2], axis=0), plain)
+        far = matmul(jnp.concatenate(tiles[1:], axis=0), marked)
+        slopes = matmul(jnp.concatenate([va[pl.ds(s, KB), :] for s in starts], axis=0), back)
+        gap = offsets_tile(heads)
+        masks = masks_of(gap, bounds, step)
+        window = gap > -WINDOW
+        scores = [near[:KB], jnp.where(window, near[KB:], far[:KB])]
+        scores += [far[KB * (1 + t) : KB * (2 + t)] for t in range(3)]
+        probs = [jnp.where(m, jnp.exp(s), 0.0) for m, s in zip(masks, scores)]
+        signals = [p * slopes[c * KB : (c + 1) * KB] for c, p in enumerate(probs)]
+        own = signals[1]
+        near_signal = jnp.concatenate([signals[0], jnp.where(window, own, 0.0)], axis=0).astype(BF)
+        far_signal = jnp.concatenate(
+            [jnp.where(window, 0.0, own)] + signals[2:], axis=0
+        ).astype(BF)
+        signal = jnp.concatenate(signals, axis=0).astype(BF)
+        prob = jnp.concatenate(probs, axis=0).astype(BF)
+        near_keys = near_far(near_signal, plain)
+        far_keys = near_far(far_signal, marked)
+        value_parts = near_far(prob, back)
+        key_parts = [near_keys[:KB], near_keys[KB:] + far_keys[:KB]]
+        key_parts += [far_keys[KB * (1 + t) : KB * (2 + t)] for t in range(3)]
+        for c, s in enumerate(starts):
+            key_sum[pl.ds(s, KB), :] += key_parts[c]
+            value_sum[pl.ds(s, KB), :] += value_parts[c * KB : (c + 1) * KB]
+        keys = jnp.concatenate([kt[:, pl.ds(s, KB)] for s in starts], axis=1)
+        full = diagonal_of(matmul(keys, signal), heads) * HD ** (-0.5)
+        query_grad[...] = full.astype(BF)
+
+    @pl.when(step >= blocks)
+    def _():
+        rows = spread.shape[0]
+        at = pl.ds(pl.multiple_of((step - blocks) * rows, rows), rows)
+        lane = lax.broadcasted_iota(jnp.int32, (rows, WIDE), 1)
+        marks = (lane >= width) & (lane < width + heads)
+        keys = jnp.where(lane < width, key_sum[at, :], 0.0)
+        keys = jnp.where(marks, key_sum[at, :] * va[at, :].astype(F32), keys)
+        spread[:, :WIDE] = keys.astype(BF)
+        spread[:, WIDE:] = jnp.where(lane < width, value_sum[at, :], 0.0).astype(BF)
+
+
+def attend_back(places, bounds, ka, va, kt, qt, mixed, grad, norm, blocks):
+    width = qt.shape[0]
+    heads = width // HD
+    total = ka.shape[0]
+    rows = 4 * KB
+    lanes = pl.BlockSpec((width, KB), lambda i, *_: (0, jnp.minimum(i, blocks - 1)))
+    return pl.pallas_call(
+        functools.partial(attend_back_kernel, blocks),
+        grid_spec=pltpu.PrefetchScalarGridSpec(
+            num_scalar_prefetch=2,
+            grid=(blocks + total // rows,),
+            in_specs=[
+                whole(ka),
+                whole(va),
+                whole(kt),
+                lanes,
+                lanes,
+                lanes,
+                pl.BlockSpec(
+                    (1, 1, heads * KB), lambda i, *_: (jnp.minimum(i, blocks - 1), 0, 0)
+                ),
+            ],
+            out_specs=[
+                pl.BlockSpec((rows, 2 * WIDE), lambda i, *_: (jnp.maximum(i - blocks, 0), 0)),
+                lanes,
+            ],
+            scratch_shapes=[pltpu.VMEM((total, WIDE), F32), pltpu.VMEM((total, WIDE), F32)],
+        ),
+        out_shape=[
+            jax.ShapeDtypeStruct((total, 2 * WIDE), BF),
+            jax.ShapeDtypeStruct((width, blocks * KB), BF),
+        ],
+        compiler_params=pltpu.CompilerParams(vmem_limit_bytes=56 * 1024 * 1024),
+        cost_estimate=pl.CostEstimate(
+            flops=10 * blocks * 5 * KB * heads * KB * WIDE,
+            bytes_accessed=total * 10 * WIDE,
+            transcendentals=blocks * 5 * KB * heads * KB,
+        ),
+        name="attend_back",
+    )(places, bounds, ka, va, kt, qt, mixed, grad, norm)
+
+
+def swap(array, flip):
+    return lax.ppermute(array, "mp", [(i, i ^ flip) for i in range(4)])
+
+
+def upward(array, ranks):
+    return lax.ppermute(array, "seq", [(i, i + 1) for i in range(ranks - 1)])
+
+
+def downward(array, ranks):
+    return lax.ppermute(array, "seq", [(i + 1, i) for i in range(ranks - 1)])
+
+
+def spread_over_mp(part):
+    across = swap(part, 2)
+    return [part, swap(part, 1), across, swap(across, 1)]
+
+
+def quarters(array, me, axis=0):
+    size = array.shape[axis] // 4
+    return [lax.dynamic_slice_in_dim(array, (me ^ j) * size, size, axis) for j in range(4)]
+
+
+def ordered(parts, me):
+    size = parts[0].shape[0]
+    out = jnp.zeros((4 * size,) + parts[0].shape[1:], parts[0].dtype)
+    for j, part in enumerate(parts):
+        out = lax.dynamic_update_slice_in_dim(out, part, (me ^ j) * size, 0)
+    return out
+
+
+def normed_parts(value):
+    center = jnp.mean(value, axis=-1, keepdims=True)
+    centered = value - center
+    spread = jnp.mean(centered * centered, axis=-1, keepdims=True)
+    scale = lax.rsqrt(spread + EPSILON)
+    return centered * scale, scale
+
+
+def norm_back(grad, hat, scale, gain):
+    g = gain * grad
+    return scale * (
+        g
+        - jnp.mean(g, axis=-1, keepdims=True)
+        - hat * jnp.mean(g * hat, axis=-1, keepdims=True)
+    )
+
+
+def body_resident(
+    inputs,
+    selection,
+    gain1,
+    shift1,
+    w_qkv,
+    b_qv,
+    w_score,
+    b_score,
+    w_out,
+    b_out,
+    gain2,
+    shift2,
+    w_up,
+    b_up,
+    w_down,
+    b_down,
+    cotangent,
+):
+    ranks = lax.axis_size("seq")
+    me, rank = lax.axis_index("mp"), lax.axis_index("seq")
+    rows, model = inputs.shape[1:]
+    quarter = rows // 4
+    total = ranks * rows
+    blocks = rows // KB
+    per = blocks // 4
+    width = w_qkv.shape[2]
+    heads = width // HD
+
+    w_ups, w_downs, w_outs = spread_over_mp(w_up), spread_over_mp(w_down), spread_over_mp(w_out)
+    b_ups = spread_over_mp(b_up)
+
+    own = quarters(inputs[0], me)
+    block = quarter // 2
+    arriving = []
+    for h in range(2):
+        part = own[0][h * block : (h + 1) * block]
+        for k in range(1, ranks):
+            part = upward(part, ranks)
+            arriving.append((k, h, spread_over_mp(part)))
+
+    pad = lambda a, n: jnp.pad(a, ((0, 0), (0, n - a.shape[1])))
+    wq, wk, wv = w_qkv[:, 0], w_qkv[:, 1], w_qkv[:, 2]
+    wqt, wkt, wvt = wq.T, wk.T, wv.T
+    bk = jnp.pad(b_score[None], ((0, 0), (width, WIDE - width - heads)))
+    bv = pad(b_qv[1:2], WIDE)
+    weights = (
+        gain1[None],
+        shift1[None],
+        pad(jnp.concatenate([wk, w_score], axis=1), WIDE),
+        wkt,
+        pad(wv, WIDE),
+        wvt,
+        bk,
+        bv,
+        b_qv[1][:, None],
+    )
+    *buffers, qt = project(
+        jnp.concatenate(own, axis=0),
+        weights,
+        None,
+        lambda j: j,
+        total,
+        block,
+        (wqt, b_qv[0][:, None]),
+    )
+    for k, h, parts in sorted(arriving, key=lambda a: a[:2]):
+        buffers = project(
+            jnp.concatenate(parts, axis=0),
+            weights,
+            buffers,
+            lambda j, k=k, h=h: 8 * k + 2 * j + h,
+            total,
+            block,
+        )
+    first_in, ka, va, kt, vt = buffers
+
+    at = jnp.arange(blocks, dtype=jnp.int32)
+    natural = ((at // per) ^ me) * per + at % per
+    block_ids = rank * blocks + natural
+    chosen = jnp.take(selection[0], natural, axis=0)[:, 1:]
+    named = jnp.concatenate([block_ids[:, None] - 1, block_ids[:, None], chosen], axis=1)
+    named = jnp.maximum(named, 0)
+    inner = named % blocks
+    places = (rank - named // blocks) * blocks + ((inner // per) ^ me) * per + inner % per
+    bounds = jnp.concatenate(
+        [
+            jnp.where(block_ids[:, None] >= 1, KB - WINDOW, 2 * KB),
+            (block_ids[:, None] - chosen) * KB - WINDOW,
+        ],
+        axis=1,
+    )
+    places, bounds = places.reshape(-1), bounds.reshape(-1)
+
+    mixed, norm = attend(places, bounds, ka, vt, qt, blocks)
+
+    pieces = [mixed[:, j * quarter : (j + 1) * quarter] for j in range(4)]
+    gathered = [pieces[0]] + [swap(pieces[j], j) for j in (1, 2, 3)]
+    features = jnp.concatenate(gathered, axis=0)
+    w_out_all = jnp.concatenate(w_outs, axis=0)
+    tokens = own[0].astype(F32)
+    hidden = tokens + rows_inner(features, w_out_all) + b_out
+    hat2, scale2 = normed_parts(hidden)
+    second_in = (hat2 * gain2 + shift2).astype(BF)
+    upstream = lax.dynamic_slice_in_dim(cotangent[0], me * quarter, quarter, 0)
+    upstream_f = upstream.astype(F32)
+    feed = 0.0
+    second_grad = 0.0
+    up_grads, down_grads, up_biases = [], [], []
+    for j in range(4):
+        pre = matmul(second_in, w_ups[j]) + b_ups[j]
+        activated, pull_gelu = jax.vjp(gelu_tanh, pre)
+        act = activated.astype(BF)
+        feed = feed + matmul(act, w_downs[j])
+        down_grads.append(rows_inner(act, upstream))
+        pre_grad = pull_gelu(cols_inner(upstream, w_downs[j]))[0].astype(BF)
+        up_grads.append(rows_inner(second_in, pre_grad))
+        up_biases.append(jnp.sum(pre_grad.astype(F32), axis=0))
+        second_grad = second_grad + cols_inner(pre_grad, w_ups[j])
+    output = (hidden + feed + b_down).astype(BF)
+    output_parts = spread_over_mp(output)
+    hidden_grad = upstream_f + norm_back(second_grad, hat2, scale2, gain2)
+    branch_grad = hidden_grad.astype(BF)
+    mixed_grads = cols_inner(w_out_all, branch_grad).astype(BF)
+    sent = [mixed_grads[j * width : (j + 1) * width] for j in range(4)]
+    returned = jnp.concatenate([sent[0]] + [swap(sent[j], j) for j in (1, 2, 3)], axis=1)
+
+    out_grads = matmul(features, branch_grad)
+    sums = [
+        jnp.sum(second_grad * hat2, axis=0),
+        jnp.sum(second_grad, axis=0),
+        jnp.sum(hidden_grad, axis=0),
+        jnp.sum(upstream_f, axis=0),
+    ]
+    packs = []
+    for j in range(4):
+        lines = jnp.stack([up_biases[j]] + sums + [jnp.zeros_like(sums[0])] * 11, axis=0)
+        packs.append(
+            jnp.concatenate(
+                [
+                    up_grads[j].astype(BF),
+                    down_grads[j].astype(BF),
+                    out_grads[j * width : (j + 1) * width].astype(BF),
+                    lines.astype(BF),
+                ],
+                axis=0,
+            )
+        )
+    kept = [packs[0] + swap(packs[1], 1), packs[2] + swap(packs[3], 1)]
+    dense = lax.psum(kept[0] + swap(kept[1], 2), ("dp", "seq"))
+
+    spread, query_grad = attend_back(places, bounds, ka, va, kt, qt, mixed, returned, norm, blocks)
+
+    w_back = jnp.concatenate(
+        [wkt, w_score.T, jnp.zeros((WIDE - width - heads, model), BF), wvt]
+        + [jnp.zeros((WIDE - width, model), BF)],
+        axis=0,
+    )
+    carried = None
+    for k in range(ranks - 1, -1, -1):
+        part = matmul(spread[k * rows : (k + 1) * rows], w_back)
+        if k == 0:
+            part = part + rows_inner(query_grad, wqt)
+        part = part.astype(BF)
+        parts = [part[j * quarter : (j + 1) * quarter] for j in range(4)]
+        mine = parts[0] + swap(parts[1], 1) + swap(parts[2] + swap(parts[3], 1), 2)
+        carried = mine if carried is None else mine + downward(carried, ranks)
+    first_grad = carried.astype(F32)
+
+    key_value_grad = rows_inner(first_in, spread)
+    query_weight_grad = lax.dot_general(
+        first_in[:rows], query_grad, (((0,), (1,)), ((), ())), preferred_element_type=F32
+    )
+    spread_sum = jnp.sum(spread.astype(F32), axis=0)
+    query_sum = jnp.sum(query_grad.astype(F32), axis=1)
+    score_at = width + heads
+    qkv_pack = jnp.concatenate(
+        [
+            jnp.concatenate(
+                [
+                    query_weight_grad,
+                    key_value_grad[:, :score_at],
+                    key_value_grad[:, WIDE : WIDE + width],
+                ],
+                axis=1,
+            ),
+            jnp.concatenate(
+                [query_sum, spread_sum[:score_at], spread_sum[WIDE : WIDE + width]], axis=0
+            )[None],
+        ],
+        axis=0,
+    )
+    dense, qkv_pack = lax.optimization_barrier((dense, qkv_pack.astype(BF)))
+    qkv_sum = lax.psum(qkv_pack, ("dp", "seq")).astype(F32)
+
+    hat1, scale1 = normed_parts(tokens)
+    input_part = (hidden_grad + norm_back(first_grad, hat1, scale1, gain1)).astype(BF)
+    input_grad = ordered(spread_over_mp(input_part), me)
+    norm1 = lax.psum(
+        jnp.stack([jnp.sum(first_grad * hat1, axis=0), jnp.sum(first_grad, axis=0)], axis=0),
+        ("dp", "seq", "mp"),
+    )
+    dense = dense.astype(F32)
+    hidden_units = w_up.shape[1]
+    at_down = model + hidden_units
+    lines = dense[at_down + width :]
+    qkv_grad = jnp.stack(
+        [
+            qkv_sum[:model, :width],
+            qkv_sum[:model, width : 2 * width],
+            qkv_sum[:model, 2 * width + heads :],
+        ],
+        axis=1,
+    )
+    qv_bias_grad = jnp.stack([qkv_sum[model, :width], qkv_sum[model, 2 * width + heads :]], axis=0)
+    return (
+        ordered(output_parts, me)[None],
+        input_grad[None],
+        norm1[0],
+        norm1[1],
+        qkv_grad,
+        qv_bias_grad,
+        qkv_sum[:model, 2 * width : 2 * width + heads],
+        qkv_sum[model, 2 * width : 2 * width + heads],
+        dense[at_down : at_down + width],
+        lines[3],
+        lines[1],
+        lines[2],
+        dense[:model],
+        lines[0],
+        dense[model:at_down],
+        lines[4],
+    )
+
+
+RESIDENT_TOKENS = 8192
+
+
 def solution(mesh):
+    def body(*args):
+        tokens = args[0].shape[1] * mesh.shape["seq"]
+        resident = mesh.shape["mp"] == 4 and tokens <= RESIDENT_TOKENS
+        return (body_resident if resident else body_general)(*args)
+
     return jax.shard_map(
         body,
         mesh=mesh,

time: 1250 us -> 707 us (0.57)
  waiting for transfers between devices: 766 us -> 266 us
  other arithmetic: 152 us -> 48.6 us
  Pallas kernels: 0 us -> 78.8 us
  matrix products: 138 us -> 67.5 us
  starting transfers between devices: 0.99 us -> 50.1 us
  local copies, waits for them, and re-layouts: 110 us -> 129 us
  blocking collectives: 57.9 us -> 40.7 us
    psum x4 -> x2, waiting for transfers between devices: 514 us -> 110 us  [the longest x1 72.9 us: body_resident(): qkv_sum = lax.psum(qkv_pack, ('dp', 'seq')).astype(F32)]
    reduce_scatter x2 -> x0, waiting for transfers between devices: 159 us -> none  [the longest x1 112 us: body(): lax.psum_scatter(value_spread.reshape(total_blocks * KB, local_width), 's...]
    ppermute x0 -> x66, waiting for transfers between devices: none -> 156 us  [the longest x57 146 us: swap(): return lax.ppermute(array, 'mp', [(i, i ^ flip) for i in range(4)])]
    all_gather x2 -> x0, waiting for transfers between devices: 92.8 us -> none  [the longest x1 57.8 us: body(): lax.all_gather(key_rows, 'seq', axis=0, tiled=True)]
    pallas_call x0 -> x9, Pallas kernels: none -> 78.8 us  [the longest x7 32.7 us: project(): pl.pallas_call(functools.partial(project_kernel, buffers is None), grid=(...]
    dot_general x13 -> x14, matrix products: 103 us -> 25.2 us  [the longest x13 21.9 us: matmul(): return jnp.dot(left, right, preferred_element_type=F32)]
    scatter-add x3 -> x0, other arithmetic: 59.3 us -> none  [the longest x2 48.3 us: body(): jnp.zeros((total_blocks, KB, local_heads, HD), jnp.float32).at[picked]]
    concatenate x0 -> x6, local copies, waits for them, and re-layouts: none -> 58.6 us  [the longest x4 49.1 us: body_resident(): jnp.concatenate([up_grads[j].astype(BF), down_grads[j].astype(BF), out_gr...]
  transfers between devices with their start and end apart: 9 -> 68, of which waited for: 8 -> 16; matrix products, arithmetic and copies ran while one was open for 17% -> 29% of each run, Pallas kernels for 0% -> 11%
where the time goes in v1:
time: 707 us; the launch traced here: 696 us
  waiting for transfers between devices  266 us (38%)
  local copies, waits for them, and re-layouts  129 us (18%)
  Pallas kernels  78.8 us (11%)
  matrix products  67.5 us (10%)
  starting transfers between devices  50.1 us (7%)
  other arithmetic  48.6 us (7%)
  blocking collectives  40.7 us (6%)
  between operations  15.8 us (2%)
    ppermute x57, waiting for transfers between devices, swap(): return lax.ppermute(array, 'mp', [(i, i ^ flip) for i in range(4)])  146 us
    psum x1, waiting for transfers between devices, body_resident(): qkv_sum = lax.psum(qkv_pack, ('dp', 'seq')).astype(F32)  72.9 us
    concatenate x4, local copies, waits for them, and re-layouts, body_resident(): jnp.concatenate([up_grads[j].astype(BF), down_grads[j].astype(BF), out_gr...  49.1 us
    psum x1, blocking collectives, body_resident(): lax.psum(jnp.stack([jnp.sum(first_grad * hat1, axis=0), jnp.sum(first_gra...  40.7 us
    psum x1, waiting for transfers between devices, body_resident(): dense = lax.psum(kept[0] + swap(kept[1], 2), ('dp', 'seq'))  36.9 us
    pallas_call x7, Pallas kernels, project(): pl.pallas_call(functools.partial(project_kernel, buffers is None), grid=(...  32.7 us
    pallas_call x1, Pallas kernels, attend_back(): pl.pallas_call(functools.partial(attend_back_kernel, blocks), grid_spec=p...  32.1 us
    dot_general x11, matrix products, rows_inner(): lax.dot_general(left, right, (((0,), (0,)), ((), ())), preferred_element_...  30.8 us
  transfers between devices with their start and end apart: 68, of which 16 were waited for; matrix products, arithmetic and copies ran while one was open for 29% of the time, Pallas kernels for 11%

profile of v1, /device:TPU:0, one launch (start us, length us, event | category | flops | bytes accessed | tf_op | source)
XLA Modules:
  0.0 696.4 jit_solution(9320509876063197870)
XLA Ops:
  9.4 5.7 collective-permute-start.6
  37.0 8.2 %project.7 = (bf16[8192,768]{1,0:T(8,128)(2,1)}, bf16[8192,256]{1,0:T(8,128)(2,1)S(1)}, bf16[8192,256]{1,0:T(8,128)(2,1)S(1)}, bf16[192,8192]{1,0:T(8,128)(2,1)S...) custom-call(bf16[2048,768]{1,0:T(8,128)(2,1)S(1)} %copy-done.17, ...), custom_call_target="tpu_custom_call" | custom-call | flops 3221225472 | bytes 10485760 | tf_op jit(solution)/shard_map/project/pallas_call | solution.py:359
  58.6 5.5 collective-permute-done.22
  67.7 4.5 collective-permute-done.19
  80.7 9.4 %concatenate.83 = bf16[512,768]{1,0:T(8,128)(2,1)} concatenate(bf16[192,768]{1,0:T(8,128)(2,1)} %get-tuple-element.183.refs_4_, bf16[3,768]{1,0:T(4,128)(2,1)} %bitcast.135, bf16[61,768]{1,0:T(8,128)(2,1)} %broadcast_in_dim.91, bf16[192,768]{1,0:T(8,128)(2,1)} %get-tuple-element.184.refs_6_, bf16[64,768]{1,0:T(8,128)(2,1)} %broadcast_in_dim.92), dimensions={0} | concatenate | bytes 1572864 | tf_op jit(solution)/shard_map/concatenate | solution.py:794
  101.6 4.1 collective-permute-done.13
  106.2 5.7 collective-permute-done.2
  121.6 4.1 project.9
  130.6 4.1 project.10
  139.4 4.1 project.12
  143.6 4.1 project.13
  149.7 13.9 %attend.1 = (bf16[192,2048]{1,0:T(8,128)(2,1)S(1)}, f32[16,1,384]{2,1,0:T(1,128)S(1)}) custom-call(s32[80]{0:T(128)S(1)} %copy-done.22, s32[64]{0:T(128)S(1)} %copy-done.21, bf16[8192,256]{1,0:T(8,128)(2,1)S(1)} %get-tuple-element.88.ka, bf16[192,8192]{1,0:T(8,128)(2,1)S(1)} %get-tuple-element.89.vt, bf16[192,2048]{1,0:T(8,128)(2,1)S(1)} %copy-done.24), custom_call_target="tpu_custom_call" | custom-call | flops 4026531840 | bytes 8388608 | tf_op jit(solution)/shard_map/attend/pallas_call | solution.py:457
  166.6 5.1 collective-permute-done.25
  183.7 17.6 %collective-permute-done.34 = f32[768]{0:T(1024)S(1)} collective-permute-done((f32[768]{0:T(1024)S(1)}, f32[768]{0:T(1024)S(1)}, u32[]{:S(2)}, u32[]{:S(2)}) %collective-permute-start.34) | collective-permute-done | bytes 3104 | tf_op jit(solution)/shard_map/ppermute | solution.py:595
  201.8 24.3 %collective-permute-done.35 = bf16[768,768]{1,0:T(8,128)(2,1)S(1)} collective-permute-done((bf16[768,768]{1,0:T(8,128)(2,1)S(1)}, bf16[768,768]{1,0:T(8,128)(2,1)S(1)}, u32[]{:S(2)}, u32[]{:S(2)}) %collective-permute-start.35) | collective-permute-done | bytes 1179680 | tf_op jit(solution)/shard_map/ppermute | solution.py:595
  266.3 12.5 %concatenate.87 = bf16[1744,768]{1,0:T(8,128)(2,1)} concatenate(bf16[768,768]{1,0:T(8,128)(2,1)} %convolution_convert_fusion.4, bf16[768,768]{1,0:T(8,128)(2,1)S(1)} %convolution_convert_fusion.3, bf16[192,768]{1,0:T(8,128)(2,1)S(1)} %get-tuple-element.177, bf16[1,768]{1,0:T(2,128)(2,1)} %stack.82, bf16[1,768]{1,0:T(2,128)(2,1)} %reshape.210, bf16[1,768]{1,0:T(2,128)(2,1)} %reshape.211, ...), dimensions={0} | concatenate | bytes 5357568 | tf_op jit(solution)/shard_map/concatenate | solution.py:779
  281.8 32.1 %attend_back.1 = (bf16[8192,512]{1,0:T(8,128)(2,1)}, bf16[192,2048]{1,0:T(8,128)(2,1)}) custom-call(s32[80]{0:T(128)} %fusion.96.places, s32[64]{0:T(128)} %reshape.209.bounds, bf16[8192,256]{1,0:T(8,128)(2,1)} %copy-done.2, bf16[8192,256]{1,0:T(8,128)(2,1)} %copy-done.5, bf16[192,8192]{1,0:T(8,128)(2,1)} %copy-done.6, bf16[192,2048]{1,0:T(8,128)(2,1)} %copy-done.23, ...), custom_call_target="tpu_custom_call" | custom-call | flops 10066329600 | bytes 20971520 | tf_op jit(solution)/shard_map/attend_back/pallas_call | solution.py:558
  328.0 14.7 %collective-permute-done.56 = bf16[512,768]{1,0:T(8,128)(2,1)S(1)} collective-permute-done((bf16[512,768]{1,0:T(8,128)(2,1)S(1)}, bf16[512,768]{1,0:T(8,128)(2,1)S(1)}, u32[]{:S(2)}, u32[]{:S(2)}) %collective-permute-start.56) | collective-permute-done | bytes 786464 | tf_op jit(solution)/shard_map/ppermute | solution.py:595
  350.1 8.8 %collective-permute-done.53 = bf16[512,768]{1,0:T(8,128)(2,1)S(1)} collective-permute-done((bf16[512,768]{1,0:T(8,128)(2,1)S(1)}, bf16[512,768]{1,0:T(8,128)(2,1)S(1)}, u32[]{:S(2)}, u32[]{:S(2)}) %collective-permute-start.53) | collective-permute-done | bytes 786464 | tf_op jit(solution)/shard_map/ppermute | solution.py:595
  359.4 4.2 collective-permute-done.57
  370.8 14.2 %concatenate.85 = bf16[1744,768]{1,0:T(8,128)(2,1)} concatenate(bf16[768,768]{1,0:T(8,128)(2,1)} %convolution_convert_fusion.8, bf16[768,768]{1,0:T(8,128)(2,1)} %convolution_convert_fusion.7, bf16[192,768]{1,0:T(8,128)(2,1)S(1)} %get-tuple-element.176, bf16[1,768]{1,0:T(2,128)(2,1)S(1)} %copy-done.69, bf16[1,768]{1,0:T(2,128)(2,1)S(1)} %copy-done.55, ...), dimensions={0} | concatenate | bytes 5357568 | tf_op jit(solution)/shard_map/concatenate | solution.py:779
  385.0 11.2 %concatenate.86 = bf16[1744,768]{1,0:T(8,128)(2,1)S(1)} concatenate(bf16[768,768]{1,0:T(8,128)(2,1)} %convolution_convert_fusion.6, bf16[768,768]{1,0:T(8,128)(2,1)} %convolution_convert_fusion.5, bf16[192,768]{1,0:T(8,128)(2,1)} %get-tuple-element.178, bf16[1,768]{1,0:T(2,128)(2,1)S(1)} %copy-done.70, bf16[1,768]{1,0:T(2,128)(2,1)S(1)} %copy-done.55, ...), dimensions={0} | concatenate | bytes 5357568 | tf_op jit(solution)/shard_map/concatenate | solution.py:779
  404.2 11.2 %concatenate.84 = bf16[1744,768]{1,0:T(8,128)(2,1)S(1)} concatenate(bf16[768,768]{1,0:T(8,128)(2,1)} %convolution_convert_fusion.11, bf16[768,768]{1,0:T(8,128)(2,1)} %convolution_convert_fusion.10, bf16[192,768]{1,0:T(8,128)(2,1)} %get-tuple-element.179, bf16[1,768]{1,0:T(2,128)(2,1)S(1)} %copy-done.68, bf16[1,768]{1,0:T(2,128)(2,1)S(1)} %copy-done.55, ...), dimensions={0} | concatenate | bytes 5357568 | tf_op jit(solution)/shard_map/concatenate | solution.py:779
  422.5 13.6 %convolution_convert_fusion.12 = bf16[768,512]{0,1:T(8,128)(2,1)} fusion(bf16[8192,768]{1,0:T(8,128)(2,1)} %get-tuple-element.97, bf16[8192,512]{1,0:T(8,128)(2,1)} %get-tuple-element.95), kind=kOutput, calls=%fused_computation.102 | convolution fusion | flops 6442844160 | bytes 21757952 | tf_op jit(solution)/shard_map/dot_general | solution.py:32
  436.2 42.2 %collective-permute-done.65 = bf16[1744,768]{1,0:T(8,128)(2,1)} collective-permute-done((bf16[1744,768]{1,0:T(8,128)(2,1)}, bf16[1744,768]{1,0:T(8,128)(2,1)}, u32[]{:S(2)}, u32[]{:S(2)}) %collective-permute-start.65) | collective-permute-done | bytes 2678816 | tf_op jit(solution)/shard_map/ppermute | solution.py:595
  478.4 4.4 add_add_fusion
  483.2 11.6 %collective-permute-done.47 = bf16[512,768]{1,0:T(8,128)(2,1)} collective-permute-done((bf16[512,768]{1,0:T(8,128)(2,1)}, bf16[512,768]{1,0:T(8,128)(2,1)}, u32[]{:S(2)}, u32[]{:S(2)}) %collective-permute-start.47) | collective-permute-done | bytes 786464 | tf_op jit(solution)/shard_map/ppermute | solution.py:595
  504.6 4.7 reduce.5
  515.1 5.0 collective-permute-done.61
  522.2 40.7 %psum.21 = f32[2,768]{1,0:T(2,128)S(1)} all-reduce(f32[2,768]{1,0:T(2,128)S(1)} %pad_maximum_fusion.14), channel_id=1, replica_groups=mesh['dp'=2,'seq'=4,'mp'=4] {'dp','seq','mp'}, use_global_device_ids=true, to_apply=%region_10.11 | all-reduce | flops 1536 | bytes 12288 | tf_op jit(solution)/shard_map/psum | solution.py:839
  564.8 36.9 %all-reduce.7.cloned.1.call-done = bf16[1744,768]{1,0:T(8,128)(2,1)} async-done(((bf16[1744,768]{1,0:T(8,128)(2,1)}), bf16[1744,768]{1,0:T(8,128)(2,1)}) %all-reduce.7.cloned.1.call-update) | async-done | bytes 2678800 | tf_op jit(solution)/shard_map/psum | solution.py:790
  609.9 72.9 %all-reduce.9.cloned.1.call-done = bf16[769,579]{0,1:T(8,128)(2,1)} async-done(((bf16[769,579]{0,1:T(8,128)(2,1)}), bf16[769,579]{0,1:T(8,128)(2,1)}) %all-reduce.9.cloned.1.call-update) | async-done | bytes 890518 | tf_op jit(solution)/shard_map/psum | solution.py:834
  (451 shorter events, 219.4 us)
Async XLA Ops:
  7.2 594.4 %all-reduce.7.cloned.1.call-start = ((), (), s32[]{:S(2)}) async-start(), calls=%async_computation | async-start | bytes 5357568 | tf_op jit(solution)/shard_map/psum | solution.py:790
  9.4 42.5 %collective-permute-start.6 = (bf16[256,768]{1,0:T(8,128)(2,1)}, bf16[256,768]{1,0:T(8,128)(2,1)}, u32[]{:S(2)}, u32[]{:S(2)}) collective-permute-start(bf16[256,768]{1,0:T(8,128)(2,1)} %get-tuple-element.169), channel_id=1, source_target_pairs={{0,4},{4,8},{8,12},{1,5},{5,9},{9,13},{2,6},{6,10},{10,14},{3,7},{... | collective-permute-start | bytes 1179656 | tf_op jit(solution)/shard_map/ppermute | solution.py:599
  15.1 38.6 %collective-permute-start = (bf16[256,768]{1,0:T(8,128)(2,1)}, bf16[256,768]{1,0:T(8,128)(2,1)}, u32[]{:S(2)}, u32[]{:S(2)}) collective-permute-start(bf16[256,768]{1,0:T(8,128)(2,1)} %get-tuple-element.170), channel_id=1, source_target_pairs={{0,4},{4,8},{8,12},{1,5},{5,9},{9,13},{2,6},{6,10},{10,14},{3,7},{... | collective-permute-start | bytes 1179656 | tf_op jit(solution)/shard_map/ppermute | solution.py:599
  18.6 40.0 %collective-permute-start.27 = (bf16[192,768]{1,0:T(8,128)(2,1)}, bf16[192,768]{1,0:T(8,128)(2,1)}, u32[]{:S(2)}, u32[]{:S(2)}) collective-permute-start(bf16[192,768]{1,0:T(8,128)(2,1)} %param.25), channel_id=1, source_target_pairs={{0,1},{1,0},{2,3},{3,2},{4,5},{5,4},{6,7},{7,6},{8,9},{9,8},{10,11... | collective-permute-start | bytes 884744 | tf_op jit(solution)/shard_map/ppermute | solution.py:595
  58.6 32.7 %collective-permute-start.18 = (bf16[256,768]{1,0:T(8,128)(2,1)}, bf16[256,768]{1,0:T(8,128)(2,1)}, u32[]{:S(2)}, u32[]{:S(2)}) collective-permute-start(bf16[256,768]{1,0:T(8,128)(2,1)} %collective-permute-done), channel_id=1, source_target_pairs={{0,1},{1,0},{2,3},{3,2},{4,5},{5,4},{6,7},{7,6},{8,9},{9,8},{10,11... | collective-permute-start | bytes 1179656 | tf_op jit(solution)/shard_map/ppermute | solution.py:595
  64.1 27.5 %collective-permute-start.1 = (bf16[256,768]{1,0:T(8,128)(2,1)}, bf16[256,768]{1,0:T(8,128)(2,1)}, u32[]{:S(2)}, u32[]{:S(2)}) collective-permute-start(bf16[256,768]{1,0:T(8,128)(2,1)} %collective-permute-done), channel_id=1, source_target_pairs={{0,4},{4,8},{8,12},{1,5},{5,9},{9,13},{2,6},{6,10},{10,14},{3,7},{... | collective-permute-start | bytes 1179656 | tf_op jit(solution)/shard_map/ppermute | solution.py:599
  67.7 26.7 %collective-permute-start.23 = (bf16[256,768]{1,0:T(8,128)(2,1)}, bf16[256,768]{1,0:T(8,128)(2,1)}, u32[]{:S(2)}, u32[]{:S(2)}) collective-permute-start(bf16[256,768]{1,0:T(8,128)(2,1)} %collective-permute-done.22), channel_id=1, source_target_pairs={{0,1},{1,0},{2,3},{3,2},{4,5},{5,4},{6,7},{7,6},{8,9},{9,8},{10,11... | collective-permute-start | bytes 1179656 | tf_op jit(solution)/shard_map/ppermute | solution.py:595
  101.1 27.3 %collective-permute-start.12 = (bf16[256,768]{1,0:T(8,128)(2,1)}, bf16[256,768]{1,0:T(8,128)(2,1)S(1)}, u32[]{:S(2)}, u32[]{:S(2)}) collective-permute-start(bf16[256,768]{1,0:T(8,128)(2,1)} %collective-permute-done.1), channel_id=1, source_target_pairs={{0,1},{1,0},{2,3},{3,2},{4,5},{5,4},{6,7},{7,6},{8,9},{9,8},{10,11... | collective-permute-start | bytes 1179656 | tf_op jit(solution)/shard_map/ppermute | solution.py:595
  138.8 87.3 %collective-permute-start.30 = (bf16[768,768]{1,0:T(8,128)(2,1)S(1)}, bf16[768,768]{1,0:T(8,128)(2,1)S(1)}, u32[]{:S(2)}, u32[]{:S(2)}) collective-permute-start(bf16[768,768]{1,0:T(8,128)(2,1)S(1)} %copy-done.80), channel_id=1, source_target_pairs={{0,1},{1,0},{2,3},{3,2},{4,5},{5,4},{6,7},{7,6},{8,9},{9,8},{10,11... | collective-permute-start | bytes 3538952 | tf_op jit(solution)/shard_map/ppermute | solution.py:595
  138.9 26.9 %collective-permute-start.29 = (bf16[192,768]{1,0:T(8,128)(2,1)S(1)}, bf16[192,768]{1,0:T(8,128)(2,1)S(1)}, u32[]{:S(2)}, u32[]{:S(2)}) collective-permute-start(bf16[192,768]{1,0:T(8,128)(2,1)S(1)} %collective-permute-done.28), channel_id=1, source_target_pairs={{0,1},{1,0},{2,3},{3,2},{4,5},{5,4},{6,7},{7,6},{8,9},{9,8},{10,11... | collective-permute-start | bytes 884744 | tf_op jit(solution)/shard_map/ppermute | solution.py:595
  165.8 35.5 %collective-permute-start.33 = (bf16[768,768]{1,0:T(8,128)(2,1)S(1)}, bf16[768,768]{1,0:T(8,128)(2,1)S(1)}, u32[]{:S(2)}, u32[]{:S(2)}) collective-permute-start(bf16[768,768]{1,0:T(8,128)(2,1)S(1)} %copy-done.80), channel_id=1, source_target_pairs={{0,2},{1,3},{2,0},{3,1},{4,6},{5,7},{6,4},{7,5},{8,10},{9,11},{10,... | collective-permute-start | bytes 3538952 | tf_op jit(solution)/shard_map/ppermute | solution.py:595
  171.7 29.6 %collective-permute-start.34 = (f32[768]{0:T(1024)S(1)}, f32[768]{0:T(1024)S(1)}, u32[]{:S(2)}, u32[]{:S(2)}) collective-permute-start(f32[768]{0:T(1024)S(1)} %copy-done.83), channel_id=1, source_target_pairs={{0,2},{1,3},{2,0},{3,1},{4,6},{5,7},{6,4},{7,5},{8,10},{9,11},{10,... | collective-permute-start | bytes 9224 | tf_op jit(solution)/shard_map/ppermute | solution.py:595
  175.0 51.1 %collective-permute-start.35 = (bf16[768,768]{1,0:T(8,128)(2,1)S(1)}, bf16[768,768]{1,0:T(8,128)(2,1)S(1)}, u32[]{:S(2)}, u32[]{:S(2)}) collective-permute-start(bf16[768,768]{1,0:T(8,128)(2,1)S(1)} %copy-done.81), channel_id=1, source_target_pairs={{0,2},{1,3},{2,0},{3,1},{4,6},{5,7},{6,4},{7,5},{8,10},{9,11},{10,... | collective-permute-start | bytes 3538952 | tf_op jit(solution)/shard_map/ppermute | solution.py:595
  183.3 49.4 %collective-permute-start.32 = (bf16[768,768]{1,0:T(8,128)(2,1)S(1)}, bf16[768,768]{1,0:T(8,128)(2,1)S(1)}, u32[]{:S(2)}, u32[]{:S(2)}) collective-permute-start(bf16[768,768]{1,0:T(8,128)(2,1)S(1)} %copy-done.81), channel_id=1, source_target_pairs={{0,1},{1,0},{2,3},{3,2},{4,5},{5,4},{6,7},{7,6},{8,9},{9,8},{10,11... | collective-permute-start | bytes 3538952 | tf_op jit(solution)/shard_map/ppermute | solution.py:595
  201.3 48.6 %collective-permute-start.37 = (f32[768]{0:T(1024)S(1)}, f32[768]{0:T(1024)S(1)}, u32[]{:S(2)}, u32[]{:S(2)}) collective-permute-start(f32[768]{0:T(1024)S(1)} %collective-permute-done.34), channel_id=1, source_target_pairs={{0,1},{1,0},{2,3},{3,2},{4,5},{5,4},{6,7},{7,6},{8,9},{9,8},{10,11... | collective-permute-start | bytes 9224 | tf_op jit(solution)/shard_map/ppermute | solution.py:595
  201.3 48.6 %collective-permute-start.36 = (bf16[768,768]{1,0:T(8,128)(2,1)S(1)}, bf16[768,768]{1,0:T(8,128)(2,1)S(1)}, u32[]{:S(2)}, u32[]{:S(2)}) collective-permute-start(bf16[768,768]{1,0:T(8,128)(2,1)S(1)} %collective-permute-done.33), channel_id=1, source_target_pairs={{0,1},{1,0},{2,3},{3,2},{4,5},{5,4},{6,7},{7,6},{8,9},{9,8},{10,11... | collective-permute-start | bytes 3538952 | tf_op jit(solution)/shard_map/ppermute | solution.py:595
  278.9 117.4 %collective-permute-start.64 = (bf16[1744,768]{1,0:T(8,128)(2,1)}, bf16[1744,768]{1,0:T(8,128)(2,1)}, u32[]{:S(2)}, u32[]{:S(2)}) collective-permute-start(bf16[1744,768]{1,0:T(8,128)(2,1)} %concatenate.87), channel_id=1, source_target_pairs={{0,1},{1,0},{2,3},{3,2},{4,5},{5,4},{6,7},{7,6},{8,9},{9,8},{10,11... | collective-permute-start | bytes 8036360 | tf_op jit(solution)/shard_map/ppermute | solution.py:595
  326.5 32.4 %collective-permute-start.53 = (bf16[512,768]{1,0:T(8,128)(2,1)S(1)}, bf16[512,768]{1,0:T(8,128)(2,1)S(1)}, u32[]{:S(2)}, u32[]{:S(2)}) collective-permute-start(bf16[512,768]{1,0:T(8,128)(2,1)S(1)} %slice_add_fusion.2), channel_id=1, source_target_pairs={{0,2},{1,3},{2,0},{3,1},{4,6},{5,7},{6,4},{7,5},{8,10},{9,11},{10,... | collective-permute-start | bytes 2359304 | tf_op jit(solution)/shard_map/ppermute | solution.py:595
  348.5 51.8 %collective-permute-start.46 = (bf16[512,768]{1,0:T(8,128)(2,1)}, bf16[512,768]{1,0:T(8,128)(2,1)}, u32[]{:S(2)}, u32[]{:S(2)}) collective-permute-start(bf16[512,768]{1,0:T(8,128)(2,1)} %get-tuple-element.159), channel_id=1, source_target_pairs={{0,1},{1,0},{2,3},{3,2},{4,5},{5,4},{6,7},{7,6},{8,9},{9,8},{10,11... | collective-permute-start | bytes 2359304 | tf_op jit(solution)/shard_map/ppermute | solution.py:595
  349.6 51.3 %collective-permute-start.48 = (bf16[512,768]{1,0:T(8,128)(2,1)}, bf16[512,768]{1,0:T(8,128)(2,1)}, u32[]{:S(2)}, u32[]{:S(2)}) collective-permute-start(bf16[512,768]{1,0:T(8,128)(2,1)} %get-tuple-element.160), channel_id=1, source_target_pairs={{0,1},{1,0},{2,3},{3,2},{4,5},{5,4},{6,7},{7,6},{8,9},{9,8},{10,11... | collective-permute-start | bytes 2359304 | tf_op jit(solution)/shard_map/ppermute | solution.py:595
  358.9 58.8 %collective-permute-start.50 = (bf16[512,768]{1,0:T(8,128)(2,1)}, bf16[512,768]{1,0:T(8,128)(2,1)}, u32[]{:S(2)}, u32[]{:S(2)}) collective-permute-start(bf16[512,768]{1,0:T(8,128)(2,1)} %slice_add_fusion.4), channel_id=1, source_target_pairs={{0,2},{1,3},{2,0},{3,1},{4,6},{5,7},{6,4},{7,5},{8,10},{9,11},{10,... | collective-permute-start | bytes 2359304 | tf_op jit(solution)/shard_map/ppermute | solution.py:595
  364.7 53.1 %collective-permute-start.58 = (bf16[512,768]{1,0:T(8,128)(2,1)}, bf16[512,768]{1,0:T(8,128)(2,1)}, u32[]{:S(2)}, u32[]{:S(2)}) collective-permute-start(bf16[512,768]{1,0:T(8,128)(2,1)} %fusion.54), channel_id=1, source_target_pairs={{4,0},{8,4},{12,8},{5,1},{9,5},{13,9},{6,2},{10,6},{14,10},{7,3},{... | collective-permute-start | bytes 2359304 | tf_op jit(solution)/shard_map/ppermute | solution.py:603
  396.2 39.8 %collective-permute-start.63 = (bf16[1744,768]{1,0:T(8,128)(2,1)}, bf16[1744,768]{1,0:T(8,128)(2,1)}, u32[]{:S(2)}, u32[]{:S(2)}) collective-permute-start(bf16[1744,768]{1,0:T(8,128)(2,1)} %concatenate.85), channel_id=1, source_target_pairs={{0,1},{1,0},{2,3},{3,2},{4,5},{5,4},{6,7},{7,6},{8,9},{9,8},{10,11... | collective-permute-start | bytes 8036360 | tf_op jit(solution)/shard_map/ppermute | solution.py:595
  400.9 77.6 %collective-permute-start.65 = (bf16[1744,768]{1,0:T(8,128)(2,1)}, bf16[1744,768]{1,0:T(8,128)(2,1)}, u32[]{:S(2)}, u32[]{:S(2)}) collective-permute-start(bf16[1744,768]{1,0:T(8,128)(2,1)} %add.446), channel_id=1, source_target_pairs={{0,2},{1,3},{2,0},{3,1},{4,6},{5,7},{6,4},{7,5},{8,10},{9,11},{10,... | collective-permute-start | bytes 8036360 | tf_op jit(solution)/shard_map/ppermute | solution.py:595
  417.7 65.4 %collective-permute-start.45 = (bf16[512,768]{1,0:T(8,128)(2,1)}, bf16[512,768]{1,0:T(8,128)(2,1)}, u32[]{:S(2)}, u32[]{:S(2)}) collective-permute-start(bf16[512,768]{1,0:T(8,128)(2,1)} %get-tuple-element.158), channel_id=1, source_target_pairs={{0,1},{1,0},{2,3},{3,2},{4,5},{5,4},{6,7},{7,6},{8,9},{9,8},{10,11... | collective-permute-start | bytes 2359304 | tf_op jit(solution)/shard_map/ppermute | solution.py:595
  417.7 77.1 %collective-permute-start.47 = (bf16[512,768]{1,0:T(8,128)(2,1)}, bf16[512,768]{1,0:T(8,128)(2,1)}, u32[]{:S(2)}, u32[]{:S(2)}) collective-permute-start(bf16[512,768]{1,0:T(8,128)(2,1)} %slice_add_fusion.6), channel_id=1, source_target_pairs={{0,2},{1,3},{2,0},{3,1},{4,6},{5,7},{6,4},{7,5},{8,10},{9,11},{10,... | collective-permute-start | bytes 2359304 | tf_op jit(solution)/shard_map/ppermute | solution.py:595
  421.2 73.6 %collective-permute-start.59 = (bf16[512,768]{1,0:T(8,128)(2,1)}, bf16[512,768]{1,0:T(8,128)(2,1)}, u32[]{:S(2)}, u32[]{:S(2)}) collective-permute-start(bf16[512,768]{1,0:T(8,128)(2,1)} %fusion.56), channel_id=1, source_target_pairs={{4,0},{8,4},{12,8},{5,1},{9,5},{13,9},{6,2},{10,6},{14,10},{7,3},{... | collective-permute-start | bytes 2359304 | tf_op jit(solution)/shard_map/ppermute | solution.py:603
  436.0 74.8 %collective-permute-start.39 = (bf16[512,768]{1,0:T(8,128)(2,1)}, bf16[512,768]{1,0:T(8,128)(2,1)}, u32[]{:S(2)}, u32[]{:S(2)}) collective-permute-start(bf16[512,768]{1,0:T(8,128)(2,1)} %get-tuple-element.203), channel_id=1, source_target_pairs={{0,1},{1,0},{2,3},{3,2},{4,5},{5,4},{6,7},{7,6},{8,9},{9,8},{10,11... | collective-permute-start | bytes 2359304 | tf_op jit(solution)/shard_map/ppermute | solution.py:595
  478.4 41.7 %collective-permute-start.41 = (bf16[512,768]{1,0:T(8,128)(2,1)}, bf16[512,768]{1,0:T(8,128)(2,1)}, u32[]{:S(2)}, u32[]{:S(2)}) collective-permute-start(bf16[512,768]{1,0:T(8,128)(2,1)} %collective-permute-done.40), channel_id=1, source_target_pairs={{0,1},{1,0},{2,3},{3,2},{4,5},{5,4},{6,7},{7,6},{8,9},{9,8},{10,11... | collective-permute-start | bytes 2359304 | tf_op jit(solution)/shard_map/ppermute | solution.py:595
  482.8 199.9 %all-reduce.9.cloned.1.call-start = ((), (), s32[]{:S(2)}) async-start(), calls=%async_computation.1 | async-start | bytes 2093056 | tf_op jit(solution)/shard_map/psum | solution.py:834
  510.8 52.8 %collective-permute-start.60 = (bf16[512,768]{1,0:T(8,128)(2,1)}, bf16[512,768]{1,0:T(8,128)(2,1)}, u32[]{:S(2)}, u32[]{:S(2)}) collective-permute-start(bf16[512,768]{1,0:T(8,128)(2,1)} %get-tuple-element.150), channel_id=1, source_target_pairs={{0,1},{1,0},{2,3},{3,2},{4,5},{5,4},{6,7},{7,6},{8,9},{9,8},{10,11... | collective-permute-start | bytes 2359304 | tf_op jit(solution)/shard_map/ppermute | solution.py:595
  520.1 82.9 %collective-permute-start.62 = (bf16[512,768]{1,0:T(8,128)(2,1)}, bf16[512,768]{1,0:T(8,128)(2,1)}, u32[]{:S(2)}, u32[]{:S(2)}) collective-permute-start(bf16[512,768]{1,0:T(8,128)(2,1)} %collective-permute-done.61), channel_id=1, source_target_pairs={{0,1},{1,0},{2,3},{3,2},{4,5},{5,4},{6,7},{7,6},{8,9},{9,8},{10,11... | collective-permute-start | bytes 2359304 | tf_op jit(solution)/shard_map/ppermute | solution.py:595
  (124 other events, 1397.7 us)
Sparse Core Ops, SparseCore 0:
  483.0 118.5 all-reduce.6
  605.7 77.0 all-reduce.8

commit v2 on v0

--- a/solution.py
+++ b/solution.py
@@ -1,6 +1,10 @@
+import functools
+
 import jax
 import jax.numpy as jnp
 from jax import lax
+from jax.experimental import pallas as pl
+from jax.experimental.pallas import tpu as pltpu
 from jax.sharding import PartitionSpec as P
 
 HD = 64
@@ -63,7 +67,7 @@
     )
 
 
-def body(
+def body_general(
     inputs,
     selection,
     gain1,
@@ -272,7 +276,935 @@
     )
 
 
+WIDE = 256
+BF = jnp.bfloat16
+F32 = jnp.float32
+ANYWHERE = pl.BlockSpec(memory_space=pl.ANY)
+
+
+def matmul(left, right):
+    return jnp.dot(left, right, preferred_element_type=F32)
+
+
+def near_far(left, right):
+    return lax.dot_general(left, right, (((1,), (1,)), ((), ())), preferred_element_type=F32)
+
+
+def taking(microseconds):
+    return pl.CostEstimate(
+        flops=int(microseconds * 1.1e9), bytes_accessed=int(microseconds * 1e5), transcendentals=0
+    )
+
+
+def vmem(mebibytes):
+    return pltpu.CompilerParams(vmem_limit_bytes=mebibytes * 1024 * 1024)
+
+
+def ordered_after(kernel, at, count):
+    return lambda *refs: kernel(*refs[:at], *refs[at + count :])
+
+
+def whole(array):
+    shape = array.shape
+    return pl.BlockSpec(shape, lambda *_: (0,) * len(shape), pipeline_mode=pl.Buffered(1))
+
+
+def normed_parts(value):
+    center = jnp.mean(value, axis=-1, keepdims=True)
+    centered = value - center
+    spread = jnp.mean(centered * centered, axis=-1, keepdims=True)
+    scale = lax.rsqrt(spread + EPSILON)
+    return centered * scale, scale
+
+
+def norm_back(grad, hat, scale, gain):
+    g = gain * grad
+    return scale * (
+        g
+        - jnp.mean(g, axis=-1, keepdims=True)
+        - hat * jnp.mean(g * hat, axis=-1, keepdims=True)
+    )
+
+
+def column_sums(array):
+    return jnp.sum(array, axis=0, keepdims=True)
+
+
+def project_rows(width, value, vectors, lines, weights, fi, ka, va, kt, vt, qt):
+    hat, _ = normed_parts(value.astype(F32))
+    normed = (hat * vectors[0:1, :] + vectors[1:2, :]).astype(BF)
+    fi[...] = normed
+    half = WIDE // 2
+    heads = width // HD
+    keys = matmul(normed, weights[0][...]) + lines[0:1, :]
+    values = matmul(normed, weights[1][...]) + lines[1:2, :]
+    high = keys[:, half:]
+    lane = lax.broadcasted_iota(jnp.int32, high.shape, 1) - (width - half)
+    small = jnp.exp(-jnp.abs(high))
+    mark = jnp.minimum(high, 0.0) - jnp.log1p(small)
+    slope = jnp.where(high >= 0, small, 1.0) / (1.0 + small)
+    ones = jnp.where((lane >= heads) & (lane < heads + 3), 1.0, 0.0)
+    marked = (lane >= 0) & (lane < heads)
+    ka[:, :half] = keys[:, :half].astype(BF)
+    ka[:, half:] = jnp.where(lane < 0, high, jnp.where(marked, mark, ones)).astype(BF)
+    va[:, :half] = values[:, :half].astype(BF)
+    va[:, half:] = jnp.where(
+        lane < 0, values[:, half:], jnp.where(marked, slope, ones)
+    ).astype(BF)
+    kt[...] = keys.T[:width].astype(BF)
+    vt[...] = values.T[:width].astype(BF)
+    if qt is not None:
+        query = (matmul(normed, weights[2][...]) + lines[2:3, :]).astype(BF).astype(F32)
+        qt[...] = (query * HD ** (-0.5)).T[:width].astype(BF)
+
+
+def project_own_kernel(ids, x, vectors, lines, wk, wv, wq, fi, ka, va, kt, vt, qt):
+    del ids
+    project_rows(qt.shape[0], x[...], vectors, lines, (wk, wv, wq), fi, ka, va, kt, vt, qt)
+
+
+def project_kernel(count, *refs):
+    vectors, lines, wk, wv = refs[:4]
+    pieces = refs[4 : 4 + count]
+    fi, ka, va, kt, vt, held, sems = refs[9 + count :]
+    step = pl.program_id(0)
+
+    def copy(j):
+        return pltpu.make_async_copy(pieces[j], held.at[j], sems.at[j])
+
+    @pl.when(step == 0)
+    def _():
+        for j in range(count):
+            copy(j).start()
+
+    for j in range(count):
+
+        @pl.when(step == j)
+        def _(j=j):
+            copy(j).wait()
+
+    project_rows(kt.shape[0], held[step], vectors, lines, (wk, wv), fi, ka, va, kt, vt, None)
+
+
+def project_shapes(total, model, width):
+    return [
+        jax.ShapeDtypeStruct((total, model), BF),
+        jax.ShapeDtypeStruct((total, WIDE), BF),
+        jax.ShapeDtypeStruct((total, WIDE), BF),
+        jax.ShapeDtypeStruct((width, total), BF),
+        jax.ShapeDtypeStruct((width, total), BF),
+    ]
+
+
+def project_specs(block, model, width, place):
+    rows = lambda cols: pl.BlockSpec((block, cols), lambda j, *_: (place(j), 0))
+    flat = pl.BlockSpec((width, block), lambda j, *_: (0, place(j)))
+    return [rows(model), rows(WIDE), rows(WIDE), flat, flat]
+
+
+def project_own(ids, x, vectors, lines, weights, width, total, block, after):
+    rows, model = x.shape
+    per = rows // 4 // block
+    operands = [vectors, lines, *weights]
+    return pl.pallas_call(
+        ordered_after(project_own_kernel, 2 + len(operands), len(after)),
+        grid_spec=pltpu.PrefetchScalarGridSpec(
+            num_scalar_prefetch=1,
+            grid=(rows // block,),
+            in_specs=[
+                pl.BlockSpec(
+                    (block, model),
+                    lambda j, ids: (
+                        jnp.bitwise_xor(lax.div(j, per), ids[0]) * per + lax.rem(j, per),
+                        0,
+                    ),
+                )
+            ]
+            + [whole(a) for a in operands]
+            + [ANYWHERE] * len(after),
+            out_specs=project_specs(block, model, width, lambda j: j)
+            + [pl.BlockSpec((width, block), lambda j, *_: (0, j))],
+        ),
+        out_shape=project_shapes(total, model, width) + [jax.ShapeDtypeStruct((width, rows), BF)],
+        compiler_params=vmem(32),
+        cost_estimate=taking(8),
+        name="project_own",
+    )(ids, x, *operands, *after)
+
+
+def project(pieces, place, vectors, lines, weights, buffers, after=()):
+    block, model = pieces[0].shape
+    total, width = buffers[0].shape[0], buffers[3].shape[0]
+    count = len(pieces)
+    operands = [vectors, lines, *weights]
+    return pl.pallas_call(
+        ordered_after(
+            functools.partial(project_kernel, count), len(operands) + count + 5, len(after)
+        ),
+        grid=(count,),
+        in_specs=[whole(a) for a in operands] + [ANYWHERE] * (count + 5 + len(after)),
+        out_specs=project_specs(block, model, width, place),
+        out_shape=project_shapes(total, model, width),
+        scratch_shapes=[
+            pltpu.VMEM((count, block, model), BF),
+            pltpu.SemaphoreType.DMA((count,)),
+        ],
+        input_output_aliases={len(operands) + count + i: i for i in range(5)},
+        compiler_params=vmem(32),
+        cost_estimate=taking(count),
+        name="project",
+    )(*operands, *pieces, *buffers, *after)
+
+
+def head_diagonal(rows, tail):
+    width = rows.shape[0]
+    heads = width // HD
+    columns = []
+    for h in range(heads):
+        parts = []
+        if h > 0:
+            parts.append(jnp.zeros((h * HD, KB), BF))
+        parts.append(rows[h * HD : (h + 1) * HD])
+        if h < heads - 1:
+            parts.append(jnp.zeros(((heads - 1 - h) * HD, KB), BF))
+        columns.append(jnp.concatenate(parts, axis=0))
+    top = jnp.concatenate(columns, axis=1)
+    rest = jnp.zeros((WIDE - width - 16, heads * KB), BF)
+    return jnp.concatenate([top, tail.astype(BF), rest], axis=0)
+
+
+def tail_rows(heads, marked, term):
+    shape = (16, heads * KB)
+    row = lax.broadcasted_iota(jnp.int32, shape, 0)
+    column = lax.broadcasted_iota(jnp.int32, shape, 1) // KB
+    tail = jnp.where(row == column, 1.0, 0.0) if marked else jnp.zeros(shape, F32)
+    if term is not None:
+        for piece in range(3):
+            part = term.astype(BF).astype(F32)
+            tail = jnp.where(row == heads + piece, part, tail)
+            term = term - part
+    return tail
+
+
+def offsets_tile(heads):
+    shape = (KB, heads * KB)
+    key = lax.broadcasted_iota(jnp.int32, shape, 0)
+    query = lax.rem(lax.broadcasted_iota(jnp.int32, shape, 1), KB)
+    return key - query
+
+
+def spots(ids, chosen, step, blocks):
+    me, rank, per = ids[0], ids[1], blocks // 4
+    natural = jnp.bitwise_xor(lax.div(step, per), me) * per + lax.rem(step, per)
+    block = rank * blocks + natural
+    picked = [chosen[natural, t] for t in (1, 2, 3)]
+    starts = []
+    for name in [jnp.maximum(block - 1, 0), block, *picked]:
+        inner = lax.rem(name, blocks)
+        place = (rank - lax.div(name, blocks)) * blocks + lax.rem(inner, per)
+        place = place + jnp.bitwise_xor(lax.div(inner, per), me) * per
+        starts.append(pl.multiple_of(place * KB, KB))
+    first = jnp.where(block >= 1, KB - WINDOW, 2 * KB)
+    return starts, [first] + [(block - c) * KB - WINDOW for c in picked]
+
+
+def masks_of(gap, bounds):
+    return [gap > bounds[0], gap <= 0] + [gap <= b for b in bounds[1:]]
+
+
+def diagonal_of(full, heads):
+    return jnp.concatenate(
+        [full[h * HD : (h + 1) * HD, h * KB : (h + 1) * KB] for h in range(heads)], axis=0
+    )
+
+
+def attend_kernel(blocks, ids, chosen, ka, vt, qt, *outs):
+    *mixed, norm = outs
+    step = pl.program_id(0)
+    width = qt.shape[0]
+    heads = width // HD
+    query = qt[...]
+    plain = head_diagonal(query, tail_rows(heads, False, None))
+    marked = head_diagonal(query, tail_rows(heads, True, None))
+    starts, bounds = spots(ids, chosen, step, blocks)
+    tiles = [ka[pl.ds(s, KB), :] for s in starts]
+    near = matmul(jnp.concatenate(tiles[:2], axis=0), plain)
+    far = matmul(jnp.concatenate(tiles[1:], axis=0), marked)
+    gap = offsets_tile(heads)
+    scores = [near[:KB], jnp.where(gap > -WINDOW, near[KB:], far[:KB])]
+    scores += [far[KB * (1 + t) : KB * (2 + t)] for t in range(3)]
+    scores = [jnp.where(m, s, NEGATIVE) for m, s in zip(masks_of(gap, bounds), scores)]
+    top = functools.reduce(jnp.maximum, scores)
+    top = jnp.max(top, axis=0, keepdims=True)
+    weights = [jnp.exp(s - top) for s in scores]
+    total = jnp.sum(functools.reduce(jnp.add, weights), axis=0, keepdims=True)
+    stacked = jnp.concatenate([w.astype(BF) for w in weights], axis=0)
+    values = jnp.concatenate([vt[:, pl.ds(s, KB)] for s in starts], axis=1)
+    full = matmul(values, stacked) / total
+    result = diagonal_of(full, heads).astype(BF)
+    norm[0] = top + jnp.log(total)
+    for p in range(4):
+
+        @pl.when(lax.div(step, blocks // 4) == p)
+        def _(p=p):
+            mixed[p][...] = result
+
+
+def attend(ids, chosen, ka, vt, qt, blocks):
+    width = qt.shape[0]
+    heads = width // HD
+    per = blocks // 4
+    piece = lambda p: pl.BlockSpec(
+        (width, KB), lambda i, *_: (0, jnp.clip(i - per * p, 0, per - 1))
+    )
+    return pl.pallas_call(
+        functools.partial(attend_kernel, blocks),
+        grid_spec=pltpu.PrefetchScalarGridSpec(
+            num_scalar_prefetch=2,
+            grid=(blocks,),
+            in_specs=[whole(ka), whole(vt), pl.BlockSpec((width, KB), lambda i, *_: (0, i))],
+            out_specs=[piece(p) for p in range(4)]
+            + [pl.BlockSpec((1, 1, heads * KB), lambda i, *_: (i, 0, 0))],
+        ),
+        out_shape=[jax.ShapeDtypeStruct((width, per * KB), BF)] * 4
+        + [jax.ShapeDtypeStruct((blocks, 1, heads * KB), F32)],
+        compiler_params=vmem(40),
+        cost_estimate=taking(14),
+        name="attend",
+    )(ids, chosen, ka, vt, qt)
+
+
+def attend_back_kernel(
+    blocks,
+    ids,
+    chosen,
+    ka,
+    va,
+    kt,
+    qt,
+    norm,
+    *refs,
+):
+    grads = refs[:4]
+    spread, query_grad, totals, key_sum, value_sum, grad_all, sems = refs[4:]
+    step = pl.program_id(0)
+    width = qt.shape[0]
+    heads = width // HD
+    per = blocks // 4
+
+    def copy(j):
+        return pltpu.make_async_copy(grads[j], grad_all.at[j], sems.at[j])
+
+    @pl.when(step == 0)
+    def _():
+        for j in range(4):
+            copy(j).start()
+        key_sum[...] = jnp.zeros_like(key_sum)
+        value_sum[...] = jnp.zeros_like(value_sum)
+        totals[...] = jnp.zeros_like(totals)
+        for j in range(4):
+            copy(j).wait()
+
+    @pl.when(step < blocks)
+    def _():
+        query = qt[...]
+        lanes = pl.ds(pl.multiple_of(lax.rem(step, per) * KB, KB), KB)
+        upstream = grad_all[lax.div(step, per), :, lanes]
+        plain = head_diagonal(query, tail_rows(heads, False, -norm[0]))
+        marked = head_diagonal(query, tail_rows(heads, True, -norm[0]))
+        back = head_diagonal(upstream, tail_rows(heads, False, None))
+        starts, bounds = spots(ids, chosen, step, blocks)
+        tiles = [ka[pl.ds(s, KB), :] for s in starts]
+        near = matmul(jnp.concatenate(tiles[:2], axis=0), plain)
+        far = matmul(jnp.concatenate(tiles[1:], axis=0), marked)
+        slopes = matmul(jnp.concatenate([va[pl.ds(s, KB), :] for s in starts], axis=0), back)
+        gap = offsets_tile(heads)
+        masks = masks_of(gap, bounds)
+        window = gap > -WINDOW
+        scores = [near[:KB], jnp.where(window, near[KB:], far[:KB])]
+        scores += [far[KB * (1 + t) : KB * (2 + t)] for t in range(3)]
+        probs = [jnp.where(m, jnp.exp(s), 0.0) for m, s in zip(masks, scores)]
+        terms = [p * slopes[c * KB : (c + 1) * KB] for c, p in enumerate(probs)]
+        delta = column_sums(functools.reduce(jnp.add, terms))
+        signals = [t - p * delta for t, p in zip(terms, probs)]
+        own = signals[1]
+        near_signal = jnp.concatenate([signals[0], jnp.where(window, own, 0.0)], axis=0).astype(BF)
+        far_exact = jnp.concatenate([jnp.where(window, 0.0, own)] + signals[2:], axis=0)
+        far_signal = far_exact.astype(BF)
+        signal = jnp.concatenate(signals, axis=0).astype(BF)
+        prob = jnp.concatenate(probs, axis=0).astype(BF)
+        near_keys = near_far(near_signal, plain)
+        far_keys = near_far(far_signal, marked)
+        rest = (far_exact - far_signal.astype(F32)).astype(BF)
+        far_rest = near_far(rest, marked[WIDE // 2 :])
+        value_parts = near_far(prob, back)
+        key_parts = [near_keys[:KB], near_keys[KB:] + far_keys[:KB]]
+        key_parts += [far_keys[KB * (1 + t) : KB * (2 + t)] for t in range(3)]
+        for c, s in enumerate(starts):
+            key_sum[pl.ds(s, KB), :] += key_parts[c]
+            value_sum[pl.ds(s, KB), :] += value_parts[c * KB : (c + 1) * KB]
+            if c > 0:
+                key_sum[pl.ds(s, KB), WIDE // 2 :] += far_rest[(c - 1) * KB : c * KB]
+        keys = jnp.concatenate([kt[:, pl.ds(s, KB)] for s in starts], axis=1)
+        full = diagonal_of(matmul(keys, signal), heads) * HD ** (-0.5)
+        full = jnp.concatenate([full, jnp.zeros((WIDE - width, KB), F32)], axis=0).T
+        query_grad[...] = full.astype(BF)
+        totals[:, 2 * WIDE :] += column_sums(full)
+
+    @pl.when(step >= blocks)
+    def _():
+        rows = spread.shape[0]
+        at = pl.ds(pl.multiple_of((step - blocks) * rows, rows), rows)
+        lane = lax.broadcasted_iota(jnp.int32, (rows, WIDE), 1)
+        marks = (lane >= width) & (lane < width + heads)
+        keys = jnp.where(lane < width, key_sum[at, :], 0.0)
+        keys = jnp.where(marks, key_sum[at, :] * va[at, :].astype(F32), keys)
+        values = jnp.where(lane < width, value_sum[at, :], 0.0)
+        spread[:, :WIDE] = keys.astype(BF)
+        spread[:, WIDE:] = values.astype(BF)
+        totals[:, :WIDE] += column_sums(keys)
+        totals[:, WIDE : 2 * WIDE] += column_sums(values)
+
+
+def attend_back(ids, chosen, ka, va, kt, qt, norm, grads, blocks, after=()):
+    width = qt.shape[0]
+    heads = width // HD
+    total = ka.shape[0]
+    rows = 4 * KB
+    last = lambda i: jnp.minimum(i, blocks - 1)
+    return pl.pallas_call(
+        ordered_after(functools.partial(attend_back_kernel, blocks), 11, len(after)),
+        grid_spec=pltpu.PrefetchScalarGridSpec(
+            num_scalar_prefetch=2,
+            grid=(blocks + total // rows,),
+            in_specs=[
+                whole(ka),
+                whole(va),
+                whole(kt),
+                pl.BlockSpec((width, KB), lambda i, *_: (0, last(i))),
+                pl.BlockSpec((1, 1, heads * KB), lambda i, *_: (last(i), 0, 0)),
+            ]
+            + [ANYWHERE] * (4 + len(after)),
+            out_specs=[
+                pl.BlockSpec((rows, 2 * WIDE), lambda i, *_: (jnp.maximum(i - blocks, 0), 0)),
+                pl.BlockSpec((KB, WIDE), lambda i, *_: (last(i), 0)),
+                pl.BlockSpec((1, 3 * WIDE), lambda i, *_: (0, 0)),
+            ],
+            scratch_shapes=[
+                pltpu.VMEM((total, WIDE), F32),
+                pltpu.VMEM((total, WIDE), F32),
+                pltpu.VMEM((4, width, blocks // 4 * KB), BF),
+                pltpu.SemaphoreType.DMA((4,)),
+            ],
+        ),
+        out_shape=[
+            jax.ShapeDtypeStruct((total, 2 * WIDE), BF),
+            jax.ShapeDtypeStruct((blocks * KB, WIDE), BF),
+            jax.ShapeDtypeStruct((1, 3 * WIDE), F32),
+        ],
+        compiler_params=vmem(56),
+        cost_estimate=taking(36),
+        name="attend_back",
+    )(ids, chosen, ka, va, kt, qt, norm, *grads, *after)
+
+
+def feed_forward_kernel(order, ids, vectors, tokens, upstream, *refs):
+    features, outs, ups, downs = refs[:4], refs[4:8], refs[8:12], refs[12:16]
+    mixed_grads = refs[16:20]
+    output, hidden_grad, kept, sent, kept_out, sent_out, sums, up_biases = refs[20:28]
+    out_all, up_all, down_all, hidden, hat, scale, second_in, feed, second_grad, sems = refs[28:]
+    step = pl.program_id(0)
+    width = features[0].shape[0]
+    model = tokens.shape[1]
+
+    def copies(j, turned=False):
+        slot = order.index(j)
+        up, down = (downs[j], ups[j]) if turned else (ups[j], downs[j])
+        return [
+            pltpu.make_async_copy(up, up_all.at[slot], sems.at[4 + slot]),
+            pltpu.make_async_copy(down, down_all.at[slot], sems.at[8 + slot]),
+        ]
+
+    def out_copy(j):
+        return pltpu.make_async_copy(outs[j], out_all.at[j], sems.at[j])
+
+    @pl.when(step == 0)
+    def _():
+        for j in range(4):
+            out_copy(j).start()
+        for j in order:
+            if j < 2:
+                for copy in copies(j):
+                    copy.start()
+            else:
+
+                @pl.when(ids[2] == 0)
+                def _(j=j):
+                    for copy in copies(j):
+                        copy.start()
+
+                @pl.when(ids[2] != 0)
+                def _(j=j):
+                    for copy in copies(j, True):
+                        copy.start()
+
+        for j in range(4):
+            out_copy(j).wait()
+        branch = vectors[2:3, :]
+        for j in range(4):
+            branch = branch + rows_inner(features[j][...], out_all[j, :width, :])
+        value = tokens[...].astype(F32) + branch
+        hidden[...] = value
+        normed, inverse = normed_parts(value)
+        scale[...] = inverse
+        hat[...] = normed
+        second_in[...] = (normed * vectors[3:4, :] + vectors[4:5, :]).astype(BF)
+        feed[...] = jnp.zeros_like(feed)
+        second_grad[...] = jnp.zeros_like(second_grad)
+
+    for slot, j in enumerate(order):
+
+        @pl.when(step == slot)
+        def _(j=j):
+            for copy in copies(j):
+                copy.wait()
+
+    bias = jnp.zeros((1, model), F32)
+    for slot, j in enumerate(order):
+        lines = out_all[j, width : width + 16, :].astype(F32)
+        bias = jnp.where(step == slot, lines[0:1] + lines[1:2], bias)
+    up, down = up_all[step], down_all[step]
+    pre = matmul(second_in[...], up) + bias
+    slope = 0.7978845608028654
+    square = pre * pre
+    bend = jnp.tanh(slope * pre * (1.0 + 0.044715 * square))
+    act = (0.5 * pre * (1.0 + bend)).astype(BF)
+    derivative = 0.5 * (1.0 + bend) + 0.5 * pre * (1.0 - bend * bend) * slope * (
+        1.0 + 3 * 0.044715 * square
+    )
+    feed[...] += matmul(act, down)
+    pre_grad = near_far(upstream[...], down) * derivative
+    pre_low = pre_grad.astype(BF)
+    up_biases[0] = column_sums(pre_low.astype(F32))
+    second_grad[...] += near_far(pre_low, up)
+    up_grad = rows_inner(second_in[...], pre_low).astype(BF)
+    down_grad = rows_inner(act, upstream[...]).astype(BF)
+
+    @pl.when(step < 2)
+    def _():
+        sent[0, :model] = up_grad
+        sent[0, model:] = down_grad
+
+    @pl.when(step >= 2)
+    def _():
+        kept[0, :model] = up_grad
+        kept[0, model:] = down_grad
+
+    @pl.when(step == 3)
+    def _():
+        output[...] = (hidden[...] + feed[...] + vectors[5:6, :]).astype(BF)
+        grad = second_grad[...]
+        normed = hat[...]
+        upstream_f = upstream[...].astype(F32)
+        back = upstream_f + norm_back(grad, normed, scale[...], vectors[3:4, :])
+        hidden_grad[...] = back
+        low = back.astype(BF)
+        for j in range(4):
+            mixed_grads[j][...] = near_far(out_all[j, :width, :], low).astype(BF)
+            out_grad = matmul(features[j][...], low).astype(BF)
+            (sent_out if j % 2 else kept_out)[j // 2] = out_grad
+        sums[...] = jnp.concatenate(
+            [column_sums(a) for a in (grad * normed, grad, back, upstream_f)], axis=0
+        )
+
+
+def feed_forward(ids, vectors, tokens, upstream, features, outs, ups, downs):
+    width, quarter = features[0].shape
+    model = tokens.shape[1]
+    order = (1, 3, 0, 2)
+    flat = lambda a: pl.BlockSpec(a.shape, lambda j, *_: (0,) * len(a.shape))
+    mine = pl.BlockSpec(
+        (quarter, model), lambda j, ids: (ids[0], 0), pipeline_mode=pl.Buffered(1)
+    )
+    shape = jax.ShapeDtypeStruct
+    out_shape = [shape((width, quarter), BF)] * 4 + [
+        shape((quarter, model), BF),
+        shape((quarter, model), F32),
+        shape((2, 2 * model, model), BF),
+        shape((2, 2 * model, model), BF),
+        shape((2, width, model), BF),
+        shape((2, width, model), BF),
+        shape((4, model), F32),
+        shape((4, 1, model), F32),
+    ]
+    out_specs = [flat(a) for a in out_shape]
+    out_specs[6] = pl.BlockSpec((1, 2 * model, model), lambda j, *_: (jnp.maximum(j - 2, 0), 0, 0))
+    out_specs[7] = pl.BlockSpec((1, 2 * model, model), lambda j, *_: (jnp.minimum(j, 1), 0, 0))
+    out_specs[11] = pl.BlockSpec((1, 1, model), lambda j, *_: (j, 0, 0))
+    return pl.pallas_call(
+        functools.partial(feed_forward_kernel, order),
+        grid_spec=pltpu.PrefetchScalarGridSpec(
+            num_scalar_prefetch=1,
+            grid=(4,),
+            in_specs=[whole(vectors), mine, mine]
+            + [whole(a) for a in features]
+            + [ANYWHERE] * 12,
+            out_specs=out_specs,
+            scratch_shapes=[
+                pltpu.VMEM((4, width + 16, model), BF),
+                pltpu.VMEM((4, model, model), BF),
+                pltpu.VMEM((4, model, model), BF),
+                pltpu.VMEM((quarter, model), F32),
+                pltpu.VMEM((quarter, model), F32),
+                pltpu.VMEM((quarter, 1), F32),
+                pltpu.VMEM((quarter, model), BF),
+                pltpu.VMEM((quarter, model), F32),
+                pltpu.VMEM((quarter, model), F32),
+                pltpu.SemaphoreType.DMA((12,)),
+            ],
+        ),
+        out_shape=out_shape,
+        compiler_params=vmem(56),
+        cost_estimate=taking(30),
+        name="feed_forward",
+    )(ids, vectors, tokens, upstream, *features, *outs, *ups, *downs)
+
+
+def push_kernel(spread, wk, wv, *refs):
+    kept, sent = refs[-2:]
+    step = pl.program_id(0)
+    part = near_far(spread[:, :WIDE], wk[...]) + near_far(spread[:, WIDE:], wv[...])
+    if len(refs) > 2:
+        part = part + near_far(refs[0][...], refs[1][...])
+    part = part.astype(BF)
+
+    @pl.when(step < 2)
+    def _():
+        sent[0] = part
+
+    @pl.when(step >= 2)
+    def _():
+        kept[0] = part
+
+
+def push(spread, weights, k, quarter, query_grad=None, after=()):
+    wk, wv, wq = weights
+    model = wk.shape[0]
+    quarter_of = lambda j: 2 * j + 1 - jnp.where(j >= 2, 5, 0)
+    operands = [spread, wk, wv]
+    in_specs = [
+        pl.BlockSpec((quarter, 2 * WIDE), lambda j: (4 * k + quarter_of(j), 0)),
+        whole(wk),
+        whole(wv),
+    ]
+    if query_grad is not None:
+        operands += [query_grad, wq]
+        in_specs += [pl.BlockSpec((quarter, WIDE), lambda j: (quarter_of(j), 0)), whole(wq)]
+    return pl.pallas_call(
+        ordered_after(push_kernel, len(operands), len(after)),
+        grid=(4,),
+        in_specs=in_specs + [ANYWHERE] * len(after),
+        out_specs=[
+            pl.BlockSpec((1, quarter, model), lambda j: (jnp.maximum(j - 2, 0), 0, 0)),
+            pl.BlockSpec((1, quarter, model), lambda j: (jnp.minimum(j, 1), 0, 0)),
+        ],
+        out_shape=[jax.ShapeDtypeStruct((2, quarter, model), BF)] * 2,
+        compiler_params=vmem(24),
+        cost_estimate=taking(3),
+        name="push",
+    )(*operands, *after)
+
+
+def finish_kernel(
+    ids, vectors, tokens, arrived, mine, hidden_grad, sums, up_biases, totals, input_part, small
+):
+    first_grad = arrived[...].astype(F32) + mine[...].astype(F32)
+    hat, scale = normed_parts(tokens[...].astype(F32))
+    back = hidden_grad[...] + norm_back(first_grad, hat, scale, vectors[0:1, :])
+    input_part[...] = back.astype(BF)
+    small[...] = jnp.zeros_like(small)
+    small[0:4, :] = sums[...]
+    for slot, j in enumerate((1, 3, 0, 2)):
+        small[pl.ds(4 + jnp.bitwise_xor(ids[0], j), 1), :] = up_biases[slot]
+    small[pl.ds(8 + ids[0], 1), :] = totals[...]
+    small[12:13, :] = column_sums(first_grad * hat)
+    small[13:14, :] = column_sums(first_grad)
+
+
+def finish(ids, vectors, tokens, arrived, mine, hidden_grad, sums, up_biases, totals):
+    quarter, model = mine.shape
+    operands = [arrived, mine, hidden_grad, sums, up_biases, totals]
+    return pl.pallas_call(
+        finish_kernel,
+        grid_spec=pltpu.PrefetchScalarGridSpec(
+            num_scalar_prefetch=1,
+            grid=(1,),
+            in_specs=[
+                whole(vectors),
+                pl.BlockSpec((quarter, model), lambda j, ids: (ids[0], 0)),
+            ]
+            + [whole(a) for a in operands],
+            out_specs=[
+                pl.BlockSpec((quarter, model), lambda j, *_: (0, 0)),
+                pl.BlockSpec((16, model), lambda j, *_: (0, 0)),
+            ],
+        ),
+        out_shape=[
+            jax.ShapeDtypeStruct((quarter, model), BF),
+            jax.ShapeDtypeStruct((16, model), F32),
+        ],
+        compiler_params=vmem(32),
+        cost_estimate=taking(4),
+        name="finish",
+    )(ids, vectors, tokens, *operands)
+
+
+def ordered_kernel(ids, *refs):
+    *parts, out = refs
+    for j, part in enumerate(parts):
+
+        @pl.when(pl.program_id(0) == j)
+        def _(part=part):
+            out[...] = part[...].astype(out.dtype)
+
+
+def ordered(ids, which, parts, kind):
+    size, model = parts[0].shape
+    count = len(parts)
+    return pl.pallas_call(
+        ordered_kernel,
+        grid_spec=pltpu.PrefetchScalarGridSpec(
+            num_scalar_prefetch=1,
+            grid=(count,),
+            in_specs=[whole(a) for a in parts],
+            out_specs=pl.BlockSpec(
+                (size, model), lambda j, ids: (jnp.bitwise_xor(ids[which], j), 0)
+            ),
+        ),
+        out_shape=jax.ShapeDtypeStruct((count * size, model), kind),
+        compiler_params=vmem(24),
+        cost_estimate=taking(3),
+        name="ordered",
+    )(ids, *parts)
+
+
+def held_until(array, after):
+    return pl.pallas_call(
+        lambda *refs: None,
+        in_specs=[ANYWHERE] * (1 + len(after)),
+        out_specs=ANYWHERE,
+        out_shape=jax.ShapeDtypeStruct(array.shape, array.dtype),
+        input_output_aliases={0: 0},
+        name="held",
+    )(array, *after)
+
+
+def swap(array, flip, axis="mp"):
+    return lax.ppermute(array, axis, [(i, i ^ flip) for i in range(lax.axis_size(axis))])
+
+
+def upward(array, ranks):
+    return lax.ppermute(array, "seq", [(i, i + 1) for i in range(ranks - 1)])
+
+
+def downward(array, ranks):
+    return lax.ppermute(array, "seq", [(i + 1, i) for i in range(ranks - 1)])
+
+
+def spread_over_mp(part):
+    across = swap(part, 2)
+    return [part, swap(part, 1), across, swap(across, 1)]
+
+
+def body_resident(
+    inputs,
+    selection,
+    gain1,
+    shift1,
+    w_qkv,
+    b_qv,
+    w_score,
+    b_score,
+    w_out,
+    b_out,
+    gain2,
+    shift2,
+    w_up,
+    b_up,
+    w_down,
+    b_down,
+    cotangent,
+):
+    ranks = lax.axis_size("seq")
+    me, rank, side = lax.axis_index("mp"), lax.axis_index("seq"), lax.axis_index("dp")
+    ids = jnp.stack([me, rank, side]).astype(jnp.int32)
+    rows, model = inputs.shape[1:]
+    quarter = rows // 4
+    block = quarter // 2
+    total = ranks * rows
+    blocks = rows // KB
+    width = w_qkv.shape[2]
+    heads = width // HD
+
+    own = lax.dynamic_slice_in_dim(inputs[0], me * quarter, quarter, 0)
+    arriving = {}
+    for h in range(2):
+        part = own[h * block : (h + 1) * block]
+        for k in range(1, ranks):
+            part = upward(part, ranks)
+            arriving[k, h] = spread_over_mp(part)
+
+    b_high = b_up.astype(BF)
+    b_low = (b_up - b_high.astype(F32)).astype(BF)
+    out_rows = jnp.concatenate(
+        [w_out, b_high[None], b_low[None], jnp.zeros((14, model), BF)], axis=0
+    )
+    w_outs = spread_over_mp(out_rows)
+    first = swap(jnp.where(side == 0, w_up, w_down), 2)
+    second = swap(first, 1, "dp")
+    w_ups = [w_up, swap(w_up, 1), first, swap(first, 1)]
+    w_downs = [w_down, swap(w_down, 1), second, swap(second, 1)]
+
+    vectors = jnp.stack([gain1, shift1, b_out, gain2, shift2, b_down] + [gain1] * 2, axis=0)
+    lines = jnp.pad(
+        jnp.stack([jnp.pad(b_score, (width, WIDE - width - heads))[:width], b_qv[1], b_qv[0]]),
+        ((0, 5), (0, WIDE - width)),
+    )
+    lines = lax.dynamic_update_slice(lines, b_score[None], (0, width))
+    wide = lambda a: jnp.pad(a, ((0, 0), (0, WIDE - a.shape[1])))
+    wq, wv = wide(w_qkv[:, 0]), wide(w_qkv[:, 2])
+    wk = wide(jnp.concatenate([w_qkv[:, 1], w_score], axis=1))
+
+    last = [arriving[ranks - 1, h][0] for h in range(2)]
+    *buffers, qt = project_own(
+        ids, inputs[0], vectors, lines, (wk, wv, wq), width, total, block, last
+    )
+    for k in range(1, ranks - 1):
+        pieces = [arriving[k, h][j] for j in range(4) for h in range(2)]
+        buffers = project(
+            pieces, lambda j, k=k: 8 * k + j, vectors, lines, (wk, wv), buffers, [(first, second)[k - 1]]
+        )
+    for h in range(2):
+        buffers = project(
+            arriving[ranks - 1, h],
+            lambda j, h=h: 8 * (ranks - 1) + 2 * j + h,
+            vectors,
+            lines,
+            (wk, wv),
+            buffers,
+        )
+    first_in, ka, va, kt, vt = buffers
+
+    chosen = selection[0]
+    *mixed, norm = attend(ids, chosen, ka, vt, qt, blocks)
+
+    features = [mixed[0]] + [swap(mixed[j], j) for j in (1, 2, 3)]
+    *mixed_grads, output, hidden_grad, kept, sent, kept_out, sent_out, sums, up_biases = (
+        feed_forward(ids, vectors, inputs[0], cotangent[0], features, w_outs, w_ups, w_downs)
+    )
+    returned = [mixed_grads[0]] + [swap(mixed_grads[j], j) for j in (1, 2, 3)]
+
+    given, given_out = swap(sent, 1), swap(sent_out, 1)
+    part = 3 * model // 2
+    across = [kept[1, :part] + given[1, :part], kept[1, part:] + given[1, part:]]
+    across_out = kept_out[1] + given_out[1]
+    crossing = [swap(a, 2) for a in (*across, across_out)]
+
+    spread, query_grad, totals = attend_back(
+        ids, chosen, ka, va, kt, qt, norm, returned, blocks, (*across, across_out)
+    )
+
+    carried, crossed = None, []
+    for k in range(ranks - 1, -1, -1):
+        pushed, pushed_out = push(
+            spread,
+            (wk, wv, wq),
+            k,
+            quarter,
+            query_grad if k == 0 else None,
+            crossing[:1] if k == 2 else crossing[1:] if k == 0 else (),
+        )
+        arrived = swap(pushed_out, 1)
+        crossed.append(swap(pushed[1] + arrived[1], 2))
+        mine = pushed[0] + arrived[0] + crossed[-1]
+        if k > 0:
+            carried = downward(mine if carried is None else mine + carried, ranks)
+
+    key_value_grad = rows_inner(first_in, spread)
+    query_weight_grad = rows_inner(first_in[:rows], query_grad)
+    qkv_pack = jnp.concatenate(
+        [
+            key_value_grad[:, :WIDE],
+            key_value_grad[:, WIDE : WIDE + width],
+            query_weight_grad[:, :width],
+        ],
+        axis=1,
+    )
+    qkv_pack = qkv_pack.astype(BF)
+    half = model // 2
+    qkv_mine = lax.dynamic_slice_in_dim(qkv_pack, side * half, half, 0)
+    qkv_sent = lax.dynamic_slice_in_dim(qkv_pack, (1 - side) * half, half, 0)
+    qkv_mine = qkv_mine + swap(qkv_sent, 1, "dp")
+    for flip in (1, 2):
+        qkv_mine = qkv_mine + swap(qkv_mine, flip, "seq")
+    qkv_sum = ordered(ids, 2, [qkv_mine, swap(qkv_mine, 1, "dp")], F32)
+
+    dense = [
+        kept[0, :part] + given[0, :part] + crossing[0],
+        kept[0, part:] + given[0, part:] + crossing[1],
+        kept_out[0] + given_out[0] + crossing[2],
+    ]
+    dense = lax.psum(dense, ("dp", "seq"))
+    *dense, out_grad = [a.astype(F32) for a in dense]
+    dense = jnp.concatenate(dense, axis=0)
+
+    input_part, small = finish(
+        ids, vectors, inputs[0], carried, mine, hidden_grad, sums, up_biases, totals
+    )
+    output_parts = spread_over_mp(held_until(output, crossed))
+    input_grad = ordered(ids, 0, spread_over_mp(input_part), BF)
+    for axis, flips in (("mp", (1, 2)), ("dp", (1,)), ("seq", (1, 2))):
+        for flip in flips:
+            small = small + swap(small, flip, axis)
+    up_bias = lax.dynamic_slice_in_dim(small, 4 + me, 1, 0)[0]
+    biases = lax.dynamic_slice_in_dim(small, 8 + me, 1, 0)[0]
+    query_at, value_at = WIDE + width, WIDE
+    qkv_grad = jnp.stack(
+        [qkv_sum[:, query_at:], qkv_sum[:, :width], qkv_sum[:, value_at:query_at]], axis=1
+    )
+    qv_bias_grad = jnp.stack(
+        [biases[2 * WIDE : 2 * WIDE + width], biases[WIDE : WIDE + width]], axis=0
+    )
+    return (
+        ordered(ids, 0, output_parts, BF)[None],
+        input_grad[None],
+        small[12],
+        small[13],
+        qkv_grad,
+        qv_bias_grad,
+        qkv_sum[:, width : width + heads],
+        biases[width : width + heads],
+        out_grad,
+        small[2],
+        small[0],
+        small[1],
+        dense[:model],
+        up_bias,
+        dense[model:],
+        small[3],
+    )
+
+
+RESIDENT_TOKENS = 8192
+
+
 def solution(mesh):
+    def body(*args):
+        tokens = args[0].shape[1] * mesh.shape["seq"]
+        resident = mesh.shape["mp"] == 4 and mesh.shape["dp"] == 2
+        resident = resident and mesh.shape["seq"] == 4 and tokens <= RESIDENT_TOKENS
+        return (body_resident if resident else body_general)(*args)
+
     return jax.shard_map(
         body,
         mesh=mesh,

time: 1250 us -> 510 us (0.41)
  waiting for transfers between devices: 766 us -> 191 us
  Pallas kernels: 0 us -> 143 us
  matrix products: 138 us -> 12.7 us
  other arithmetic: 152 us -> 33.7 us
  local copies, waits for them, and re-layouts: 110 us -> 32.6 us
  starting transfers between devices: 0.99 us -> 72.7 us
  blocking collectives: 57.9 us -> 0 us
    psum x4 -> x1, waiting for transfers between devices: 514 us -> 44 us  [body_resident(): dense = lax.psum(dense, ('dp', 'seq'))]
    reduce_scatter x2 -> x0, waiting for transfers between devices: 159 us -> none  [the longest x1 112 us: body(): lax.psum_scatter(value_spread.reshape(total_blocks * KB, local_width), 's...]
    ppermute x0 -> x70, waiting for transfers between devices: none -> 147 us  [the longest x61 108 us: swap(): lax.ppermute(array, axis, [(i, i ^ flip) for i in range(lax.axis_size(axi...]
    pallas_call x0 -> x17, Pallas kernels: none -> 143 us  [the longest x1 40.3 us: attend_back(): pl.pallas_call(ordered_after(functools.partial(attend_back_kernel, blocks...]
    dot_general x16 -> x0, matrix products: 115 us -> none  [the longest x1 17.1 us: block_scores(): jnp.einsum('gihd,gcjhd->ghicj', query_blocks, key_cand, preferred_element...]
    all_gather x2 -> x0, waiting for transfers between devices: 92.8 us -> none  [the longest x1 57.8 us: body(): lax.all_gather(key_rows, 'seq', axis=0, tiled=True)]
    ppermute x0 -> x70, starting transfers between devices: none -> 72.7 us  [the longest x61 43.6 us: swap(): lax.ppermute(array, axis, [(i, i ^ flip) for i in range(lax.axis_size(axi...]
    scatter-add x3 -> x0, other arithmetic: 59.3 us -> none  [the longest x2 48.3 us: body(): jnp.zeros((total_blocks, KB, local_heads, HD), jnp.float32).at[picked]]
  transfers between devices with their start and end apart: 9 -> 71, of which waited for: 8 -> 23; matrix products, arithmetic and copies ran while one was open for 17% -> 13% of each run, Pallas kernels for 0% -> 22%
where the time goes in v2:
time: 510 us; the launch traced here: 502 us
  waiting for transfers between devices  191 us (37%)
  Pallas kernels  143 us (28%)
  starting transfers between devices  72.7 us (14%)
  other arithmetic  33.7 us (7%)
  local copies, waits for them, and re-layouts  32.6 us (6%)
  between operations  15.7 us (3%)
  matrix products  12.7 us (2%)
    ppermute x61, waiting for transfers between devices, swap(): lax.ppermute(array, axis, [(i, i ^ flip) for i in range(lax.axis_size(axi...  108 us
    psum x1, waiting for transfers between devices, body_resident(): dense = lax.psum(dense, ('dp', 'seq'))  44 us
    ppermute x61, starting transfers between devices, swap(): lax.ppermute(array, axis, [(i, i ^ flip) for i in range(lax.axis_size(axi...  43.6 us
    pallas_call x1, Pallas kernels, attend_back(): pl.pallas_call(ordered_after(functools.partial(attend_back_kernel, blocks...  40.3 us
    pallas_call x1, Pallas kernels, feed_forward(): pl.pallas_call(functools.partial(feed_forward_kernel, order), grid_spec=p...  30.8 us
    ppermute x3, waiting for transfers between devices, downward(): return lax.ppermute(array, 'seq', [(i + 1, i) for i in range(ranks - 1)])  26.1 us
    pallas_call x4, Pallas kernels, project(): pl.pallas_call(ordered_after(functools.partial(project_kernel, count), le...  26.1 us
    ppermute x6, starting transfers between devices, upward(): return lax.ppermute(array, 'seq', [(i, i + 1) for i in range(ranks - 1)])  24.9 us
  transfers between devices with their start and end apart: 71, of which 23 were waited for; matrix products, arithmetic and copies ran while one was open for 13% of the time, Pallas kernels for 22%

profile of v2, /device:TPU:0, one launch (start us, length us, event | category | flops | bytes accessed | tf_op | source)
XLA Modules:
  0.0 501.9 jit_solution(13736329099308975428)
XLA Ops:
  9.3 5.7 %collective-permute-start = (bf16[256,768]{1,0:T(8,128)(2,1)S(1)}, bf16[256,768]{1,0:T(8,128)(2,1)}, u32[]{:S(2)}, u32[]{:S(2)}) collective-permute-start(bf16[256,768]{1,0:T(8,128)(2,1)S(1)} %get-tuple-element.157), channel_id=1, source_target_pairs={{0,4},{4,8},{8,12},{1,5},{5,9},{9,13},{2,6},{6,10},{10,14},{3,7},{... | collective-permute-start | bytes 1179656 | tf_op jit(solution)/shard_map/ppermute | solution.py:1007
  23.7 4.5 collective-permute-start.1
  28.3 4.0 collective-permute-done.6.refs_4_
  32.2 5.0 %collective-permute-start.7 = (bf16[256,768]{1,0:T(8,128)(2,1)S(1)}, bf16[256,768]{1,0:T(8,128)(2,1)}, u32[]{:S(2)}, u32[]{:S(2)}) collective-permute-start(bf16[256,768]{1,0:T(8,128)(2,1)S(1)} %collective-permute-done.6.refs_4_), channel_id=1, source_target_pairs={{0,4},{4,8},{8,12},{1,5},{5,9},{9,13},{2,6},{6,10},{10,14},{3,7},{... | collective-permute-start | bytes 1179656 | tf_op jit(solution)/shard_map/ppermute | solution.py:1007
  42.7 5.1 %collective-permute-done.7.refs_4_ = bf16[256,768]{1,0:T(8,128)(2,1)} collective-permute-done((bf16[256,768]{1,0:T(8,128)(2,1)S(1)}, bf16[256,768]{1,0:T(8,128)(2,1)}, u32[]{:S(2)}, u32[]{:S(2)}) %collective-permute-start.7) | collective-permute-done | bytes 393248 | tf_op jit(solution)/shard_map/ppermute | solution.py:1007
  47.8 8.8 %collective-permute-done.20.refs_8_ = bf16[256,768]{1,0:T(8,128)(2,1)} collective-permute-done((bf16[256,768]{1,0:T(8,128)(2,1)S(1)}, bf16[256,768]{1,0:T(8,128)(2,1)}, u32[]{:S(2)}, u32[]{:S(2)}) %collective-permute-start.20) | collective-permute-done | bytes 393248 | tf_op jit(solution)/shard_map/ppermute | solution.py:1003
  56.6 3.5 collective-permute-start.2
  63.3 3.5 collective-permute-start.8
  85.0 7.7 %project_own.1 = (bf16[8192,768]{1,0:T(8,128)(2,1)}, bf16[8192,256]{1,0:T(8,128)(2,1)S(1)}, bf16[8192,256]{1,0:T(8,128)(2,1)S(1)}, bf16[192,8192]{1,0:T(8,128)(2...) custom-call(s32[3]{0:T(128)S(1)} %pad_add_fusion.refs_0_.ids, bf16[2048,768]{1,0:T(8,128)(2,1)S(1)} %bitcast.77, ...), custom_call_target="tpu_custom_call" | custom-call | flops 8800000000 | bytes 800000 | tf_op jit(solution)/shard_map/project_own/pallas_call | solution.py:409
  98.9 8.0 %project.4 = (bf16[8192,768]{1,0:T(8,128)(2,1)}, bf16[8192,256]{1,0:T(8,128)(2,1)S(1)}, bf16[8192,256]{1,0:T(8,128)(2,1)S(1)}, bf16[192,8192]{1,0:T(8,128)(2,1)S(1)}, bf16[192,8192]{1,0:T(8,128)(2,1)S(1)}) custom-call(f32[8,768]{1,0:T(8,128)S(1)} %stack.68.refs_2_.refs_0_.vectors, ...), custom_call_target="tpu_custom_call", output_to_operand_aliasing={{0}: (12, {}), {1}: (13, {}), {2}: (14, {}), {3}: (15, {}),... | custom-call | flops 8800000000 | bytes 800000 | tf_op jit(solution)/shard_map/project/pallas_call | solution.py:440
  109.5 8.7 %project.5 = (bf16[8192,768]{1,0:T(8,128)(2,1)}, bf16[8192,256]{1,0:T(8,128)(2,1)S(1)}, bf16[8192,256]{1,0:T(8,128)(2,1)S(1)}, bf16[192,8192]{1,0:T(8,128)(2,1)S(1)}, bf16[192,8192]{1,0:T(8,128)(2,1)S(1)}) custom-call(f32[8,768]{1,0:T(8,128)S(1)} %stack.68.refs_2_.refs_0_.vectors, ...), custom_call_target="tpu_custom_call", output_to_operand_aliasing={{0}: (12, {}), {1}: (13, {}), {2}: (14, {}), {3}: (15, {}),... | custom-call | flops 8800000000 | bytes 800000 | tf_op jit(solution)/shard_map/project/pallas_call | solution.py:440
  118.8 6.1 %collective-permute-done.4.refs_6_ = bf16[256,768]{1,0:T(8,128)(2,1)S(1)} collective-permute-done((bf16[256,768]{1,0:T(8,128)(2,1)S(1)}, bf16[256,768]{1,0:T(8,128)(2,1)S(1)}, u32[]{:S(2)}, u32[]{:S(2)}) %collective-permute-start.4) | collective-permute-done | bytes 393248 | tf_op jit(solution)/shard_map/ppermute | solution.py:1003
  125.4 4.7 project.6
  130.8 4.7 project.7
  136.4 14.9 %attend.1 = (bf16[192,512]{1,0:T(8,128)(2,1)S(1)}, bf16[192,512]{1,0:T(8,128)(2,1)S(1)}, bf16[192,512]{1,0:T(8,128)(2,1)S(1)}, bf16[192,512]{1,0:T(8,128)(2,1)S(1)}, f32[16,1,384]{2,1,0:T(1,128)S(1)}) custom-call(s32[3]{0:T(128)S(1)} %pad_add_fusion.refs_0_.ids, s32[16,4]{1,0:T(8,128)S(1)} %copy.58.chosen.refs_1_, ...), custom_call_target="tpu_custom_call" | custom-call | flops 15399999488 | bytes 1400000 | tf_op jit(solution)/shard_map/attend/pallas_call | solution.py:560
  154.0 6.2 %collective-permute-done.27.refs_2_ = bf16[192,512]{1,0:T(8,128)(2,1)S(1)} collective-permute-done((bf16[192,512]{1,0:T(8,128)(2,1)S(1)}, bf16[192,512]{1,0:T(8,128)(2,1)S(1)}, u32[]{:S(2)}, u32[]{:S(2)}) %collective-permute-start.27) | collective-permute-done | bytes 196640 | tf_op jit(solution)/shard_map/ppermute | solution.py:1003
  163.4 30.8 %feed_forward.1 = (bf16[192,512]{1,0:T(8,128)(2,1)}, bf16[192,512]{1,0:T(8,128)(2,1)}, bf16[192,512]{1,0:T(8,128)(2,1)}, bf16[192,512]{1,0:T(8,128)(2,1)}, bf16[...) custom-call(s32[3]{0:T(128)} %copy-done.13, ...), custom_call_target="tpu_custom_call" | custom-call | flops 32999999488 | bytes 3000000 | tf_op jit(solution)/shard_map/feed_forward/pallas_call | solution.py:844
  197.0 5.6 %collective-permute-done.40 = bf16[2,192,768]{2,1,0:T(8,128)(2,1)S(1)} collective-permute-done((bf16[2,192,768]{2,1,0:T(8,128)(2,1)}, bf16[2,192,768]{2,1,0:T(8,128)(2,1)S(1)}, u32[]{:S(2)}, u32[]{:S(2)}) %collective-permute-start.40) | collective-permute-done | bytes 589856 | tf_op jit(solution)/shard_map/ppermute | solution.py:1003
  210.9 40.3 %attend_back.1 = (bf16[8192,512]{1,0:T(8,128)(2,1)}, bf16[2048,256]{1,0:T(8,128)(2,1)}, f32[1,768]{1,0:T(1,128)}) custom-call(s32[3]{0:T(128)} %copy-done.13, s32[16,4]{1,0:T(8,128)} %copy-done.12, bf16[8192,256]{1,0:T(8,128)(2,1)} %copy-done, bf16[8192,256]{1,0:T(8,128)(2,1)} %copy-done.1, bf16[192,8192]{1,0:T(8,128)(2,1)} %copy-done.2, ...), custom_call_target="tpu_custom_call" | custom-call | flops 39600001024 | bytes 3600000 | tf_op jit(solution)/shard_map/attend_back/pallas_call | solution.py:675
  258.0 9.8 %fusion.34 = bf16[768,512]{1,0:T(8,128)(2,1)S(1)} fusion(bf16[8192,768]{1,0:T(8,128)(2,1)} %get-tuple-element.127, bf16[8192,512]{1,0:T(8,128)(2,1)S(1)} %copy-done.23), kind=kOutput, calls=%fused_computation.76 | convolution fusion | flops 6442450944 | bytes 21757952 | tf_op jit(solution)/shard_map/dot_general | solution.py:32
  282.3 6.1 %collective-permute-done.66 = bf16[384,640]{1,0:T(8,128)(2,1)S(1)} collective-permute-done((bf16[384,640]{1,0:T(8,128)(2,1)S(1)}, bf16[384,640]{1,0:T(8,128)(2,1)S(1)}, u32[]{:S(2)}, u32[]{:S(2)}) %collective-permute-start.66) | collective-permute-done | bytes 491552 | tf_op jit(solution)/shard_map/ppermute | solution.py:1003
  289.7 7.3 %collective-permute-done.42.refs_1_ = bf16[512,768]{1,0:T(8,128)(2,1)S(1)} collective-permute-done((bf16[512,768]{1,0:T(8,128)(2,1)S(1)}, bf16[512,768]{1,0:T(8,128)(2,1)S(1)}, u32[]{:S(2)}, u32[]{:S(2)}) %collective-permute-start.42) | collective-permute-done | bytes 786464 | tf_op jit(solution)/shard_map/ppermute | solution.py:1003
  300.2 9.5 %collective-permute-done.48.refs_5_ = bf16[384,768]{1,0:T(8,128)(2,1)S(1)} collective-permute-done((bf16[384,768]{1,0:T(8,128)(2,1)S(1)}, bf16[384,768]{1,0:T(8,128)(2,1)S(1)}, u32[]{:S(2)}, u32[]{:S(2)}) %collective-permute-start.48) | collective-permute-done | bytes 589856 | tf_op jit(solution)/shard_map/ppermute | solution.py:1003
  309.7 4.5 push.7
  319.5 7.0 %collective-permute-done.45.refs_2_ = bf16[512,768]{1,0:T(8,128)(2,1)S(1)} collective-permute-done((bf16[512,768]{1,0:T(8,128)(2,1)S(1)}, bf16[512,768]{1,0:T(8,128)(2,1)S(1)}, u32[]{:S(2)}, u32[]{:S(2)}) %collective-permute-start.45) | collective-permute-done | bytes 786464 | tf_op jit(solution)/shard_map/ppermute | solution.py:1003
  339.4 4.1 collective-permute-done.47.refs_3_
  343.5 21.1 %collective-permute-done.56 = bf16[512,768]{1,0:T(8,128)(2,1)} collective-permute-done((bf16[512,768]{1,0:T(8,128)(2,1)}, bf16[512,768]{1,0:T(8,128)(2,1)}, u32[]{:S(2)}, u32[]{:S(2)}) %collective-permute-start.56) | collective-permute-done | bytes 786464 | tf_op jit(solution)/shard_map/ppermute | solution.py:1011
  370.2 29.7 %collective-permute-done.68 = bf16[384,640]{1,0:T(8,128)(2,1)} collective-permute-done((bf16[384,640]{1,0:T(8,128)(2,1)}, bf16[384,640]{1,0:T(8,128)(2,1)}, u32[]{:S(2)}, u32[]{:S(2)}) %collective-permute-start.68) | collective-permute-done | bytes 491552 | tf_op jit(solution)/shard_map/ppermute | solution.py:1003
  402.8 4.3 collective-permute-done.57.arrived
  418.3 7.8 %collective-permute-done.62 = f32[16,768]{1,0:T(8,128)S(1)} collective-permute-done((f32[16,768]{1,0:T(8,128)S(1)}, f32[16,768]{1,0:T(8,128)S(1)}, u32[]{:S(2)}, u32[]{:S(2)}) %collective-permute-start.62) | collective-permute-done | bytes 49184 | tf_op jit(solution)/shard_map/ppermute | solution.py:1003
  433.0 44.0 %all-reduce.7.cloned.1.call-done = (bf16[192,768]{1,0:T(8,128)(2,1)}, bf16[1152,768]{1,0:T(8,128)(2,1)}, bf16[384,768]{1,0:T(8,128)(2,1)}) async-done(((bf16[192,768]{1,0:T(8,128)(2,1)}, bf16[1152,768]{1,0:T(8,128)(2,1)}, bf16[384,768]{1,0:T(8,128)(2,1)}), (bf16[192,768]{1,0:T(8,128)(2,1)}, bf16[1152,768]{1,0:T(8,128)(2,1)}, bf16[384,768]{1,0:T(8,128)(2,1)})) %all-reduce.7.cloned.1.call-update) | async-done | bytes 2654224 | tf_op jit(solution)/shard_map/psum | solution.py:1157
  485.6 4.3 ordered.3
  (340 shorter events, 149.1 us)
Async XLA Ops:
  7.2 469.9 %all-reduce.7.cloned.1.call-start = ((), (), s32[]{:S(2)}) async-start(), calls=%async_computation | async-start | bytes 5308416 | tf_op jit(solution)/shard_map/psum | solution.py:1157
  18.9 61.5 %collective-permute-start.24 = (bf16[768,768]{1,0:T(8,128)(2,1)}, bf16[768,768]{1,0:T(8,128)(2,1)S(1)}, u32[]{:S(2)}, u32[]{:S(2)}) collective-permute-start(bf16[768,768]{1,0:T(8,128)(2,1)} %broadcast_select_fusion), channel_id=1, source_target_pairs={{0,2},{1,3},{2,0},{3,1},{4,6},{5,7},{6,4},{7,5},{8,10},{9,11},{10,... | collective-permute-start | bytes 3538952 | tf_op jit(solution)/shard_map/ppermute | solution.py:1003
  38.8 24.5 %collective-permute-start.21 = (bf16[256,768]{1,0:T(8,128)(2,1)}, bf16[256,768]{1,0:T(8,128)(2,1)}, u32[]{:S(2)}, u32[]{:S(2)}) collective-permute-start(bf16[256,768]{1,0:T(8,128)(2,1)} %collective-permute-done.refs_5_), channel_id=1, source_target_pairs={{0,2},{1,3},{2,0},{3,1},{4,6},{5,7},{6,4},{7,5},{8,10},{9,11},{10,... | collective-permute-start | bytes 1179656 | tf_op jit(solution)/shard_map/ppermute | solution.py:1003
  40.6 26.1 %collective-permute-start.18 = (bf16[256,768]{1,0:T(8,128)(2,1)S(1)}, bf16[256,768]{1,0:T(8,128)(2,1)S(1)}, u32[]{:S(2)}, u32[]{:S(2)}) collective-permute-start(bf16[256,768]{1,0:T(8,128)(2,1)S(1)} %collective-permute-done.6.refs_4_), channel_id=1, source_target_pairs={{0,1},{1,0},{2,3},{3,2},{4,5},{5,4},{6,7},{7,6},{8,9},{9,8},{10,11... | collective-permute-start | bytes 1179656 | tf_op jit(solution)/shard_map/ppermute | solution.py:1003
  47.8 29.9 %collective-permute-start.19 = (bf16[256,768]{1,0:T(8,128)(2,1)}, bf16[256,768]{1,0:T(8,128)(2,1)}, u32[]{:S(2)}, u32[]{:S(2)}) collective-permute-start(bf16[256,768]{1,0:T(8,128)(2,1)} %collective-permute-done.refs_5_), channel_id=1, source_target_pairs={{0,1},{1,0},{2,3},{3,2},{4,5},{5,4},{6,7},{7,6},{8,9},{9,8},{10,11... | collective-permute-start | bytes 1179656 | tf_op jit(solution)/shard_map/ppermute | solution.py:1003
  56.6 22.7 %collective-permute-start.2 = (bf16[256,768]{1,0:T(8,128)(2,1)S(1)}, bf16[256,768]{1,0:T(8,128)(2,1)S(1)}, u32[]{:S(2)}, u32[]{:S(2)}) collective-permute-start(bf16[256,768]{1,0:T(8,128)(2,1)S(1)} %collective-permute-done.1.refs_5_), channel_id=1, source_target_pairs={{0,4},{4,8},{8,12},{1,5},{5,9},{9,13},{2,6},{6,10},{10,14},{3,7},{... | collective-permute-start | bytes 1179656 | tf_op jit(solution)/shard_map/ppermute | solution.py:1007
  80.4 29.1 %collective-permute-start.25 = (bf16[768,768]{1,0:T(8,128)(2,1)S(1)}, bf16[768,768]{1,0:T(8,128)(2,1)}, u32[]{:S(2)}, u32[]{:S(2)}) collective-permute-start(bf16[768,768]{1,0:T(8,128)(2,1)S(1)} %collective-permute-done.24.refs_17_.refs_10_), channel_id=1, source_target_pairs={{0,16},{16,0},{1,17},{17,1},{2,18},{18,2},{3,19},{19,3},{4,20},{20... | collective-permute-start | bytes 3538952 | tf_op jit(solution)/shard_map/ppermute | solution.py:1003
  106.9 23.2 %collective-permute-start.30 = (bf16[208,768]{1,0:T(8,128)(2,1)S(1)}, bf16[208,768]{1,0:T(8,128)(2,1)S(1)}, u32[]{:S(2)}, u32[]{:S(2)}) collective-permute-start(bf16[208,768]{1,0:T(8,128)(2,1)S(1)} %maximum_maximum_fusion.refs_4_), channel_id=1, source_target_pairs={{0,2},{1,3},{2,0},{3,1},{4,6},{5,7},{6,4},{7,5},{8,10},{9,11},{10,... | collective-permute-start | bytes 958472 | tf_op jit(solution)/shard_map/ppermute | solution.py:1003
  108.5 27.1 %collective-permute-start.29 = (bf16[208,768]{1,0:T(8,128)(2,1)S(1)}, bf16[208,768]{1,0:T(8,128)(2,1)S(1)}, u32[]{:S(2)}, u32[]{:S(2)}) collective-permute-start(bf16[208,768]{1,0:T(8,128)(2,1)S(1)} %maximum_maximum_fusion.refs_4_), channel_id=1, source_target_pairs={{0,1},{1,0},{2,3},{3,2},{4,5},{5,4},{6,7},{7,6},{8,9},{9,8},{10,11... | collective-permute-start | bytes 958472 | tf_op jit(solution)/shard_map/ppermute | solution.py:1003
  118.3 34.2 %collective-permute-start.32 = (bf16[768,768]{1,0:T(8,128)(2,1)S(1)}, bf16[768,768]{1,0:T(8,128)(2,1)}, u32[]{:S(2)}, u32[]{:S(2)}) collective-permute-start(bf16[768,768]{1,0:T(8,128)(2,1)S(1)} %copy-done.40), channel_id=1, source_target_pairs={{0,1},{1,0},{2,3},{3,2},{4,5},{5,4},{6,7},{7,6},{8,9},{9,8},{10,11... | collective-permute-start | bytes 3538952 | tf_op jit(solution)/shard_map/ppermute | solution.py:1003
  130.1 23.9 %collective-permute-start.34 = (bf16[768,768]{1,0:T(8,128)(2,1)}, bf16[768,768]{1,0:T(8,128)(2,1)S(1)}, u32[]{:S(2)}, u32[]{:S(2)}) collective-permute-start(bf16[768,768]{1,0:T(8,128)(2,1)} %refs_12_.1), channel_id=1, source_target_pairs={{0,1},{1,0},{2,3},{3,2},{4,5},{5,4},{6,7},{7,6},{8,9},{9,8},{10,11... | collective-permute-start | bytes 3538952 | tf_op jit(solution)/shard_map/ppermute | solution.py:1003
  130.2 21.8 %collective-permute-start.31 = (bf16[208,768]{1,0:T(8,128)(2,1)S(1)}, bf16[208,768]{1,0:T(8,128)(2,1)S(1)}, u32[]{:S(2)}, u32[]{:S(2)}) collective-permute-start(bf16[208,768]{1,0:T(8,128)(2,1)S(1)} %collective-permute-done.30.refs_6_), channel_id=1, source_target_pairs={{0,1},{1,0},{2,3},{3,2},{4,5},{5,4},{6,7},{7,6},{8,9},{9,8},{10,11... | collective-permute-start | bytes 958472 | tf_op jit(solution)/shard_map/ppermute | solution.py:1003
  130.7 23.3 %collective-permute-start.33 = (bf16[768,768]{1,0:T(8,128)(2,1)S(1)}, bf16[768,768]{1,0:T(8,128)(2,1)S(1)}, u32[]{:S(2)}, u32[]{:S(2)}) collective-permute-start(bf16[768,768]{1,0:T(8,128)(2,1)S(1)} %collective-permute-done.24.refs_17_.refs_10_), channel_id=1, source_target_pairs={{0,1},{1,0},{2,3},{3,2},{4,5},{5,4},{6,7},{7,6},{8,9},{9,8},{10,11... | collective-permute-start | bytes 3538952 | tf_op jit(solution)/shard_map/ppermute | solution.py:1003
  135.6 27.1 %collective-permute-start.35 = (bf16[768,768]{1,0:T(8,128)(2,1)}, bf16[768,768]{1,0:T(8,128)(2,1)}, u32[]{:S(2)}, u32[]{:S(2)}) collective-permute-start(bf16[768,768]{1,0:T(8,128)(2,1)} %collective-permute-done.25.refs_17_.refs_14_), channel_id=1, source_target_pairs={{0,1},{1,0},{2,3},{3,2},{4,5},{5,4},{6,7},{7,6},{8,9},{9,8},{10,11... | collective-permute-start | bytes 3538952 | tf_op jit(solution)/shard_map/ppermute | solution.py:1003
  203.5 77.4 %collective-permute-start.49 = (bf16[192,768]{1,0:T(8,128)(2,1)S(1)}, bf16[192,768]{1,0:T(8,128)(2,1)S(1)}, u32[]{:S(2)}, u32[]{:S(2)}) collective-permute-start(bf16[192,768]{1,0:T(8,128)(2,1)S(1)} %fusion.30.refs_13_), channel_id=1, source_target_pairs={{0,2},{1,3},{2,0},{3,1},{4,6},{5,7},{6,4},{7,5},{8,10},{9,11},{10,... | collective-permute-start | bytes 884744 | tf_op jit(solution)/shard_map/ppermute | solution.py:1003
  207.3 60.4 %collective-permute-start.43 = (bf16[1152,768]{1,0:T(8,128)(2,1)S(1)}, bf16[1152,768]{1,0:T(8,128)(2,1)S(1)}, u32[]{:S(2)}, u32[]{:S(2)}) collective-permute-start(bf16[1152,768]{1,0:T(8,128)(2,1)S(1)} %fusion.4.refs_11_), channel_id=1, source_target_pairs={{0,2},{1,3},{2,0},{3,1},{4,6},{5,7},{6,4},{7,5},{8,10},{9,11},{10,... | collective-permute-start | bytes 5308424 | tf_op jit(solution)/shard_map/ppermute | solution.py:1003
  270.5 27.9 %collective-permute-start.44 = (bf16[2,512,768]{2,1,0:T(8,128)(2,1)S(1)}, bf16[2,512,768]{2,1,0:T(8,128)(2,1)S(1)}, u32[]{:S(2)}, u32[]{:S(2)}) collective-permute-start(bf16[2,512,768]{2,1,0:T(8,128)(2,1)S(1)} %get-tuple-element.115), channel_id=1, source_target_pairs={{0,1},{1,0},{2,3},{3,2},{4,5},{5,4},{6,7},{7,6},{8,9},{9,8},{10,11... | collective-permute-start | bytes 4718600 | tf_op jit(solution)/shard_map/ppermute | solution.py:1003
  280.9 35.3 %collective-permute-start.46 = (bf16[2,512,768]{2,1,0:T(8,128)(2,1)S(1)}, bf16[2,512,768]{2,1,0:T(8,128)(2,1)S(1)}, u32[]{:S(2)}, u32[]{:S(2)}) collective-permute-start(bf16[2,512,768]{2,1,0:T(8,128)(2,1)S(1)} %get-tuple-element.117), channel_id=1, source_target_pairs={{0,1},{1,0},{2,3},{3,2},{4,5},{5,4},{6,7},{7,6},{8,9},{9,8},{10,11... | collective-permute-start | bytes 4718600 | tf_op jit(solution)/shard_map/ppermute | solution.py:1003
  281.8 27.9 %collective-permute-start.48 = (bf16[384,768]{1,0:T(8,128)(2,1)S(1)}, bf16[384,768]{1,0:T(8,128)(2,1)S(1)}, u32[]{:S(2)}, u32[]{:S(2)}) collective-permute-start(bf16[384,768]{1,0:T(8,128)(2,1)S(1)} %copy-done.42), channel_id=1, source_target_pairs={{0,2},{1,3},{2,0},{3,1},{4,6},{5,7},{6,4},{7,5},{8,10},{9,11},{10,... | collective-permute-start | bytes 1769480 | tf_op jit(solution)/shard_map/ppermute | solution.py:1003
  289.4 45.5 %collective-permute-start.67 = (bf16[384,640]{1,0:T(8,128)(2,1)}, bf16[384,640]{1,0:T(8,128)(2,1)}, u32[]{:S(2)}, u32[]{:S(2)}) collective-permute-start(bf16[384,640]{1,0:T(8,128)(2,1)} %fusion.26), channel_id=1, source_target_pairs={{0,4},{4,0},{8,12},{12,8},{1,5},{5,1},{9,13},{13,9},{2,6},{6,2},{1... | collective-permute-start | bytes 1474568 | tf_op jit(solution)/shard_map/ppermute | solution.py:1003
  297.2 22.3 %collective-permute-start.55 = (bf16[512,768]{1,0:T(8,128)(2,1)S(1)}, bf16[512,768]{1,0:T(8,128)(2,1)S(1)}, u32[]{:S(2)}, u32[]{:S(2)}) collective-permute-start(bf16[512,768]{1,0:T(8,128)(2,1)S(1)} %fusion.8), channel_id=1, source_target_pairs={{4,0},{8,4},{12,8},{5,1},{9,5},{13,9},{6,2},{10,6},{14,10},{7,3},{... | collective-permute-start | bytes 2359304 | tf_op jit(solution)/shard_map/ppermute | solution.py:1011
  298.6 27.9 %collective-permute-start.45 = (bf16[512,768]{1,0:T(8,128)(2,1)S(1)}, bf16[512,768]{1,0:T(8,128)(2,1)S(1)}, u32[]{:S(2)}, u32[]{:S(2)}) collective-permute-start(bf16[512,768]{1,0:T(8,128)(2,1)S(1)} %fusion.17), channel_id=1, source_target_pairs={{0,2},{1,3},{2,0},{3,1},{4,6},{5,7},{6,4},{7,5},{8,10},{9,11},{10,... | collective-permute-start | bytes 2359304 | tf_op jit(solution)/shard_map/ppermute | solution.py:1003
  317.2 26.3 %collective-permute-start.47 = (bf16[512,768]{1,0:T(8,128)(2,1)}, bf16[512,768]{1,0:T(8,128)(2,1)}, u32[]{:S(2)}, u32[]{:S(2)}) collective-permute-start(bf16[512,768]{1,0:T(8,128)(2,1)} %fusion.16), channel_id=1, source_target_pairs={{0,2},{1,3},{2,0},{3,1},{4,6},{5,7},{6,4},{7,5},{8,10},{9,11},{10,... | collective-permute-start | bytes 2359304 | tf_op jit(solution)/shard_map/ppermute | solution.py:1003
  327.7 36.9 %collective-permute-start.56 = (bf16[512,768]{1,0:T(8,128)(2,1)}, bf16[512,768]{1,0:T(8,128)(2,1)}, u32[]{:S(2)}, u32[]{:S(2)}) collective-permute-start(bf16[512,768]{1,0:T(8,128)(2,1)} %fusion.11), channel_id=1, source_target_pairs={{4,0},{8,4},{12,8},{5,1},{9,5},{13,9},{6,2},{10,6},{14,10},{7,3},{... | collective-permute-start | bytes 2359304 | tf_op jit(solution)/shard_map/ppermute | solution.py:1011
  333.3 35.2 %collective-permute-start.51 = (bf16[512,768]{1,0:T(8,128)(2,1)S(1)}, bf16[512,768]{1,0:T(8,128)(2,1)}, u32[]{:S(2)}, u32[]{:S(2)}) collective-permute-start(bf16[512,768]{1,0:T(8,128)(2,1)S(1)} %fusion.15), channel_id=1, source_target_pairs={{0,2},{1,3},{2,0},{3,1},{4,6},{5,7},{6,4},{7,5},{8,10},{9,11},{10,... | collective-permute-start | bytes 2359304 | tf_op jit(solution)/shard_map/ppermute | solution.py:1003
  337.0 62.8 %collective-permute-start.68 = (bf16[384,640]{1,0:T(8,128)(2,1)}, bf16[384,640]{1,0:T(8,128)(2,1)}, u32[]{:S(2)}, u32[]{:S(2)}) collective-permute-start(bf16[384,640]{1,0:T(8,128)(2,1)} %add.202), channel_id=1, source_target_pairs={{0,8},{4,12},{8,0},{12,4},{1,9},{5,13},{9,1},{13,5},{2,10},{6,14},... | collective-permute-start | bytes 1474568 | tf_op jit(solution)/shard_map/ppermute | solution.py:1003
  367.0 40.0 %collective-permute-start.57 = (bf16[512,768]{1,0:T(8,128)(2,1)}, bf16[512,768]{1,0:T(8,128)(2,1)S(1)}, u32[]{:S(2)}, u32[]{:S(2)}) collective-permute-start(bf16[512,768]{1,0:T(8,128)(2,1)} %fusion.14), channel_id=1, source_target_pairs={{4,0},{8,4},{12,8},{5,1},{9,5},{13,9},{6,2},{10,6},{14,10},{7,3},{... | collective-permute-start | bytes 2359304 | tf_op jit(solution)/shard_map/ppermute | solution.py:1011
  368.6 46.1 %collective-permute-start.53 = (bf16[512,768]{1,0:T(8,128)(2,1)}, bf16[512,768]{1,0:T(8,128)(2,1)}, u32[]{:S(2)}, u32[]{:S(2)}) collective-permute-start(bf16[512,768]{1,0:T(8,128)(2,1)} %held.1.refs_0_), channel_id=1, source_target_pairs={{0,2},{1,3},{2,0},{3,1},{4,6},{5,7},{6,4},{7,5},{8,10},{9,11},{10,... | collective-permute-start | bytes 2359304 | tf_op jit(solution)/shard_map/ppermute | solution.py:1003
  413.0 66.6 %collective-permute-start.59 = (bf16[512,768]{1,0:T(8,128)(2,1)S(1)}, bf16[512,768]{1,0:T(8,128)(2,1)S(1)}, u32[]{:S(2)}, u32[]{:S(2)}) collective-permute-start(bf16[512,768]{1,0:T(8,128)(2,1)S(1)} %get-tuple-element.125.refs_0_), channel_id=1, source_target_pairs={{0,2},{1,3},{2,0},{3,1},{4,6},{5,7},{6,4},{7,5},{8,10},{9,11},{10,... | collective-permute-start | bytes 2359304 | tf_op jit(solution)/shard_map/ppermute | solution.py:1003
  414.7 70.9 %collective-permute-start.52 = (bf16[512,768]{1,0:T(8,128)(2,1)S(1)}, bf16[512,768]{1,0:T(8,128)(2,1)}, u32[]{:S(2)}, u32[]{:S(2)}) collective-permute-start(bf16[512,768]{1,0:T(8,128)(2,1)S(1)} %copy-done.5), channel_id=1, source_target_pairs={{0,1},{1,0},{2,3},{3,2},{4,5},{5,4},{6,7},{7,6},{8,9},{9,8},{10,11... | collective-permute-start | bytes 2359304 | tf_op jit(solution)/shard_map/ppermute | solution.py:1003
  414.7 70.9 %collective-permute-start.54 = (bf16[512,768]{1,0:T(8,128)(2,1)}, bf16[512,768]{1,0:T(8,128)(2,1)}, u32[]{:S(2)}, u32[]{:S(2)}) collective-permute-start(bf16[512,768]{1,0:T(8,128)(2,1)} %collective-permute-done.53.refs_2_), channel_id=1, source_target_pairs={{0,1},{1,0},{2,3},{3,2},{4,5},{5,4},{6,7},{7,6},{8,9},{9,8},{10,11... | collective-permute-start | bytes 2359304 | tf_op jit(solution)/shard_map/ppermute | solution.py:1003
  426.2 52.9 %collective-permute-start.63 = (f32[16,768]{1,0:T(8,128)S(1)}, f32[16,768]{1,0:T(8,128)S(1)}, u32[]{:S(2)}, u32[]{:S(2)}) collective-permute-start(f32[16,768]{1,0:T(8,128)S(1)} %add.195), channel_id=1, source_target_pairs={{0,16},{16,0},{1,17},{17,1},{2,18},{18,2},{3,19},{19,3},{4,20},{20... | collective-permute-start | bytes 147464 | tf_op jit(solution)/shard_map/ppermute | solution.py:1003
  (110 other events, 1922.0 us)
Sparse Core Ops, SparseCore 0:
  332.1 144.9 all-reduce.6

commit v3 on v2

--- a/solution.py
+++ b/solution.py
@@ -280,6 +280,7 @@
 BF = jnp.bfloat16
 F32 = jnp.float32
 ANYWHERE = pl.BlockSpec(memory_space=pl.ANY)
+PAIR = 4
 
 
 def matmul(left, right):
@@ -330,7 +331,7 @@
     return jnp.sum(array, axis=0, keepdims=True)
 
 
-def project_rows(width, value, vectors, lines, weights, fi, ka, va, kt, vt, qt):
+def project_rows(width, value, vectors, lines, weights, fi, ka, va, qt):
     hat, _ = normed_parts(value.astype(F32))
     normed = (hat * vectors[0:1, :] + vectors[1:2, :]).astype(BF)
     fi[...] = normed
@@ -351,26 +352,27 @@
     va[:, half:] = jnp.where(
         lane < 0, values[:, half:], jnp.where(marked, slope, ones)
     ).astype(BF)
-    kt[...] = keys.T[:width].astype(BF)
-    vt[...] = values.T[:width].astype(BF)
     if qt is not None:
         query = (matmul(normed, weights[2][...]) + lines[2:3, :]).astype(BF).astype(F32)
         qt[...] = (query * HD ** (-0.5)).T[:width].astype(BF)
 
 
-def project_own_kernel(ids, x, vectors, lines, wk, wv, wq, fi, ka, va, kt, vt, qt):
+def project_own_kernel(ids, x, vectors, lines, wk, wv, wq, fi, ka, va, qt):
     del ids
-    project_rows(qt.shape[0], x[...], vectors, lines, (wk, wv, wq), fi, ka, va, kt, vt, qt)
-
-
-def project_kernel(count, *refs):
+    project_rows(qt.shape[0], x[...], vectors, lines, (wk, wv, wq), fi, ka, va, qt)
+
+
+def project_kernel(sources, arrays, width, *refs):
     vectors, lines, wk, wv = refs[:4]
-    pieces = refs[4 : 4 + count]
-    fi, ka, va, kt, vt, held, sems = refs[9 + count :]
+    fi, ka, va, held, sems = refs[7 + arrays :]
     step = pl.program_id(0)
+    count, block = held.shape[:2]
 
     def copy(j):
-        return pltpu.make_async_copy(pieces[j], held.at[j], sems.at[j])
+        array, row = sources[j]
+        return pltpu.make_async_copy(
+            refs[4 + array].at[pl.ds(row, block), :], held.at[j], sems.at[j]
+        )
 
     @pl.when(step == 0)
     def _():
@@ -383,23 +385,20 @@
         def _(j=j):
             copy(j).wait()
 
-    project_rows(kt.shape[0], held[step], vectors, lines, (wk, wv), fi, ka, va, kt, vt, None)
-
-
-def project_shapes(total, model, width):
+    project_rows(width, held[step], vectors, lines, (wk, wv), fi, ka, va, None)
+
+
+def project_shapes(total, model):
     return [
         jax.ShapeDtypeStruct((total, model), BF),
         jax.ShapeDtypeStruct((total, WIDE), BF),
         jax.ShapeDtypeStruct((total, WIDE), BF),
-        jax.ShapeDtypeStruct((width, total), BF),
-        jax.ShapeDtypeStruct((width, total), BF),
     ]
 
 
-def project_specs(block, model, width, place):
+def project_specs(block, model, place):
     rows = lambda cols: pl.BlockSpec((block, cols), lambda j, *_: (place(j), 0))
-    flat = pl.BlockSpec((width, block), lambda j, *_: (0, place(j)))
-    return [rows(model), rows(WIDE), rows(WIDE), flat, flat]
+    return [rows(model), rows(WIDE), rows(WIDE)]
 
 
 def project_own(ids, x, vectors, lines, weights, width, total, block, after):
@@ -422,38 +421,40 @@
             ]
             + [whole(a) for a in operands]
             + [ANYWHERE] * len(after),
-            out_specs=project_specs(block, model, width, lambda j: j)
+            out_specs=project_specs(block, model, lambda j: j)
             + [pl.BlockSpec((width, block), lambda j, *_: (0, j))],
         ),
-        out_shape=project_shapes(total, model, width) + [jax.ShapeDtypeStruct((width, rows), BF)],
+        out_shape=project_shapes(total, model) + [jax.ShapeDtypeStruct((width, rows), BF)],
         compiler_params=vmem(32),
         cost_estimate=taking(8),
         name="project_own",
     )(ids, x, *operands, *after)
 
 
-def project(pieces, place, vectors, lines, weights, buffers, after=()):
-    block, model = pieces[0].shape
-    total, width = buffers[0].shape[0], buffers[3].shape[0]
-    count = len(pieces)
+def project(arrays, sources, block, width, place, vectors, lines, weights, buffers, after=()):
+    model = arrays[0].shape[1]
+    total = buffers[0].shape[0]
+    count, given = len(sources), len(arrays)
     operands = [vectors, lines, *weights]
     return pl.pallas_call(
         ordered_after(
-            functools.partial(project_kernel, count), len(operands) + count + 5, len(after)
+            functools.partial(project_kernel, sources, given, width),
+            len(operands) + given + 3,
+            len(after),
         ),
         grid=(count,),
-        in_specs=[whole(a) for a in operands] + [ANYWHERE] * (count + 5 + len(after)),
-        out_specs=project_specs(block, model, width, place),
-        out_shape=project_shapes(total, model, width),
+        in_specs=[whole(a) for a in operands] + [ANYWHERE] * (given + 3 + len(after)),
+        out_specs=project_specs(block, model, place),
+        out_shape=project_shapes(total, model),
         scratch_shapes=[
             pltpu.VMEM((count, block, model), BF),
             pltpu.SemaphoreType.DMA((count,)),
         ],
-        input_output_aliases={len(operands) + count + i: i for i in range(5)},
+        input_output_aliases={len(operands) + given + i: i for i in range(3)},
         compiler_params=vmem(32),
         cost_estimate=taking(count),
         name="project",
-    )(*operands, *pieces, *buffers, *after)
+    )(*operands, *arrays, *buffers, *after)
 
 
 def head_diagonal(rows, tail):
@@ -518,60 +519,71 @@
     )
 
 
-def attend_kernel(blocks, ids, chosen, ka, vt, qt, *outs):
+def attend_kernel(blocks, ids, chosen, ka, va, qt, *outs):
     *mixed, norm = outs
     step = pl.program_id(0)
     width = qt.shape[0]
     heads = width // HD
-    query = qt[...]
-    plain = head_diagonal(query, tail_rows(heads, False, None))
-    marked = head_diagonal(query, tail_rows(heads, True, None))
-    starts, bounds = spots(ids, chosen, step, blocks)
-    tiles = [ka[pl.ds(s, KB), :] for s in starts]
-    near = matmul(jnp.concatenate(tiles[:2], axis=0), plain)
-    far = matmul(jnp.concatenate(tiles[1:], axis=0), marked)
-    gap = offsets_tile(heads)
-    scores = [near[:KB], jnp.where(gap > -WINDOW, near[KB:], far[:KB])]
-    scores += [far[KB * (1 + t) : KB * (2 + t)] for t in range(3)]
-    scores = [jnp.where(m, s, NEGATIVE) for m, s in zip(masks_of(gap, bounds), scores)]
-    top = functools.reduce(jnp.maximum, scores)
-    top = jnp.max(top, axis=0, keepdims=True)
-    weights = [jnp.exp(s - top) for s in scores]
-    total = jnp.sum(functools.reduce(jnp.add, weights), axis=0, keepdims=True)
-    stacked = jnp.concatenate([w.astype(BF) for w in weights], axis=0)
-    values = jnp.concatenate([vt[:, pl.ds(s, KB)] for s in starts], axis=1)
-    full = matmul(values, stacked) / total
-    result = diagonal_of(full, heads).astype(BF)
-    norm[0] = top + jnp.log(total)
+
+    def block_forward(at):
+        query = qt[:, at * KB : (at + 1) * KB]
+        plain = head_diagonal(query, tail_rows(heads, False, None))
+        marked = head_diagonal(query, tail_rows(heads, True, None))
+        starts, bounds = spots(ids, chosen, step * PAIR + at, blocks)
+        tiles = [ka[pl.ds(s, KB), :] for s in starts]
+        near = matmul(jnp.concatenate(tiles[:2], axis=0), plain)
+        far = matmul(jnp.concatenate(tiles[1:], axis=0), marked)
+        gap = offsets_tile(heads)
+        scores = [near[:KB], jnp.where(gap > -WINDOW, near[KB:], far[:KB])]
+        scores += [far[KB * (1 + t) : KB * (2 + t)] for t in range(3)]
+        scores = [jnp.where(m, s, NEGATIVE) for m, s in zip(masks_of(gap, bounds), scores)]
+        top = functools.reduce(jnp.maximum, scores)
+        top = jnp.max(top, axis=0, keepdims=True)
+        weights = [jnp.exp(s - top) for s in scores]
+        total = jnp.sum(functools.reduce(jnp.add, weights), axis=0, keepdims=True)
+        stacked = jnp.concatenate([w.astype(BF) for w in weights], axis=0)
+        values = jnp.concatenate([va[pl.ds(s, KB), :] for s in starts], axis=0)
+        full = rows_inner(values, stacked) / total
+        return diagonal_of(full, heads).astype(BF), top + jnp.log(total)
+
+    results = [block_forward(at) for at in range(PAIR)]
+    for at, (_, line) in enumerate(results):
+        norm[at] = line
+    result = jnp.concatenate([value for value, _ in results], axis=1)
     for p in range(4):
 
-        @pl.when(lax.div(step, blocks // 4) == p)
+        @pl.when(lax.div(step, blocks // 4 // PAIR) == p)
         def _(p=p):
             mixed[p][...] = result
 
 
-def attend(ids, chosen, ka, vt, qt, blocks):
+def attend(ids, chosen, ka, va, qt, blocks):
     width = qt.shape[0]
     heads = width // HD
     per = blocks // 4
+    turns = per // PAIR
     piece = lambda p: pl.BlockSpec(
-        (width, KB), lambda i, *_: (0, jnp.clip(i - per * p, 0, per - 1))
+        (width, PAIR * KB), lambda i, *_: (0, jnp.clip(i - turns * p, 0, turns - 1))
     )
     return pl.pallas_call(
         functools.partial(attend_kernel, blocks),
         grid_spec=pltpu.PrefetchScalarGridSpec(
             num_scalar_prefetch=2,
-            grid=(blocks,),
-            in_specs=[whole(ka), whole(vt), pl.BlockSpec((width, KB), lambda i, *_: (0, i))],
+            grid=(blocks // PAIR,),
+            in_specs=[
+                whole(ka),
+                whole(va),
+                pl.BlockSpec((width, PAIR * KB), lambda i, *_: (0, i)),
+            ],
             out_specs=[piece(p) for p in range(4)]
-            + [pl.BlockSpec((1, 1, heads * KB), lambda i, *_: (i, 0, 0))],
+            + [pl.BlockSpec((PAIR, 1, heads * KB), lambda i, *_: (i, 0, 0))],
         ),
         out_shape=[jax.ShapeDtypeStruct((width, per * KB), BF)] * 4
         + [jax.ShapeDtypeStruct((blocks, 1, heads * KB), F32)],
         compiler_params=vmem(40),
         cost_estimate=taking(14),
         name="attend",
-    )(ids, chosen, ka, vt, qt)
+    )(ids, chosen, ka, va, qt)
 
 
 def attend_back_kernel(
@@ -580,7 +592,6 @@
     chosen,
     ka,
     va,
-    kt,
     qt,
     norm,
     *refs,
@@ -590,7 +601,7 @@
     step = pl.program_id(0)
     width = qt.shape[0]
     heads = width // HD
-    per = blocks // 4
+    per, steps = blocks // 4, blocks // PAIR
 
     def copy(j):
         return pltpu.make_async_copy(grads[j], grad_all.at[j], sems.at[j])
@@ -605,15 +616,16 @@
         for j in range(4):
             copy(j).wait()
 
-    @pl.when(step < blocks)
-    def _():
-        query = qt[...]
-        lanes = pl.ds(pl.multiple_of(lax.rem(step, per) * KB, KB), KB)
-        upstream = grad_all[lax.div(step, per), :, lanes]
-        plain = head_diagonal(query, tail_rows(heads, False, -norm[0]))
-        marked = head_diagonal(query, tail_rows(heads, True, -norm[0]))
+    def block_back(at):
+        index = step * PAIR + at
+        column = slice(at * KB, (at + 1) * KB)
+        query = qt[:, column]
+        lanes = pl.ds(pl.multiple_of(lax.rem(index, per) * KB, KB), KB)
+        upstream = grad_all[lax.div(index, per), :, lanes]
+        plain = head_diagonal(query, tail_rows(heads, False, -norm[at]))
+        marked = head_diagonal(query, tail_rows(heads, True, -norm[at]))
         back = head_diagonal(upstream, tail_rows(heads, False, None))
-        starts, bounds = spots(ids, chosen, step, blocks)
+        starts, bounds = spots(ids, chosen, index, blocks)
         tiles = [ka[pl.ds(s, KB), :] for s in starts]
         near = matmul(jnp.concatenate(tiles[:2], axis=0), plain)
         far = matmul(jnp.concatenate(tiles[1:], axis=0), marked)
@@ -635,26 +647,34 @@
         prob = jnp.concatenate(probs, axis=0).astype(BF)
         near_keys = near_far(near_signal, plain)
         far_keys = near_far(far_signal, marked)
-        rest = (far_exact - far_signal.astype(F32)).astype(BF)
-        far_rest = near_far(rest, marked[WIDE // 2 :])
         value_parts = near_far(prob, back)
         key_parts = [near_keys[:KB], near_keys[KB:] + far_keys[:KB]]
         key_parts += [far_keys[KB * (1 + t) : KB * (2 + t)] for t in range(3)]
-        for c, s in enumerate(starts):
-            key_sum[pl.ds(s, KB), :] += key_parts[c]
-            value_sum[pl.ds(s, KB), :] += value_parts[c * KB : (c + 1) * KB]
-            if c > 0:
-                key_sum[pl.ds(s, KB), WIDE // 2 :] += far_rest[(c - 1) * KB : c * KB]
-        keys = jnp.concatenate([kt[:, pl.ds(s, KB)] for s in starts], axis=1)
-        full = diagonal_of(matmul(keys, signal), heads) * HD ** (-0.5)
+        value_parts = [value_parts[c * KB : (c + 1) * KB] for c in range(5)]
+        rest = (far_exact - far_signal.astype(F32)).astype(BF)
+        far_rest = near_far(rest, marked[WIDE // 2 :])
+        far_rest = [far_rest[c * KB : (c + 1) * KB] for c in range(4)]
+        keys = jnp.concatenate([tiles[0], tiles[1]] + tiles[2:], axis=0)
+        full = diagonal_of(rows_inner(keys, signal), heads) * HD ** (-0.5)
         full = jnp.concatenate([full, jnp.zeros((WIDE - width, KB), F32)], axis=0).T
-        query_grad[...] = full.astype(BF)
-        totals[:, 2 * WIDE :] += column_sums(full)
-
-    @pl.when(step >= blocks)
+        return starts, key_parts, value_parts, far_rest, full
+
+    @pl.when(step < steps)
+    def _():
+        results = [block_back(at) for at in range(PAIR)]
+        for at, (starts, key_parts, value_parts, far_rest, full) in enumerate(results):
+            for c, s in enumerate(starts):
+                key_sum[pl.ds(s, KB), :] += key_parts[c]
+                value_sum[pl.ds(s, KB), :] += value_parts[c]
+                if c > 0:
+                    key_sum[pl.ds(s, KB), WIDE // 2 :] += far_rest[c - 1]
+            query_grad[at * KB : (at + 1) * KB, :] = full.astype(BF)
+            totals[:, 2 * WIDE :] += column_sums(full)
+
+    @pl.when(step >= steps)
     def _():
         rows = spread.shape[0]
-        at = pl.ds(pl.multiple_of((step - blocks) * rows, rows), rows)
+        at = pl.ds(pl.multiple_of((step - steps) * rows, rows), rows)
         lane = lax.broadcasted_iota(jnp.int32, (rows, WIDE), 1)
         marks = (lane >= width) & (lane < width + heads)
         keys = jnp.where(lane < width, key_sum[at, :], 0.0)
@@ -666,28 +686,28 @@
         totals[:, WIDE : 2 * WIDE] += column_sums(values)
 
 
-def attend_back(ids, chosen, ka, va, kt, qt, norm, grads, blocks, after=()):
+def attend_back(ids, chosen, ka, va, qt, norm, grads, blocks, after=()):
     width = qt.shape[0]
     heads = width // HD
     total = ka.shape[0]
-    rows = 4 * KB
-    last = lambda i: jnp.minimum(i, blocks - 1)
+    rows = 8 * KB
+    steps = blocks // PAIR
+    last = lambda i: jnp.minimum(i, steps - 1)
     return pl.pallas_call(
-        ordered_after(functools.partial(attend_back_kernel, blocks), 11, len(after)),
+        ordered_after(functools.partial(attend_back_kernel, blocks), 10, len(after)),
         grid_spec=pltpu.PrefetchScalarGridSpec(
             num_scalar_prefetch=2,
-            grid=(blocks + total // rows,),
+            grid=(steps + total // rows,),
             in_specs=[
                 whole(ka),
                 whole(va),
-                whole(kt),
-                pl.BlockSpec((width, KB), lambda i, *_: (0, last(i))),
-                pl.BlockSpec((1, 1, heads * KB), lambda i, *_: (last(i), 0, 0)),
+                pl.BlockSpec((width, PAIR * KB), lambda i, *_: (0, last(i))),
+                pl.BlockSpec((PAIR, 1, heads * KB), lambda i, *_: (last(i), 0, 0)),
             ]
             + [ANYWHERE] * (4 + len(after)),
             out_specs=[
-                pl.BlockSpec((rows, 2 * WIDE), lambda i, *_: (jnp.maximum(i - blocks, 0), 0)),
-                pl.BlockSpec((KB, WIDE), lambda i, *_: (last(i), 0)),
+                pl.BlockSpec((rows, 2 * WIDE), lambda i, *_: (jnp.maximum(i - steps, 0), 0)),
+                pl.BlockSpec((PAIR * KB, WIDE), lambda i, *_: (last(i), 0)),
                 pl.BlockSpec((1, 3 * WIDE), lambda i, *_: (0, 0)),
             ],
             scratch_shapes=[
@@ -705,14 +725,15 @@
         compiler_params=vmem(56),
         cost_estimate=taking(36),
         name="attend_back",
-    )(ids, chosen, ka, va, kt, qt, norm, *grads, *after)
+    )(ids, chosen, ka, va, qt, norm, *grads, *after)
 
 
 def feed_forward_kernel(order, ids, vectors, tokens, upstream, *refs):
     features, outs, ups, downs = refs[:4], refs[4:8], refs[8:12], refs[12:16]
     mixed_grads = refs[16:20]
-    output, hidden_grad, kept, sent, kept_out, sent_out, sums, up_biases = refs[20:28]
-    out_all, up_all, down_all, hidden, hat, scale, second_in, feed, second_grad, sems = refs[28:]
+    output, hidden_grad, kept, sent, sums, up_biases = refs[20:26]
+    out_all, up_all, down_all, hidden, hat, scale, second_in, feed, second_grad = refs[26:35]
+    staged, staged_out, sems, out_sems = refs[35:]
     step = pl.program_id(0)
     width = features[0].shape[0]
     model = tokens.shape[1]
@@ -723,6 +744,20 @@
         return [
             pltpu.make_async_copy(up, up_all.at[slot], sems.at[4 + slot]),
             pltpu.make_async_copy(down, down_all.at[slot], sems.at[8 + slot]),
+        ]
+
+    def leaving(slot, first=0, last=5):
+        target = (sent if slot < 2 else kept).at[slot % 2]
+        half, out_half = model // 2, width // 2
+        spans = [(staged, 0, 0, half), (staged, half, half + out_half, half)]
+        spans += [(staged, model, model + width, model)]
+        spans += [(staged_out, 0, half, out_half), (staged_out, out_half, model + out_half, out_half)]
+        return [
+            pltpu.make_async_copy(
+                source.at[slot, pl.ds(a, n), :], target.at[pl.ds(b, n), :], out_sems.at[slot, i]
+            )
+            for i, (source, a, b, n) in enumerate(spans)
+            if first <= i < last
         ]
 
     def out_copy(j):
@@ -790,15 +825,14 @@
     up_grad = rows_inner(second_in[...], pre_low).astype(BF)
     down_grad = rows_inner(act, upstream[...]).astype(BF)
 
-    @pl.when(step < 2)
-    def _():
-        sent[0, :model] = up_grad
-        sent[0, model:] = down_grad
-
-    @pl.when(step >= 2)
-    def _():
-        kept[0, :model] = up_grad
-        kept[0, model:] = down_grad
+    staged[step, :model] = up_grad
+    staged[step, model:] = down_grad
+    for slot in range(4):
+
+        @pl.when(step == slot)
+        def _(slot=slot):
+            for copy in leaving(slot, 0, 3):
+                copy.start()
 
     @pl.when(step == 3)
     def _():
@@ -811,11 +845,16 @@
         low = back.astype(BF)
         for j in range(4):
             mixed_grads[j][...] = near_far(out_all[j, :width, :], low).astype(BF)
-            out_grad = matmul(features[j][...], low).astype(BF)
-            (sent_out if j % 2 else kept_out)[j // 2] = out_grad
+            slot = order.index(j)
+            staged_out[slot] = matmul(features[j][...], low).astype(BF)
+            for copy in leaving(slot, 3, 5):
+                copy.start()
         sums[...] = jnp.concatenate(
             [column_sums(a) for a in (grad * normed, grad, back, upstream_f)], axis=0
         )
+        for slot in range(4):
+            for copy in leaving(slot):
+                copy.wait()
 
 
 def feed_forward(ids, vectors, tokens, upstream, features, outs, ups, downs):
@@ -830,17 +869,14 @@
     out_shape = [shape((width, quarter), BF)] * 4 + [
         shape((quarter, model), BF),
         shape((quarter, model), F32),
-        shape((2, 2 * model, model), BF),
-        shape((2, 2 * model, model), BF),
-        shape((2, width, model), BF),
-        shape((2, width, model), BF),
+        shape((2, 2 * model + width, model), BF),
+        shape((2, 2 * model + width, model), BF),
         shape((4, model), F32),
         shape((4, 1, model), F32),
     ]
     out_specs = [flat(a) for a in out_shape]
-    out_specs[6] = pl.BlockSpec((1, 2 * model, model), lambda j, *_: (jnp.maximum(j - 2, 0), 0, 0))
-    out_specs[7] = pl.BlockSpec((1, 2 * model, model), lambda j, *_: (jnp.minimum(j, 1), 0, 0))
-    out_specs[11] = pl.BlockSpec((1, 1, model), lambda j, *_: (j, 0, 0))
+    out_specs[6] = out_specs[7] = ANYWHERE
+    out_specs[9] = pl.BlockSpec((1, 1, model), lambda j, *_: (j, 0, 0))
     return pl.pallas_call(
         functools.partial(feed_forward_kernel, order),
         grid_spec=pltpu.PrefetchScalarGridSpec(
@@ -860,7 +896,10 @@
                 pltpu.VMEM((quarter, model), BF),
                 pltpu.VMEM((quarter, model), F32),
                 pltpu.VMEM((quarter, model), F32),
+                pltpu.VMEM((4, 2 * model, model), BF),
+                pltpu.VMEM((4, width, model), BF),
                 pltpu.SemaphoreType.DMA((12,)),
+                pltpu.SemaphoreType.DMA((4, 5)),
             ],
         ),
         out_shape=out_shape,
@@ -910,7 +949,7 @@
         ],
         out_shape=[jax.ShapeDtypeStruct((2, quarter, model), BF)] * 2,
         compiler_params=vmem(24),
-        cost_estimate=taking(3),
+        cost_estimate=taking(0.01),
         name="push",
     )(*operands, *after)
 
@@ -931,11 +970,11 @@
     small[13:14, :] = column_sums(first_grad)
 
 
-def finish(ids, vectors, tokens, arrived, mine, hidden_grad, sums, up_biases, totals):
+def finish(ids, vectors, tokens, arrived, mine, hidden_grad, sums, up_biases, totals, after):
     quarter, model = mine.shape
     operands = [arrived, mine, hidden_grad, sums, up_biases, totals]
     return pl.pallas_call(
-        finish_kernel,
+        ordered_after(finish_kernel, 3 + len(operands), len(after)),
         grid_spec=pltpu.PrefetchScalarGridSpec(
             num_scalar_prefetch=1,
             grid=(1,),
@@ -943,7 +982,8 @@
                 whole(vectors),
                 pl.BlockSpec((quarter, model), lambda j, ids: (ids[0], 0)),
             ]
-            + [whole(a) for a in operands],
+            + [whole(a) for a in operands]
+            + [ANYWHERE] * len(after),
             out_specs=[
                 pl.BlockSpec((quarter, model), lambda j, *_: (0, 0)),
                 pl.BlockSpec((16, model), lambda j, *_: (0, 0)),
@@ -954,9 +994,9 @@
             jax.ShapeDtypeStruct((16, model), F32),
         ],
         compiler_params=vmem(32),
-        cost_estimate=taking(4),
+        cost_estimate=taking(0.01),
         name="finish",
-    )(ids, vectors, tokens, *operands)
+    )(ids, vectors, tokens, *operands, *after)
 
 
 def ordered_kernel(ids, *refs):
@@ -983,9 +1023,195 @@
         ),
         out_shape=jax.ShapeDtypeStruct((count * size, model), kind),
         compiler_params=vmem(24),
-        cost_estimate=taking(3),
+        cost_estimate=taking(0.01),
         name="ordered",
     )(ids, *parts)
+
+
+def combine_kernel(ids, first, kept, given, own_a, far_a, stay_b, leave_b):
+    step, side = pl.program_id(0), ids[2]
+    total = (kept[...].astype(F32) + given[...].astype(F32)).astype(BF)
+
+    @pl.when(step < first)
+    def _():
+        own_a[...] = total[0]
+        far_a[...] = total[1]
+
+    @pl.when((step >= first) & (lax.div(step - first, 2) == side))
+    def _():
+        stay_b[...] = total
+
+    @pl.when((step >= first) & (lax.div(step - first, 2) != side))
+    def _():
+        leave_b[...] = total
+
+
+def combine(ids, kept, given, part):
+    _, rows, model = kept.shape
+    block = (rows - part) // 4
+    first = part // block
+    both = pl.BlockSpec((2, block, model), lambda i, ids: (0, i, 0))
+    a_rows = pl.BlockSpec((block, model), lambda i, ids: (jnp.minimum(i, first - 1), 0))
+    b_rows = lambda turn: pl.BlockSpec(
+        (2, block, model),
+        lambda i, ids: (
+            0,
+            jnp.clip(i - first - 2 * jnp.where(turn, 1 - ids[2], ids[2]), 0, 1),
+            0,
+        ),
+    )
+    shape = jax.ShapeDtypeStruct
+    return pl.pallas_call(
+        lambda ids, *refs: combine_kernel(ids, first, *refs),
+        grid_spec=pltpu.PrefetchScalarGridSpec(
+            num_scalar_prefetch=1,
+            grid=(rows // block,),
+            in_specs=[both, both],
+            out_specs=[a_rows, a_rows, b_rows(False), b_rows(True)],
+        ),
+        out_shape=[shape((part, model), BF)] * 2 + [shape((2, 2 * block, model), BF)] * 2,
+        compiler_params=vmem(24),
+        cost_estimate=taking(6),
+        name="combine",
+    )(ids, kept, given)
+
+
+def weight_sums_kernel(ids, first_in, spread, query_grad, stay, leave, held, held_query):
+    step = pl.program_id(0)
+    steps = pl.num_programs(0)
+    turned = first_in[...].T
+    rows = matmul(turned, spread[...])
+
+    @pl.when(step == 0)
+    def _():
+        held[...] = rows
+        held_query[...] = matmul(turned, query_grad[...])
+
+    @pl.when(step > 0)
+    def _():
+        held[...] += rows
+
+    @pl.when((step > 0) & (step < steps // 4))
+    def _():
+        held_query[...] += matmul(turned, query_grad[...])
+
+    @pl.when(step == steps - 1)
+    def _():
+        half = stay.shape[0]
+        width = (stay.shape[1] - WIDE) // 2
+        for part in range(2):
+            at = pl.ds(part * half, half)
+            result = jnp.concatenate(
+                [
+                    held[at, :WIDE],
+                    held[at, WIDE : WIDE + width],
+                    held_query[at, :width],
+                ],
+                axis=1,
+            ).astype(BF)
+
+            @pl.when(ids[2] == part)
+            def _(result=result):
+                stay[...] = result
+
+            @pl.when(ids[2] != part)
+            def _(result=result):
+                leave[...] = result
+
+
+def weight_sums(ids, first_in, spread, query_grad, width, after):
+    total, model = first_in.shape
+    block = query_grad.shape[0] // 2
+    shape = jax.ShapeDtypeStruct((model // 2, WIDE + 2 * width), BF)
+    flat = pl.BlockSpec(shape.shape, lambda i, ids: (0, 0))
+    return pl.pallas_call(
+        ordered_after(weight_sums_kernel, 4, len(after)),
+        grid_spec=pltpu.PrefetchScalarGridSpec(
+            num_scalar_prefetch=1,
+            grid=(total // block,),
+            in_specs=[
+                pl.BlockSpec((block, model), lambda i, ids: (i, 0)),
+                pl.BlockSpec((block, 2 * WIDE), lambda i, ids: (i, 0)),
+                pl.BlockSpec((block, WIDE), lambda i, ids: (jnp.minimum(i, 1), 0)),
+            ]
+            + [ANYWHERE] * len(after),
+            out_specs=[flat, flat],
+            scratch_shapes=[pltpu.VMEM((model, 2 * WIDE), F32), pltpu.VMEM((model, WIDE), F32)],
+        ),
+        out_shape=[shape, shape],
+        compiler_params=vmem(32),
+        cost_estimate=taking(0.01),
+        name="weight_sums",
+    )(ids, first_in, spread, query_grad, *after)
+
+
+def first_sums_kernel(ids, own_a, came_a, stay_b, came_b, stay, away, keep, send):
+    half = stay.shape[0]
+    keep[...] = (stay_b[0].astype(F32) + came_b[0].astype(F32)).astype(BF)
+    send[...] = (stay_b[1].astype(F32) + came_b[1].astype(F32)).astype(BF)
+    for part in range(2):
+        rows = pl.ds(part * half, half)
+        total = (own_a[rows, :].astype(F32) + came_a[rows, :].astype(F32)).astype(BF)
+
+        @pl.when(ids[2] == part)
+        def _(total=total):
+            stay[...] = total
+
+        @pl.when(ids[2] != part)
+        def _(total=total):
+            away[...] = total
+
+
+def first_sums(ids, own_a, came_a, stay_b, came_b):
+    part, model = own_a.shape
+    operands = [own_a, came_a, stay_b, came_b]
+    shape = jax.ShapeDtypeStruct
+    out_shape = [shape((part // 2, model), BF)] * 2 + [shape(stay_b.shape[1:], BF)] * 2
+    return pl.pallas_call(
+        first_sums_kernel,
+        grid_spec=pltpu.PrefetchScalarGridSpec(
+            num_scalar_prefetch=1,
+            grid=(1,),
+            in_specs=[whole(a) for a in operands],
+            out_specs=[pl.BlockSpec(a.shape, lambda *_: (0, 0)) for a in out_shape],
+        ),
+        out_shape=out_shape,
+        compiler_params=vmem(32),
+        cost_estimate=taking(0.01),
+        name="first_sums",
+    )(ids, *operands)
+
+
+def dense_kernel(ids, mine, theirs, up, down, out):
+    half, out_half = up.shape[0], out.shape[0]
+    for j, part in enumerate((mine, theirs)):
+
+        @pl.when(pl.program_id(0) == j)
+        def _(part=part):
+            up[...] = part[:half, :].astype(F32)
+            out[...] = part[half : half + out_half, :].astype(F32)
+            down[...] = part[half + out_half :, :].astype(F32)
+
+
+def dense_results(ids, mine, theirs, width):
+    rows, model = mine.shape
+    place = lambda size: pl.BlockSpec(
+        (size, model), lambda j, ids: (jnp.bitwise_xor(ids[2], j), 0)
+    )
+    shape = jax.ShapeDtypeStruct
+    return pl.pallas_call(
+        dense_kernel,
+        grid_spec=pltpu.PrefetchScalarGridSpec(
+            num_scalar_prefetch=1,
+            grid=(2,),
+            in_specs=[whole(mine), whole(theirs)],
+            out_specs=[place(model // 2), place(model // 2), place(width // 2)],
+        ),
+        out_shape=[shape((model, model), F32)] * 2 + [shape((width, model), F32)],
+        compiler_params=vmem(32),
+        cost_estimate=taking(0.01),
+        name="dense_results",
+    )(ids, mine, theirs)
 
 
 def held_until(array, after):
@@ -1052,7 +1278,13 @@
         part = own[h * block : (h + 1) * block]
         for k in range(1, ranks):
             part = upward(part, ranks)
-            arriving[k, h] = spread_over_mp(part)
+            arriving[k, h] = part
+    gathered = {}
+    for k in range(1, ranks):
+        for halves in ((0, 1),) if k < ranks - 1 else ((0,), (1,)):
+            mine = jnp.concatenate([arriving[k, h] for h in halves], axis=0)
+            mine = jnp.concatenate([mine, swap(mine, 2)], axis=0)
+            gathered[k, halves] = [mine, swap(mine, 1)]
 
     b_high = b_up.astype(BF)
     b_low = (b_up - b_high.astype(F32)).astype(BF)
@@ -1075,97 +1307,99 @@
     wq, wv = wide(w_qkv[:, 0]), wide(w_qkv[:, 2])
     wk = wide(jnp.concatenate([w_qkv[:, 1], w_score], axis=1))
 
-    last = [arriving[ranks - 1, h][0] for h in range(2)]
     *buffers, qt = project_own(
-        ids, inputs[0], vectors, lines, (wk, wv, wq), width, total, block, last
-    )
-    for k in range(1, ranks - 1):
-        pieces = [arriving[k, h][j] for j in range(4) for h in range(2)]
+        ids, inputs[0], vectors, lines, (wk, wv, wq), width, total, block, [arriving[ranks - 1, h] for h in range(2)]
+    )
+    for (k, halves), arrays in gathered.items():
+        count = len(halves)
         buffers = project(
-            pieces, lambda j, k=k: 8 * k + j, vectors, lines, (wk, wv), buffers, [(first, second)[k - 1]]
-        )
-    for h in range(2):
-        buffers = project(
-            arriving[ranks - 1, h],
-            lambda j, h=h: 8 * (ranks - 1) + 2 * j + h,
+            arrays,
+            [(j % 2, (j // 2 * count + i) * block) for j in range(4) for i in range(count)],
+            block,
+            width,
+            lambda j, k=k, h=halves[0], count=count: 8 * k + (2 // count) * j + h,
             vectors,
             lines,
             (wk, wv),
             buffers,
+            [(first, second)[k - 1]] if k < ranks - 1 else (),
         )
-    first_in, ka, va, kt, vt = buffers
+    first_in, ka, va = buffers
 
     chosen = selection[0]
-    *mixed, norm = attend(ids, chosen, ka, vt, qt, blocks)
+    *mixed, norm = attend(ids, chosen, ka, va, qt, blocks)
 
     features = [mixed[0]] + [swap(mixed[j], j) for j in (1, 2, 3)]
-    *mixed_grads, output, hidden_grad, kept, sent, kept_out, sent_out, sums, up_biases = (
-        feed_forward(ids, vectors, inputs[0], cotangent[0], features, w_outs, w_ups, w_downs)
+    *mixed_grads, output, hidden_grad, kept, sent, sums, up_biases = feed_forward(
+        ids, vectors, inputs[0], cotangent[0], features, w_outs, w_ups, w_downs
     )
     returned = [mixed_grads[0]] + [swap(mixed_grads[j], j) for j in (1, 2, 3)]
 
-    given, given_out = swap(sent, 1), swap(sent_out, 1)
-    part = 3 * model // 2
-    across = [kept[1, :part] + given[1, :part], kept[1, part:] + given[1, part:]]
-    across_out = kept_out[1] + given_out[1]
-    crossing = [swap(a, 2) for a in (*across, across_out)]
-
+    part = model + width
+    own_a, far_a, stay_b, leave_b = combine(ids, kept, swap(sent, 1), part)
+    came_a, came_b = swap(far_a, 2), swap(leave_b, 1, "dp")
+
+    weights = (wk, wv, wq)
     spread, query_grad, totals = attend_back(
-        ids, chosen, ka, va, kt, qt, norm, returned, blocks, (*across, across_out)
-    )
-
-    carried, crossed = None, []
-    for k in range(ranks - 1, -1, -1):
-        pushed, pushed_out = push(
-            spread,
-            (wk, wv, wq),
-            k,
-            quarter,
-            query_grad if k == 0 else None,
-            crossing[:1] if k == 2 else crossing[1:] if k == 0 else (),
-        )
-        arrived = swap(pushed_out, 1)
-        crossed.append(swap(pushed[1] + arrived[1], 2))
-        mine = pushed[0] + arrived[0] + crossed[-1]
-        if k > 0:
-            carried = downward(mine if carried is None else mine + carried, ranks)
-
-    key_value_grad = rows_inner(first_in, spread)
-    query_weight_grad = rows_inner(first_in[:rows], query_grad)
-    qkv_pack = jnp.concatenate(
-        [
-            key_value_grad[:, :WIDE],
-            key_value_grad[:, WIDE : WIDE + width],
-            query_weight_grad[:, :width],
-        ],
-        axis=1,
-    )
-    qkv_pack = qkv_pack.astype(BF)
-    half = model // 2
-    qkv_mine = lax.dynamic_slice_in_dim(qkv_pack, side * half, half, 0)
-    qkv_sent = lax.dynamic_slice_in_dim(qkv_pack, (1 - side) * half, half, 0)
-    qkv_mine = qkv_mine + swap(qkv_sent, 1, "dp")
+        ids, chosen, ka, va, qt, norm, returned, blocks, (far_a, leave_b)
+    )
+
+    weights = (wk, wv, wq)
+    stay_a, away_a, keep_b, send_b = first_sums(ids, own_a, came_a, stay_b, came_b)
+    kept_3, sent_3 = push(spread, weights, 3, quarter, None, (away_a,))
+    came_a, came_b, arrived_3 = swap(away_a, 1, "dp"), swap(send_b, 2), swap(sent_3, 1)
+    qkv, qkv_leave = weight_sums(ids, first_in, spread, query_grad, width, (sent_3,))
+    kept_2, sent_2 = push(spread, weights, 2, quarter, None, (qkv_leave,))
+    dense = jnp.concatenate([stay_a + came_a, keep_b + came_b], axis=0)
+    across = held_until(kept_3[1] + arrived_3[1], (dense, sent_2))
+    dense = lax.psum(dense, "seq")
+    sent_2, qkv_leave = held_until(sent_2, (across,)), held_until(qkv_leave, (across,))
+    crossed_3, came_qkv, arrived_2 = swap(across, 2), swap(qkv_leave, 1, "dp"), swap(sent_2, 1)
+    kept_1, sent_1 = push(spread, weights, 1, quarter, None, (across,))
+    kept_0, sent_0 = push(spread, weights, 0, quarter, query_grad, (sent_1,))
+    qkv = qkv + came_qkv
+    across = kept_2[1] + arrived_2[1]
+    carried = held_until(kept_3[0] + arrived_3[0] + crossed_3, (qkv, sent_0, across))
+    carried = downward(carried, ranks)
+    crossed_2, arrived_1, arrived_0 = swap(across, 2), swap(sent_1, 1), swap(sent_0, 1)
+    mine = kept_2[0] + arrived_2[0] + crossed_2 + carried
+    across = held_until(kept_1[1] + arrived_1[1], (mine,))
+    output_parts = spread_over_mp(held_until(output, (mine,)))
+    carried = downward(mine, ranks)
+    crossed_1 = swap(across, 2)
+    mine = kept_1[0] + arrived_1[0] + crossed_1 + carried
+    across = held_until(kept_0[1] + arrived_0[1], (mine,))
+    dense = held_until(dense, (across,))
+    qkv = lax.psum(held_until(qkv, (dense,)), "seq")
+    dense_theirs = swap(dense, 1, "dp")
+    carried = downward(mine, ranks)
+    crossed_0 = swap(across, 2)
+    mine = kept_0[0] + arrived_0[0] + crossed_0
+
+    output = ordered(ids, 0, output_parts, BF)
+    input_part, small = finish(
+        ids,
+        vectors,
+        inputs[0],
+        carried,
+        mine,
+        hidden_grad,
+        sums,
+        up_biases,
+        totals,
+        (output, dense_theirs),
+    )
+    across = swap(input_part, 2)
+    input_parts = [input_part, swap(input_part, 1), across]
+    input_parts.append(swap(held_until(across, (qkv,)), 1))
     for flip in (1, 2):
-        qkv_mine = qkv_mine + swap(qkv_mine, flip, "seq")
-    qkv_sum = ordered(ids, 2, [qkv_mine, swap(qkv_mine, 1, "dp")], F32)
-
-    dense = [
-        kept[0, :part] + given[0, :part] + crossing[0],
-        kept[0, part:] + given[0, part:] + crossing[1],
-        kept_out[0] + given_out[0] + crossing[2],
-    ]
-    dense = lax.psum(dense, ("dp", "seq"))
-    *dense, out_grad = [a.astype(F32) for a in dense]
-    dense = jnp.concatenate(dense, axis=0)
-
-    input_part, small = finish(
-        ids, vectors, inputs[0], carried, mine, hidden_grad, sums, up_biases, totals
-    )
-    output_parts = spread_over_mp(held_until(output, crossed))
-    input_grad = ordered(ids, 0, spread_over_mp(input_part), BF)
-    for axis, flips in (("mp", (1, 2)), ("dp", (1,)), ("seq", (1, 2))):
-        for flip in flips:
-            small = small + swap(small, flip, axis)
+        small = small + swap(small, flip)
+    small = small + swap(small, 1, "dp")
+    qkv_sum = ordered(ids, 2, [qkv, swap(qkv, 1, "dp")], F32)
+    up_grad, down_grad, out_grad = dense_results(ids, dense, dense_theirs, width)
+    for flip in (1, 2):
+        small = small + swap(small, flip, "seq")
+    input_grad = ordered(ids, 0, input_parts, BF)
     up_bias = lax.dynamic_slice_in_dim(small, 4 + me, 1, 0)[0]
     biases = lax.dynamic_slice_in_dim(small, 8 + me, 1, 0)[0]
     query_at, value_at = WIDE + width, WIDE
@@ -1176,7 +1410,7 @@
         [biases[2 * WIDE : 2 * WIDE + width], biases[WIDE : WIDE + width]], axis=0
     )
     return (
-        ordered(ids, 0, output_parts, BF)[None],
+        output[None],
         input_grad[None],
         small[12],
         small[13],
@@ -1188,9 +1422,9 @@
         small[2],
         small[0],
         small[1],
-        dense[:model],
+        up_grad,
         up_bias,
-        dense[model:],
+        down_grad,
         small[3],
     )
 

time: 510 us -> 484 us (0.949)
  waiting for transfers between devices: 191 us -> 172 us
  Pallas kernels: 143 us -> 156 us
  matrix products: 12.7 us -> 0 us
  other arithmetic: 33.7 us -> 27.2 us
  starting transfers between devices: 72.7 us -> 67 us
    ppermute x61 -> x50, waiting for transfers between devices: 108 us -> 63.4 us  [swap(): lax.ppermute(array, axis, [(i, i ^ flip) for i in range(lax.axis_size(axi...]
    ppermute x3, waiting for transfers between devices: 26.1 us -> 69.5 us  [downward(): return lax.ppermute(array, 'seq', [(i + 1, i) for i in range(ranks - 1)])]
    psum x1 -> x2, waiting for transfers between devices: 44 us -> 13.1 us  [the longest x1 13.1 us: body_resident(): qkv = lax.psum(held_until(qkv, (dense,)), 'seq')]
    pallas_call x5 -> x9, Pallas kernels: 27.9 us -> 49.9 us  [the longest x4 23.3 us: project(): pl.pallas_call(ordered_after(functools.partial(project_kernel, sources, g...]
    dot_general x2 -> x0, matrix products: 12.7 us -> none  [rows_inner(): lax.dot_general(left, right, (((0,), (0,)), ((), ())), preferred_element_...]
    ppermute x6, waiting for transfers between devices: 13.6 us -> 25.7 us  [upward(): return lax.ppermute(array, 'seq', [(i, i + 1) for i in range(ranks - 1)])]
    unnamed x148 -> x187, local copies, waits for them, and re-layouts: 22.7 us -> 30.7 us
    pallas_call x1, Pallas kernels: 40.3 us -> 33.8 us  [attend_back(): pl.pallas_call(ordered_after(functools.partial(attend_back_kernel, blocks...]
  transfers between devices with their start and end apart: 71 -> 61, of which waited for: 23 -> 22; matrix products, arithmetic and copies ran while one was open for 13% -> 8% of each run, Pallas kernels for 22% -> 25%
where the time goes in v3:
time: 484 us; the launch traced here: 475 us
  waiting for transfers between devices  172 us (36%)
  Pallas kernels  156 us (32%)
  starting transfers between devices  67 us (14%)
  local copies, waits for them, and re-layouts  37.6 us (8%)
  other arithmetic  27.2 us (6%)
  between operations  15.9 us (3%)
    ppermute x3, waiting for transfers between devices, downward(): return lax.ppermute(array, 'seq', [(i + 1, i) for i in range(ranks - 1)])  69.5 us
    ppermute x50, waiting for transfers between devices, swap(): lax.ppermute(array, axis, [(i, i ^ flip) for i in range(lax.axis_size(axi...  63.4 us
    ppermute x50, starting transfers between devices, swap(): lax.ppermute(array, axis, [(i, i ^ flip) for i in range(lax.axis_size(axi...  38.5 us
    pallas_call x1, Pallas kernels, attend_back(): pl.pallas_call(ordered_after(functools.partial(attend_back_kernel, blocks...  33.8 us
    unnamed x187, local copies, waits for them, and re-layouts  30.7 us
    pallas_call x1, Pallas kernels, feed_forward(): pl.pallas_call(functools.partial(feed_forward_kernel, order), grid_spec=p...  28.8 us
    ppermute x6, waiting for transfers between devices, upward(): return lax.ppermute(array, 'seq', [(i, i + 1) for i in range(ranks - 1)])  25.7 us
    ppermute x6, starting transfers between devices, upward(): return lax.ppermute(array, 'seq', [(i, i + 1) for i in range(ranks - 1)])  24.3 us
  transfers between devices with their start and end apart: 61, of which 22 were waited for; matrix products, arithmetic and copies ran while one was open for 8% of the time, Pallas kernels for 25%

profile of v3, /device:TPU:0, one launch (start us, length us, event | category | flops | bytes accessed | tf_op | source)
XLA Modules:
  0.0 475.0 jit_solution(2403496088357989171)
XLA Ops:
  8.5 5.0 %collective-permute-start.5 = (bf16[256,768]{1,0:T(8,128)(2,1)S(1)}, bf16[256,768]{1,0:T(8,128)(2,1)S(1)}, u32[]{:S(2)}, u32[]{:S(2)}) collective-permute-start(bf16[256,768]{1,0:T(8,128)(2,1)S(1)} %get-tuple-element.155), channel_id=1, source_target_pairs={{0,4},{4,8},{8,12},{1,5},{5,9},{9,13},{2,6},{6,10},{10,14},{3,7},{... | collective-permute-start | bytes 1179656 | tf_op jit(solution)/shard_map/ppermute | solution.py:1233
  13.4 3.5 collective-permute-start
  20.7 9.5 %collective-permute-done = bf16[256,768]{1,0:T(8,128)(2,1)S(1)} collective-permute-done((bf16[256,768]{1,0:T(8,128)(2,1)S(1)}, bf16[256,768]{1,0:T(8,128)(2,1)S(1)}, u32[]{:S(2)}, u32[]{:S(2)}) %collective-permute-start) | collective-permute-done | bytes 393248 | tf_op jit(solution)/shard_map/ppermute | solution.py:1233
  30.2 4.4 collective-permute-start.1
  44.1 6.5 %collective-permute-done.6 = bf16[256,768]{1,0:T(8,128)(2,1)S(1)} collective-permute-done((bf16[256,768]{1,0:T(8,128)(2,1)S(1)}, bf16[256,768]{1,0:T(8,128)(2,1)S(1)}, u32[]{:S(2)}, u32[]{:S(2)}) %collective-permute-start.6) | collective-permute-done | bytes 393248 | tf_op jit(solution)/shard_map/ppermute | solution.py:1233
  55.0 4.5 collective-permute-start.2
  68.5 6.2 %collective-permute-done.7.refs_7_ = bf16[256,768]{1,0:T(8,128)(2,1)S(1)} collective-permute-done((bf16[256,768]{1,0:T(8,128)(2,1)}, bf16[256,768]{1,0:T(8,128)(2,1)S(1)}, u32[]{:S(2)}, u32[]{:S(2)}) %collective-permute-start.7) | collective-permute-done | bytes 393248 | tf_op jit(solution)/shard_map/ppermute | solution.py:1233
  76.7 4.3 collective-permute-done.10
  82.3 7.5 %project_own.1 = (bf16[8192,768]{1,0:T(8,128)(2,1)}, bf16[8192,256]{1,0:T(8,128)(2,1)S(1)}, bf16[8192,256]{1,0:T(8,128)(2,1)S(1)}, bf16[192,2048]{1,0:T(8,128)(2,1)S(1)}) custom-call(s32[3]{0:T(128)S(1)} %pad_add_fusion.refs_0_.ids, bf16[2048,768]{1,0:T(8,128)(2,1)S(1)} %bitcast.55, f32[8,768]{1,0:T(8,128)S(1)} %stack.68.refs_2_.refs_0_.vectors.refs_1_, ...), custom_call_target="tpu_custom_call" | custom-call | flops 8800000000 | bytes 800000 | tf_op jit(solution)/shard_map/project_own/pallas_call | solution.py:408
  92.6 5.2 %collective-permute-done.3 = bf16[256,768]{1,0:T(8,128)(2,1)S(1)} collective-permute-done((bf16[256,768]{1,0:T(8,128)(2,1)S(1)}, bf16[256,768]{1,0:T(8,128)(2,1)S(1)}, u32[]{:S(2)}, u32[]{:S(2)}) %collective-permute-start.3) | collective-permute-done | bytes 393248 | tf_op jit(solution)/shard_map/ppermute | solution.py:1229
  98.4 7.7 %project.4 = (bf16[8192,768]{1,0:T(8,128)(2,1)}, bf16[8192,256]{1,0:T(8,128)(2,1)S(1)}, bf16[8192,256]{1,0:T(8,128)(2,1)S(1)}) custom-call(f32[8,768]{1,0:T(8,128)S(1)} %stack.68.refs_2_.refs_0_.vectors.refs_1_, f32[8,256]{1,0:T(8,128)S(1)} %dynamic_update_slice.3.refs_3_.refs_1_, ...), custom_call_target="tpu_custom_call", output_to_operand_aliasing={{0}: (6, {}), {1}: (7, {}), {2}: (8, {})} | custom-call | flops 8800000000 | bytes 800000 | tf_op jit(solution)/shard_map/project/pallas_call | solution.py:439
  106.7 7.6 %project.5 = (bf16[8192,768]{1,0:T(8,128)(2,1)}, bf16[8192,256]{1,0:T(8,128)(2,1)S(1)}, bf16[8192,256]{1,0:T(8,128)(2,1)S(1)}) custom-call(f32[8,768]{1,0:T(8,128)S(1)} %stack.68.refs_2_.refs_0_.vectors.refs_1_, f32[8,256]{1,0:T(8,128)S(1)} %dynamic_update_slice.3.refs_3_.refs_1_, ...), custom_call_target="tpu_custom_call", output_to_operand_aliasing={{0}: (6, {}), {1}: (7, {}), {2}: (8, {})} | custom-call | flops 8800000000 | bytes 800000 | tf_op jit(solution)/shard_map/project/pallas_call | solution.py:439
  115.0 4.0 project.6
  119.1 4.0 project.7
  124.1 12.2 %attend.1 = (bf16[192,512]{1,0:T(8,128)(2,1)S(1)}, bf16[192,512]{1,0:T(8,128)(2,1)S(1)}, bf16[192,512]{1,0:T(8,128)(2,1)S(1)}, bf16[192,512]{1,0:T(8,128)(2,1)S(1)}, f32[16,1,384]{2,1,0:T(1,128)S(1)}) custom-call(s32[3]{0:T(128)S(1)} %pad_add_fusion.refs_0_.ids, s32[16,4]{1,0:T(8,128)S(1)} %copy.59.chosen.refs_1_, ...), custom_call_target="tpu_custom_call" | custom-call | flops 15399999488 | bytes 1400000 | tf_op jit(solution)/shard_map/attend/pallas_call | solution.py:568
  139.0 6.2 %collective-permute-done.17.refs_2_ = bf16[192,512]{1,0:T(8,128)(2,1)S(1)} collective-permute-done((bf16[192,512]{1,0:T(8,128)(2,1)S(1)}, bf16[192,512]{1,0:T(8,128)(2,1)S(1)}, u32[]{:S(2)}, u32[]{:S(2)}) %collective-permute-start.17) | collective-permute-done | bytes 196640 | tf_op jit(solution)/shard_map/ppermute | solution.py:1229
  148.7 28.8 %feed_forward.1 = (bf16[192,512]{1,0:T(8,128)(2,1)}, bf16[192,512]{1,0:T(8,128)(2,1)}, bf16[192,512]{1,0:T(8,128)(2,1)}, bf16[192,512]{1,0:T(8,128)(2,1)}, bf16[...) custom-call(s32[3]{0:T(128)} %copy-done.38, ...), custom_call_target="tpu_custom_call" | custom-call | flops 32999999488 | bytes 3000000 | tf_op jit(solution)/shard_map/feed_forward/pallas_call | solution.py:880
  180.2 6.7 %collective-permute-done.29.refs_1_ = bf16[2,1728,768]{2,1,0:T(8,128)(2,1)S(1)} collective-permute-done((bf16[2,1728,768]{2,1,0:T(8,128)(2,1)}, bf16[2,1728,768]{2,1,0:T(8,128)(2,1)S(1)}, u32[]{:S(2)}, u32[]{:S(2)}) %collective-permute-start.29) | collective-permute-done | bytes 5308448 | tf_op jit(solution)/shard_map/ppermute | solution.py:1229
  189.4 5.7 %combine.1 = (bf16[960,768]{1,0:T(8,128)(2,1)S(1)}, bf16[960,768]{1,0:T(8,128)(2,1)}, bf16[2,384,768]{2,1,0:T(8,128)(2,1)S(1)}, bf16[2,384,768]{2,1,0:T(8,128)(2,1)S(1)}) custom-call(s32[3]{0:T(128)S(1)} %copy-done.39, bf16[2,1728,768]{2,1,0:T(8,128)(2,1)S(1)} %copy-done.47, bf16[2,1728,768]{2,1,0:T(8,128)(2,1)S(1)} %collective-permute-done.29.refs_1_), custom_call_target="tpu_custom_call" | custom-call | flops 6600000000 | bytes 600000 | tf_op jit(solution)/shard_map/combine/pallas_call | solution.py:1064
  200.3 33.8 %attend_back.1 = (bf16[8192,512]{1,0:T(8,128)(2,1)}, bf16[2048,256]{1,0:T(8,128)(2,1)}, f32[1,768]{1,0:T(1,128)}) custom-call(s32[3]{0:T(128)} %copy-done.38, s32[16,4]{1,0:T(8,128)} %copy-done.43, bf16[8192,256]{1,0:T(8,128)(2,1)} %copy-done.6, bf16[8192,256]{1,0:T(8,128)(2,1)} %copy-done.7, bf16[192,2048]{1,0:T(8,128)(2,1)} %copy-done.48, ...), custom_call_target="tpu_custom_call" | custom-call | flops 39600001024 | bytes 3600000 | tf_op jit(solution)/shard_map/attend_back/pallas_call | solution.py:696
  242.9 13.4 %weight_sums.1 = (bf16[384,640]{1,0:T(8,128)(2,1)S(1)}, bf16[384,640]{1,0:T(8,128)(2,1)S(1)}) custom-call(s32[3]{0:T(128)S(1)} %copy-done.40, bf16[8192,768]{1,0:T(8,128)(2,1)} %get-tuple-element.103.refs_1_, bf16[8192,512]{1,0:T(8,128)(2,1)S(1)} %copy-done.1, bf16[2048,256]{1,0:T(8,128)(2,1)S(1)} %copy-done.13, ...), custom_call_target="tpu_custom_call" | custom-call | flops 11000000 | bytes 1000 | tf_op jit(solution)/shard_map/weight_sums/pallas_call | solution.py:1127
  272.3 3.8 push.6
  280.7 3.6 push.7
  295.2 37.9 %collective-permute-done.39 = bf16[512,768]{1,0:T(8,128)(2,1)} collective-permute-done((bf16[512,768]{1,0:T(8,128)(2,1)}, bf16[512,768]{1,0:T(8,128)(2,1)}, u32[]{:S(2)}, u32[]{:S(2)}) %collective-permute-start.39) | collective-permute-done | bytes 786464 | tf_op jit(solution)/shard_map/ppermute | solution.py:1237
  341.3 15.3 %collective-permute-done.44 = bf16[512,768]{1,0:T(8,128)(2,1)} collective-permute-done((bf16[512,768]{1,0:T(8,128)(2,1)}, bf16[512,768]{1,0:T(8,128)(2,1)}, u32[]{:S(2)}, u32[]{:S(2)}) %collective-permute-start.44) | collective-permute-done | bytes 786464 | tf_op jit(solution)/shard_map/ppermute | solution.py:1229
  356.5 21.9 %collective-permute-done.45 = bf16[512,768]{1,0:T(8,128)(2,1)} collective-permute-done((bf16[512,768]{1,0:T(8,128)(2,1)}, bf16[512,768]{1,0:T(8,128)(2,1)}, u32[]{:S(2)}, u32[]{:S(2)}) %collective-permute-start.45) | collective-permute-done | bytes 786464 | tf_op jit(solution)/shard_map/ppermute | solution.py:1237
  386.0 5.2 %ordered.3.refs_9_ = bf16[2048,768]{1,0:T(8,128)(2,1)} custom-call(s32[3]{0:T(128)S(1)} %copy-done.40, bf16[512,768]{1,0:T(8,128)(2,1)S(1)} %copy-done.14, bf16[512,768]{1,0:T(8,128)(2,1)} %collective-permute-done.40.refs_1_, bf16[512,768]{1,0:T(8,128)(2,1)} %collective-permute-done.41.refs_2_, bf16[512,768]{1,0:T(8,128)(2,1)} %collective-permute-done.42.refs_3_), custom_call_target="tpu_custom_call" | custom-call | flops 11000000 | bytes 1000 | tf_op jit(solution)/shard_map/ordered/pallas_call | solution.py:1014
  391.2 11.3 %collective-permute-done.48 = bf16[512,768]{1,0:T(8,128)(2,1)} collective-permute-done((bf16[512,768]{1,0:T(8,128)(2,1)}, bf16[512,768]{1,0:T(8,128)(2,1)}, u32[]{:S(2)}, u32[]{:S(2)}) %collective-permute-start.48) | collective-permute-done | bytes 786464 | tf_op jit(solution)/shard_map/ppermute | solution.py:1229
  404.0 9.7 %collective-permute-done.46.refs_3_ = bf16[512,768]{1,0:T(8,128)(2,1)S(1)} collective-permute-done((bf16[512,768]{1,0:T(8,128)(2,1)}, bf16[512,768]{1,0:T(8,128)(2,1)S(1)}, u32[]{:S(2)}, u32[]{:S(2)}) %collective-permute-start.46) | collective-permute-done | bytes 786464 | tf_op jit(solution)/shard_map/ppermute | solution.py:1237
  416.9 13.1 %all-reduce.9.cloned.1.call-done.refs_1_.refs_0_ = bf16[384,640]{1,0:T(8,128)(2,1)} async-done(((bf16[384,640]{1,0:T(8,128)(2,1)}), bf16[384,640]{1,0:T(8,128)(2,1)}) %all-reduce.9.cloned.1.call-update) | async-done | bytes 491536 | tf_op jit(solution)/shard_map/psum | solution.py:1373
  437.4 5.3 %collective-permute-done.58.refs_1_ = bf16[384,640]{1,0:T(8,128)(2,1)S(1)} collective-permute-done((bf16[384,640]{1,0:T(8,128)(2,1)}, bf16[384,640]{1,0:T(8,128)(2,1)S(1)}, u32[]{:S(2)}, u32[]{:S(2)}) %collective-permute-start.58) | collective-permute-done | bytes 491552 | tf_op jit(solution)/shard_map/ppermute | solution.py:1229
  463.1 4.6 ordered.4
  (365 shorter events, 140.8 us)
Async XLA Ops:
  8.5 26.1 %collective-permute-start.5 = (bf16[256,768]{1,0:T(8,128)(2,1)S(1)}, bf16[256,768]{1,0:T(8,128)(2,1)S(1)}, u32[]{:S(2)}, u32[]{:S(2)}) collective-permute-start(bf16[256,768]{1,0:T(8,128)(2,1)S(1)} %get-tuple-element.155), channel_id=1, source_target_pairs={{0,4},{4,8},{8,12},{1,5},{5,9},{9,13},{2,6},{6,10},{10,14},{3,7},{... | collective-permute-start | bytes 1179656 | tf_op jit(solution)/shard_map/ppermute | solution.py:1233
  18.1 47.5 %collective-permute-start.14 = (bf16[768,768]{1,0:T(8,128)(2,1)}, bf16[768,768]{1,0:T(8,128)(2,1)}, u32[]{:S(2)}, u32[]{:S(2)}) collective-permute-start(bf16[768,768]{1,0:T(8,128)(2,1)} %broadcast_select_fusion), channel_id=1, source_target_pairs={{0,2},{1,3},{2,0},{3,1},{4,6},{5,7},{6,4},{7,5},{8,10},{9,11},{10,... | collective-permute-start | bytes 3538952 | tf_op jit(solution)/shard_map/ppermute | solution.py:1229
  39.1 25.1 %collective-permute-start.12 = (bf16[512,768]{1,0:T(8,128)(2,1)}, bf16[512,768]{1,0:T(8,128)(2,1)}, u32[]{:S(2)}, u32[]{:S(2)}) collective-permute-start(bf16[512,768]{1,0:T(8,128)(2,1)} %pad_maximum_fusion.3), channel_id=1, source_target_pairs={{0,2},{1,3},{2,0},{3,1},{4,6},{5,7},{6,4},{7,5},{8,10},{9,11},{10,... | collective-permute-start | bytes 2359304 | tf_op jit(solution)/shard_map/ppermute | solution.py:1229
  51.6 29.4 %collective-permute-start.10 = (bf16[512,768]{1,0:T(8,128)(2,1)}, bf16[512,768]{1,0:T(8,128)(2,1)}, u32[]{:S(2)}, u32[]{:S(2)}) collective-permute-start(bf16[512,768]{1,0:T(8,128)(2,1)} %pad_maximum_fusion.2), channel_id=1, source_target_pairs={{0,2},{1,3},{2,0},{3,1},{4,6},{5,7},{6,4},{7,5},{8,10},{9,11},{10,... | collective-permute-start | bytes 2359304 | tf_op jit(solution)/shard_map/ppermute | solution.py:1229
  55.0 20.3 %collective-permute-start.2 = (bf16[256,768]{1,0:T(8,128)(2,1)}, bf16[256,768]{1,0:T(8,128)(2,1)S(1)}, u32[]{:S(2)}, u32[]{:S(2)}) collective-permute-start(bf16[256,768]{1,0:T(8,128)(2,1)} %copy-done.53), channel_id=1, source_target_pairs={{0,4},{4,8},{8,12},{1,5},{5,9},{9,13},{2,6},{6,10},{10,14},{3,7},{... | collective-permute-start | bytes 1179656 | tf_op jit(solution)/shard_map/ppermute | solution.py:1233
  65.4 32.4 %collective-permute-start.13 = (bf16[1024,768]{1,0:T(8,128)(2,1)S(1)}, bf16[1024,768]{1,0:T(8,128)(2,1)S(1)}, u32[]{:S(2)}, u32[]{:S(2)}) collective-permute-start(bf16[1024,768]{1,0:T(8,128)(2,1)S(1)} %constant_dynamic-update-slice_fusion.7.refs_4_), channel_id=1, source_target_pairs={{0,1},{1,0},{2,3},{3,2},{4,5},{5,4},{6,7},{7,6},{8,9},{9,8},{10,11... | collective-permute-start | bytes 4718600 | tf_op jit(solution)/shard_map/ppermute | solution.py:1229
  65.6 40.5 %collective-permute-start.15 = (bf16[768,768]{1,0:T(8,128)(2,1)}, bf16[768,768]{1,0:T(8,128)(2,1)S(1)}, u32[]{:S(2)}, u32[]{:S(2)}) collective-permute-start(bf16[768,768]{1,0:T(8,128)(2,1)} %collective-permute-done.14.refs_9_.refs_10_), channel_id=1, source_target_pairs={{0,16},{16,0},{1,17},{17,1},{2,18},{18,2},{3,19},{19,3},{4,20},{20... | collective-permute-start | bytes 3538952 | tf_op jit(solution)/shard_map/ppermute | solution.py:1229
  75.2 22.6 %collective-permute-start.3 = (bf16[256,768]{1,0:T(8,128)(2,1)S(1)}, bf16[256,768]{1,0:T(8,128)(2,1)S(1)}, u32[]{:S(2)}, u32[]{:S(2)}) collective-permute-start(bf16[256,768]{1,0:T(8,128)(2,1)S(1)} %collective-permute-done.2.refs_8_), channel_id=1, source_target_pairs={{0,2},{1,3},{2,0},{3,1},{4,6},{5,7},{6,4},{7,5},{8,10},{9,11},{10,... | collective-permute-start | bytes 1179656 | tf_op jit(solution)/shard_map/ppermute | solution.py:1229
  82.2 24.0 %collective-permute-start.11 = (bf16[1024,768]{1,0:T(8,128)(2,1)S(1)}, bf16[1024,768]{1,0:T(8,128)(2,1)S(1)}, u32[]{:S(2)}, u32[]{:S(2)}) collective-permute-start(bf16[1024,768]{1,0:T(8,128)(2,1)S(1)} %constant_dynamic-update-slice_fusion.4.refs_4_), channel_id=1, source_target_pairs={{0,1},{1,0},{2,3},{3,2},{4,5},{5,4},{6,7},{7,6},{8,9},{9,8},{10,11... | collective-permute-start | bytes 4718600 | tf_op jit(solution)/shard_map/ppermute | solution.py:1229
  91.0 23.3 %collective-permute-start.20 = (bf16[208,768]{1,0:T(8,128)(2,1)S(1)}, bf16[208,768]{1,0:T(8,128)(2,1)S(1)}, u32[]{:S(2)}, u32[]{:S(2)}) collective-permute-start(bf16[208,768]{1,0:T(8,128)(2,1)S(1)} %copy-done.61), channel_id=1, source_target_pairs={{0,2},{1,3},{2,0},{3,1},{4,6},{5,7},{6,4},{7,5},{8,10},{9,11},{10,... | collective-permute-start | bytes 958472 | tf_op jit(solution)/shard_map/ppermute | solution.py:1229
  97.8 25.4 %collective-permute-start.19 = (bf16[208,768]{1,0:T(8,128)(2,1)S(1)}, bf16[208,768]{1,0:T(8,128)(2,1)S(1)}, u32[]{:S(2)}, u32[]{:S(2)}) collective-permute-start(bf16[208,768]{1,0:T(8,128)(2,1)S(1)} %copy-done.61), channel_id=1, source_target_pairs={{0,1},{1,0},{2,3},{3,2},{4,5},{5,4},{6,7},{7,6},{8,9},{9,8},{10,11... | collective-permute-start | bytes 958472 | tf_op jit(solution)/shard_map/ppermute | solution.py:1229
  97.9 39.5 %collective-permute-start.22 = (bf16[768,768]{1,0:T(8,128)(2,1)S(1)}, bf16[768,768]{1,0:T(8,128)(2,1)S(1)}, u32[]{:S(2)}, u32[]{:S(2)}) collective-permute-start(bf16[768,768]{1,0:T(8,128)(2,1)S(1)} %copy-done.58), channel_id=1, source_target_pairs={{0,1},{1,0},{2,3},{3,2},{4,5},{5,4},{6,7},{7,6},{8,9},{9,8},{10,11... | collective-permute-start | bytes 3538952 | tf_op jit(solution)/shard_map/ppermute | solution.py:1229
  114.4 24.5 %collective-permute-start.24 = (bf16[768,768]{1,0:T(8,128)(2,1)S(1)}, bf16[768,768]{1,0:T(8,128)(2,1)S(1)}, u32[]{:S(2)}, u32[]{:S(2)}) collective-permute-start(bf16[768,768]{1,0:T(8,128)(2,1)S(1)} %copy-done.59), channel_id=1, source_target_pairs={{0,1},{1,0},{2,3},{3,2},{4,5},{5,4},{6,7},{7,6},{8,9},{9,8},{10,11... | collective-permute-start | bytes 3538952 | tf_op jit(solution)/shard_map/ppermute | solution.py:1229
  114.5 22.4 %collective-permute-start.21 = (bf16[208,768]{1,0:T(8,128)(2,1)S(1)}, bf16[208,768]{1,0:T(8,128)(2,1)S(1)}, u32[]{:S(2)}, u32[]{:S(2)}) collective-permute-start(bf16[208,768]{1,0:T(8,128)(2,1)S(1)} %collective-permute-done.20.refs_6_), channel_id=1, source_target_pairs={{0,1},{1,0},{2,3},{3,2},{4,5},{5,4},{6,7},{7,6},{8,9},{9,8},{10,11... | collective-permute-start | bytes 958472 | tf_op jit(solution)/shard_map/ppermute | solution.py:1229
  123.2 24.4 %collective-permute-start.25 = (bf16[768,768]{1,0:T(8,128)(2,1)S(1)}, bf16[768,768]{1,0:T(8,128)(2,1)S(1)}, u32[]{:S(2)}, u32[]{:S(2)}) collective-permute-start(bf16[768,768]{1,0:T(8,128)(2,1)S(1)} %collective-permute-done.15.refs_9_.refs_14_), channel_id=1, source_target_pairs={{0,1},{1,0},{2,3},{3,2},{4,5},{5,4},{6,7},{7,6},{8,9},{9,8},{10,11... | collective-permute-start | bytes 3538952 | tf_op jit(solution)/shard_map/ppermute | solution.py:1229
  178.3 21.2 %collective-permute-start.26 = (bf16[192,512]{1,0:T(8,128)(2,1)}, bf16[192,512]{1,0:T(8,128)(2,1)S(1)}, u32[]{:S(2)}, u32[]{:S(2)}) collective-permute-start(bf16[192,512]{1,0:T(8,128)(2,1)} %get-tuple-element.95), channel_id=1, source_target_pairs={{0,1},{1,0},{2,3},{3,2},{4,5},{5,4},{6,7},{7,6},{8,9},{9,8},{10,11... | collective-permute-start | bytes 589832 | tf_op jit(solution)/shard_map/ppermute | solution.py:1229
  178.4 21.2 %collective-permute-start.27 = (bf16[192,512]{1,0:T(8,128)(2,1)}, bf16[192,512]{1,0:T(8,128)(2,1)S(1)}, u32[]{:S(2)}, u32[]{:S(2)}) collective-permute-start(bf16[192,512]{1,0:T(8,128)(2,1)} %get-tuple-element.96), channel_id=1, source_target_pairs={{0,2},{1,3},{2,0},{3,1},{4,6},{5,7},{6,4},{7,5},{8,10},{9,11},{10,... | collective-permute-start | bytes 589832 | tf_op jit(solution)/shard_map/ppermute | solution.py:1229
  195.1 39.0 %collective-permute-start.30 = (bf16[960,768]{1,0:T(8,128)(2,1)}, bf16[960,768]{1,0:T(8,128)(2,1)S(1)}, u32[]{:S(2)}, u32[]{:S(2)}) collective-permute-start(bf16[960,768]{1,0:T(8,128)(2,1)} %get-tuple-element.100.refs_10_), channel_id=1, source_target_pairs={{0,2},{1,3},{2,0},{3,1},{4,6},{5,7},{6,4},{7,5},{8,10},{9,11},{10,... | collective-permute-start | bytes 4423688 | tf_op jit(solution)/shard_map/ppermute | solution.py:1229
  196.7 37.4 %collective-permute-start.31 = (bf16[2,384,768]{2,1,0:T(8,128)(2,1)S(1)}, bf16[2,384,768]{2,1,0:T(8,128)(2,1)S(1)}, u32[]{:S(2)}, u32[]{:S(2)}) collective-permute-start(bf16[2,384,768]{2,1,0:T(8,128)(2,1)S(1)} %get-tuple-element.101.refs_11_), channel_id=1, source_target_pairs={{0,16},{16,0},{1,17},{17,1},{2,18},{18,2},{3,19},{19,3},{4,20},{20... | collective-permute-start | bytes 3538952 | tf_op jit(solution)/shard_map/ppermute | solution.py:1229
  242.1 20.4 %collective-permute-start.32 = (bf16[2,512,768]{2,1,0:T(8,128)(2,1)S(1)}, bf16[2,512,768]{2,1,0:T(8,128)(2,1)}, u32[]{:S(2)}, u32[]{:S(2)}) collective-permute-start(bf16[2,512,768]{2,1,0:T(8,128)(2,1)S(1)} %get-tuple-element.108.refs_4_), channel_id=1, source_target_pairs={{0,1},{1,0},{2,3},{3,2},{4,5},{5,4},{6,7},{7,6},{8,9},{9,8},{10,11... | collective-permute-start | bytes 4718600 | tf_op jit(solution)/shard_map/ppermute | solution.py:1229
  264.8 116.3 %all-reduce.7.cloned.1.call-start = ((), (), s32[]{:S(2)}) async-start(), calls=%async_computation | async-start | bytes 2654208 | tf_op jit(solution)/shard_map/psum | solution.py:1355
  264.8 23.1 %collective-permute-start.35 = (bf16[2,512,768]{2,1,0:T(8,128)(2,1)}, bf16[2,512,768]{2,1,0:T(8,128)(2,1)}, u32[]{:S(2)}, u32[]{:S(2)}) collective-permute-start(bf16[2,512,768]{2,1,0:T(8,128)(2,1)} %held.11), channel_id=1, source_target_pairs={{0,1},{1,0},{2,3},{3,2},{4,5},{5,4},{6,7},{7,6},{8,9},{9,8},{10,11... | collective-permute-start | bytes 4718600 | tf_op jit(solution)/shard_map/ppermute | solution.py:1229
  290.1 43.0 %collective-permute-start.39 = (bf16[512,768]{1,0:T(8,128)(2,1)}, bf16[512,768]{1,0:T(8,128)(2,1)}, u32[]{:S(2)}, u32[]{:S(2)}) collective-permute-start(bf16[512,768]{1,0:T(8,128)(2,1)} %held.13), channel_id=1, source_target_pairs={{4,0},{8,4},{12,8},{5,1},{9,5},{13,9},{6,2},{10,6},{14,10},{7,3},{... | collective-permute-start | bytes 2359304 | tf_op jit(solution)/shard_map/ppermute | solution.py:1237
  291.7 41.4 %collective-permute-start.36 = (bf16[512,768]{1,0:T(8,128)(2,1)}, bf16[512,768]{1,0:T(8,128)(2,1)}, u32[]{:S(2)}, u32[]{:S(2)}) collective-permute-start(bf16[512,768]{1,0:T(8,128)(2,1)} %fusion.9.refs_3_), channel_id=1, source_target_pairs={{0,2},{1,3},{2,0},{3,1},{4,6},{5,7},{6,4},{7,5},{8,10},{9,11},{10,... | collective-permute-start | bytes 2359304 | tf_op jit(solution)/shard_map/ppermute | solution.py:1229
  292.8 46.4 %collective-permute-start.47 = (bf16[2,512,768]{2,1,0:T(8,128)(2,1)S(1)}, bf16[2,512,768]{2,1,0:T(8,128)(2,1)}, u32[]{:S(2)}, u32[]{:S(2)}) collective-permute-start(bf16[2,512,768]{2,1,0:T(8,128)(2,1)S(1)} %copy-done.21), channel_id=1, source_target_pairs={{0,1},{1,0},{2,3},{3,2},{4,5},{5,4},{6,7},{7,6},{8,9},{9,8},{10,11... | collective-permute-start | bytes 4718600 | tf_op jit(solution)/shard_map/ppermute | solution.py:1229
  292.8 137.2 %all-reduce.9.cloned.1.call-start = ((), (), s32[]{:S(2)}) async-start(), calls=%async_computation.1 | async-start | bytes 983040 | tf_op jit(solution)/shard_map/psum | solution.py:1373
  335.7 20.8 %collective-permute-start.44 = (bf16[512,768]{1,0:T(8,128)(2,1)}, bf16[512,768]{1,0:T(8,128)(2,1)}, u32[]{:S(2)}, u32[]{:S(2)}) collective-permute-start(bf16[512,768]{1,0:T(8,128)(2,1)} %held.15), channel_id=1, source_target_pairs={{0,2},{1,3},{2,0},{3,1},{4,6},{5,7},{6,4},{7,5},{8,10},{9,11},{10,... | collective-permute-start | bytes 2359304 | tf_op jit(solution)/shard_map/ppermute | solution.py:1229
  336.3 42.2 %collective-permute-start.45 = (bf16[512,768]{1,0:T(8,128)(2,1)}, bf16[512,768]{1,0:T(8,128)(2,1)}, u32[]{:S(2)}, u32[]{:S(2)}) collective-permute-start(bf16[512,768]{1,0:T(8,128)(2,1)} %fusion.12.refs_1_), channel_id=1, source_target_pairs={{4,0},{8,4},{12,8},{5,1},{9,5},{13,9},{6,2},{10,6},{14,10},{7,3},{... | collective-permute-start | bytes 2359304 | tf_op jit(solution)/shard_map/ppermute | solution.py:1237
  337.6 44.7 %collective-permute-start.41 = (bf16[512,768]{1,0:T(8,128)(2,1)}, bf16[512,768]{1,0:T(8,128)(2,1)}, u32[]{:S(2)}, u32[]{:S(2)}) collective-permute-start(bf16[512,768]{1,0:T(8,128)(2,1)} %held.14.refs_0_), channel_id=1, source_target_pairs={{0,2},{1,3},{2,0},{3,1},{4,6},{5,7},{6,4},{7,5},{8,10},{9,11},{10,... | collective-permute-start | bytes 2359304 | tf_op jit(solution)/shard_map/ppermute | solution.py:1229
  381.2 32.6 %collective-permute-start.49 = (bf16[864,768]{1,0:T(8,128)(2,1)}, bf16[864,768]{1,0:T(8,128)(2,1)S(1)}, u32[]{:S(2)}, u32[]{:S(2)}) collective-permute-start(bf16[864,768]{1,0:T(8,128)(2,1)} %held.17.refs_1_.mine), channel_id=1, source_target_pairs={{0,16},{16,0},{1,17},{17,1},{2,18},{18,2},{3,19},{19,3},{4,20},{20... | collective-permute-start | bytes 3981320 | tf_op jit(solution)/shard_map/ppermute | solution.py:1229
  384.4 29.3 %collective-permute-start.46 = (bf16[512,768]{1,0:T(8,128)(2,1)}, bf16[512,768]{1,0:T(8,128)(2,1)S(1)}, u32[]{:S(2)}, u32[]{:S(2)}) collective-permute-start(bf16[512,768]{1,0:T(8,128)(2,1)} %fusion.6.refs_1_), channel_id=1, source_target_pairs={{4,0},{8,4},{12,8},{5,1},{9,5},{13,9},{6,2},{10,6},{14,10},{7,3},{... | collective-permute-start | bytes 2359304 | tf_op jit(solution)/shard_map/ppermute | solution.py:1237
  416.5 31.1 %collective-permute-start.51 = (bf16[512,768]{1,0:T(8,128)(2,1)}, bf16[512,768]{1,0:T(8,128)(2,1)}, u32[]{:S(2)}, u32[]{:S(2)}) collective-permute-start(bf16[512,768]{1,0:T(8,128)(2,1)} %get-tuple-element.125.refs_0_), channel_id=1, source_target_pairs={{0,2},{1,3},{2,0},{3,1},{4,6},{5,7},{6,4},{7,5},{8,10},{9,11},{10,... | collective-permute-start | bytes 2359304 | tf_op jit(solution)/shard_map/ppermute | solution.py:1229
  (116 other events, 1394.9 us)
Sparse Core Ops, SparseCore 0:
  292.9 81.5 all-reduce.6
  385.8 44.0 all-reduce.8
